TPU v7x, 32 devices: a whole 2x2x4 slice. The times are simulated.
32 devices in a mesh: row: 8 (over z, y), col: 4 (over x, core).
Axes of the slice: x: 2, y: 2, z: 4, core: 2. Of those that a mesh axis runs over, the one named last changes fastest.
Arguments:
- anc_inverse: float32 [16384, 16384], P('row', 'col')
- panel: float32 [1920, 2560], P('row', 'col'), may hold values from -0.015625 to 0.015625
- local_rows: int32 [1920], P('row'), may hold values from -1 to 2047, as said below
- inv_diag: float32 [2560, 2560], P('row', 'col')
Outputs:
- sigma_off: float32 [1920, 2560], P('row', 'col')
- sigma_diag: float32 [2560, 2560], P('row', 'col')
Inputs may be any that keep to these rules, and one draw needn't show every extreme that they name: `local_rows`: each aligned block of 240 slots lists its live ancestor rows first, distinct and ascending, then -1 in the rest; every block has at least one live slot, some block is full and some block is at most half full.
All inputs are finite; a program needn't handle non-finite values.
Results may differ from a plain program's by a relative error of at most 0.000075.
Values sent between devices are 32-bit elements; how exact they have to be, the bound alone decides.
No kernel may reach another device: no remote copies, remote signals or barrier semaphores. Data moves between devices by JAX's collectives and lax.ppermute only.
A program may use at most 128 MiB of HBM per device.

v0:
```python
import jax
import jax.numpy as jnp
from jax import lax
from jax.sharding import PartitionSpec as P


def broadcast(value, axis, source):
    kept = jnp.where(lax.axis_index(axis) == source, value, 0).astype(value.dtype)
    return lax.psum(kept, axis)


def pick_columns(rows_sel, offset, width, lists):
    region = lax.slice_in_dim(rows_sel, offset, offset + width, axis=1)
    taken = jnp.take(region, jnp.maximum(lists, 0), axis=1)
    return taken * (lists >= 0).astype(jnp.float32)[None, :]


def shards(anc_inverse, panel, local_rows, inv_diag):
    anc_rows = anc_inverse.shape[0]
    groups = lax.axis_size("row") // lax.axis_size("col")
    col_index = lax.axis_index("col")
    own_live = (local_rows >= 0).astype(jnp.float32)
    rows_sel = jnp.take(anc_inverse, jnp.maximum(local_rows, 0), axis=0) * own_live[:, None]
    widened = lax.all_gather(panel, "col", axis=1, tiled=True)
    partial_sum = jnp.zeros(widened.shape, jnp.float32)
    for member in range(groups):
        root_index = col_index * groups + member
        block_panel, block_lists = (
            broadcast(widened, "row", root_index),
            broadcast(local_rows, "row", root_index),
        )
        square = pick_columns(rows_sel, member * anc_rows, anc_rows, block_lists)
        partial_sum = partial_sum - jnp.dot(square, block_panel, precision=lax.Precision.HIGHEST)
    sigma_off = lax.psum_scatter(partial_sum, "col", scatter_dimension=1, tiled=True)
    folded = lax.psum_scatter(
        lax.dot_general(
            widened, sigma_off, (((0,), (0,)), ((), ())), precision=lax.Precision.HIGHEST
        ),
        "row",
        scatter_dimension=0,
        tiled=True,
    )
    sigma_diag = inv_diag - folded
    return (sigma_off, sigma_diag)


def solution(mesh):
    placed = (P("row", "col"), P("row", "col"), P("row"), P("row", "col"))
    return jax.shard_map(
        shards,
        mesh=mesh,
        in_specs=placed,
        out_specs=(P("row", "col"), P("row", "col")),
        check_vma=False,
    )
```

profile of v0, /device:TPU:0, one launch (start us, length us, event | category | flops | bytes accessed | tf_op | source)
XLA Modules:
  0.0 405.9 jit_solution(17762740318950121895)
XLA Ops:
  7.2 0.0 all-gather.2.cloned.1.call-start
  7.2 0.7 all-gather.2.cloned.1.call-update
  7.9 0.0 all-reduce.4.cloned.1.call-start
  8.0 29.0 %all-gather.2.cloned.1.call-done = f32[240,2560]{1,0:T(8,128)} async-done(((f32[240,640]{1,0:T(8,128)}), f32[240,2560]{1,0:T(8,128)}) %all-gather.2.cloned.1.call-update) | async-done | bytes 2457616 | tf_op jit(solution)/shard_map/all_gather | solution.py:24
  36.9 4.5 %broadcast_select_fusion = (f32[240,2560]{1,0:T(8,128)}, f32[240,2560]{1,0:T(8,128)}) fusion(f32[240,2560]{1,0:T(8,128)} %all-gather.2.cloned.1.call-done, pred[]{:T(512)S(6)} %eq.9, pred[]{:T(512)S(6)} %eq.8), kind=kLoop, calls=%fused_computation.7 | loop fusion | flops 1228800 | bytes 7372802 | tf_op jit(solution)/shard_map/jit(_where)/select_n | solution.py:8
  41.4 0.0 copy-start.3
  41.4 0.0 all-reduce.4.cloned.1.call-update
  41.4 0.0 reduce-scatter.5.cloned.1.call-start
  41.5 0.6 copy-done.3
  42.1 17.1 %gather_fusion = f32[240,4096]{1,0:T(8,128)} fusion(f32[2048,4096]{1,0:T(8,128)} %param.6, s32[1024]{0:T(1024)S(1)} %pad_clamp_fusion.2), kind=kCustom, calls=%fused_computation.2 | custom fusion | bytes 7865280 | tf_op jit(solution)/shard_map/jit(_take)/gather | solution.py:23
  59.2 2.7 select_multiply_fusion
  61.9 1.6 fusion.10
  63.6 1.8 copy.10
  65.4 1.9 copy.11
  67.3 13.1 %all-reduce = (s32[240]{0:T(256)S(1)}, s32[240]{0:T(256)S(1)}) all-reduce(s32[240]{0:T(256)S(1)} %get-tuple-element.21, s32[240]{0:T(256)S(1)} %get-tuple-element.19), channel_id=1, replica_groups=mesh['row'=8,'col'=4] {'row'}, use_global_device_ids=true, to_apply=%region_0.1 | all-reduce | flops 480 | bytes 3840 | tf_op jit(solution)/shard_map/psum | solution.py:9
  80.4 2.5 gather_fusion.1
  83.0 0.9 gather_fusion.2
  84.0 133.0 %all-reduce.4.cloned.1.call-done = (f32[240,2560]{1,0:T(8,128)}, f32[240,2560]{1,0:T(8,128)}) async-done(((f32[240,2560]{1,0:T(8,128)}, f32[240,2560]{1,0:T(8,128)}), (f32[240,2560]{1,0:T(8,128)}, f32[240,2560]{1,0:T(8,128)})) %all-reduce.4.cloned.1.call-update) | async-done | bytes 4915216 | tf_op jit(solution)/shard_map/psum | solution.py:9
  217.0 0.0 copy-start.1
  217.0 4.3 %convolution_subtract_fusion.1 = f32[240,2560]{1,0:T(8,128)S(1)} fusion(f32[240,2560]{1,0:T(8,128)} %get-tuple-element.9, f32[240,240]{1,0:T(8,128)S(1)} %gather_fusion.1, f32[240]{0:T(256)S(1)} %get-tuple-element.24, pred[240]{0:T(512)(128)(4,1)S(1)} %get-tuple-element.25), kind=kOutput, calls=%fused_computation.5 | convolution fusion | flops 1770201600 | bytes 5146800 | tf_op jit(solution)/shard_map/dot_general | solution.py:33
  221.2 0.0 copy-done.1
  221.2 4.0 convolution_subtract_fusion
  225.2 0.0 copy-start
  225.2 0.0 reduce-scatter.5.cloned.1.call-update
  225.2 0.2 reduce-scatter.7.cloned.1.call-start
  225.5 32.6 %reduce-scatter.5.cloned.1.call-done = f32[240,640]{1,0:T(8,128)} async-done(((f32[240,2560]{1,0:T(8,128)}), f32[240,640]{1,0:T(8,128)}) %reduce-scatter.5.cloned.1.call-update) | async-done | bytes 614416 | tf_op jit(solution)/shard_map/reduce_scatter | solution.py:34
  258.1 0.0 copy-done
  258.1 8.5 %convolution_bitcast_fusion = f32[2560,640]{0,1:T(8,128)} fusion(f32[240,640]{1,0:T(8,128)} %reduce-scatter.5.cloned.1.call-done, f32[240,2560]{1,0:T(8,128)S(1)} %copy-done), kind=kOutput, calls=%fused_computation.3 | convolution fusion | flops 4718592000 | bytes 9625600 | tf_op jit(solution)/shard_map/dot_general | solution.py:36
  266.5 8.2 %copy.14 = f32[2560,640]{1,0:T(8,128)} copy(f32[2560,640]{0,1:T(8,128)} %convolution_bitcast_fusion) | data formatting | bytes 13107200
  274.7 0.0 copy-start.2
  274.7 0.0 reduce-scatter.7.cloned.1.call-update
  274.7 1.1 copy-done.2
  275.8 0.3 copy.12
  276.2 120.4 %reduce-scatter.7.cloned.1.call-done = f32[320,640]{1,0:T(8,128)} async-done(((f32[2560,640]{1,0:T(8,128)}), f32[320,640]{1,0:T(8,128)}) %reduce-scatter.7.cloned.1.call-update) | async-done | bytes 819216
  396.6 1.5 copy.15
  398.1 0.1 sub.11
  398.2 1.2 copy.13
  (7 shorter events, 0.0 us)
Async XLA Ops:
  7.2 29.8 %all-gather.2.cloned.1.call-start = ((), (), s32[]{:S(2)}) async-start(), calls=%async_computation.2 | async-start | bytes 3072000 | tf_op jit(solution)/shard_map/all_gather | solution.py:24
  7.9 209.1 %all-reduce.4.cloned.1.call-start = ((), (), s32[]{:S(2)}) async-start(), calls=%async_computation.5 | async-start | bytes 9830400 | tf_op jit(solution)/shard_map/psum | solution.py:9
  41.4 0.7 copy-start.3
  41.4 216.6 %reduce-scatter.5.cloned.1.call-start = ((), (), s32[]{:S(2)}) async-start(), calls=%async_computation.3 | async-start | bytes 3072000 | tf_op jit(solution)/shard_map/reduce_scatter | solution.py:34
  217.0 4.3 %copy-start.1 = (f32[240,2560]{1,0:T(8,128)S(1)}, f32[240,2560]{1,0:T(8,128)}, u32[]{:S(2)}) copy-start(f32[240,2560]{1,0:T(8,128)} %get-tuple-element.10) | copy-start | bytes 7372804
  225.2 32.8 %copy-start = (f32[240,2560]{1,0:T(8,128)S(1)}, f32[240,2560]{1,0:T(8,128)}, u32[]{:S(2)}) copy-start(f32[240,2560]{1,0:T(8,128)} %all-gather.2.cloned.1.call-done) | copy-start | bytes 7372804
  225.2 171.3 %reduce-scatter.7.cloned.1.call-start = ((), (), s32[]{:S(2)}) async-start(), calls=%async_computation.4 | async-start | bytes 7372800
  274.7 1.1 copy-start.2
Sparse Core Ops, SparseCore 0:
  9.6 27.3 all-gather.1
  41.6 175.3 all-reduce.3
  225.4 32.6 reduce-scatter.4
  274.8 121.7 reduce-scatter.6
where the time goes:
time: 407 us; the launch traced here: 406 us
  waiting for transfers between devices  316 us (78%)
  local copies, waits for them, and re-layouts  38.8 us (10%)
  matrix products  16.7 us (4%)
  between operations  13.8 us (3%)
  blocking collectives  13.1 us (3%)
  other arithmetic  7.38 us (2%)
    psum x1, waiting for transfers between devices, broadcast(): return lax.psum(kept, axis)  133 us
    unnamed x5, waiting for transfers between devices  121 us
    reduce_scatter x1, waiting for transfers between devices, shards(): lax.psum_scatter(partial_sum, 'col', scatter_dimension=1, tiled=True)  32.6 us
    all_gather x1, waiting for transfers between devices, shards(): widened = lax.all_gather(panel, 'col', axis=1, tiled=True)  29 us
    gather x1, local copies, waits for them, and re-layouts, shards(): jnp.take(anc_inverse, jnp.maximum(local_rows, 0), axis=0)  17.1 us
    psum x1, blocking collectives, broadcast(): return lax.psum(kept, axis)  13.1 us
    unnamed x12, local copies, waits for them, and re-layouts  12.9 us
    dot_general x1, matrix products, shards(): lax.dot_general(widened, sigma_off, (((0,), (0,)), ((), ())), precision=l...  8.45 us
  transfers between devices with their start and end apart: 4, of which 4 were waited for; matrix products, arithmetic and copies ran while one was open for 7% of the time, Pallas kernels for 0%

commit v1 on v0

v1 whole, which is shorter than its diff:
```python
import functools

import jax
import jax.numpy as jnp
from jax import lax
from jax.experimental import pallas as pl
from jax.experimental.pallas import tpu as pltpu
from jax.sharding import PartitionSpec as P

MEMBERS = 2
BF16 = jnp.bfloat16
F32 = jnp.float32


def split(x):
    high = x.astype(BF16)
    return high, (x - high.astype(F32)).astype(BF16)


def dot(a, b):
    return jnp.dot(a, b, preferred_element_type=F32)


def dot3(a, b):
    return dot(a[0], b[0]) + (dot(a[0], b[1]) + dot(a[1], b[0]))


def whole(*shape):
    return pl.BlockSpec(shape, lambda *_: (0,) * len(shape))


def params():
    return pltpu.CompilerParams(vmem_limit_bytes=48 * 2**20)


def cost(flops, moved):
    return pl.CostEstimate(flops=flops, bytes_accessed=moved, transcendentals=0)


def pick_kernel(rows_ref, member_ref, anc, own_ref, lists_ref, keep_ref, send_ref, picked, sem):
    count, width = picked.shape[0], picked.shape[1] // MEMBERS

    def fetch(i, carry):
        row = jnp.maximum(rows_ref[i], 0)
        pltpu.make_async_copy(anc.at[pl.ds(row, 1), :], picked.at[pl.ds(i, 1), :], sem).start()
        return carry

    lax.fori_loop(0, count, fetch, 0, unroll=8)
    pltpu.make_async_copy(anc.at[pl.ds(0, count), :], picked, sem).wait()
    live = own_ref[...] >= 0
    ancestor = lax.broadcasted_iota(jnp.int32, (width, count), 0)
    for k, out in enumerate((keep_ref, send_ref)):
        member = jnp.bitwise_xor(member_ref[0], k)
        region = picked[:, pl.ds(pl.multiple_of(member * width, 128), width)]
        high, low = split(region)
        chosen = (ancestor == lists_ref[k : k + 1, :]).astype(BF16)
        out[...] = jnp.where(live, dot(high, chosen) + dot(low, chosen), 0.0)


def pick(anc, rows, member, lists):
    count, width = rows.shape[0], anc.shape[1]
    square = jax.ShapeDtypeStruct((count, count), F32)
    return pl.pallas_call(
        pick_kernel,
        grid_spec=pltpu.PrefetchScalarGridSpec(
            num_scalar_prefetch=2,
            grid=(1,),
            in_specs=[pl.BlockSpec(memory_space=pl.ANY), whole(count, 1), whole(MEMBERS, count)],
            out_specs=[whole(count, count)] * 2,
            scratch_shapes=[pltpu.VMEM((count, width), F32), pltpu.SemaphoreType.DMA],
        ),
        out_shape=(square, square),
        compiler_params=params(),
        cost_estimate=cost(4 * count * count * width, 4 * count * width),
        name="pick_compact",
    )(rows, member, anc, rows[:, None], lists)


def off_kernel(order_ref, pieces_ref, *refs):
    blocks, (own_ref, other_ref) = refs[:-2], refs[-2:]
    count = own_ref.shape[0]
    total = None
    for step, block in enumerate(blocks):
        term = dot3(split(pieces_ref[order_ref[step]]), split(block[...]))
        total = term if total is None else total + term
    own_ref[...] = -total[:count]
    other_ref[...] = -total[count:]


def off_parts(order, pieces, blocks):
    count, width = blocks[0].shape
    out = jax.ShapeDtypeStruct((count, width), F32)
    return pl.pallas_call(
        off_kernel,
        grid_spec=pltpu.PrefetchScalarGridSpec(
            num_scalar_prefetch=1,
            grid=(1,),
            in_specs=[whole(*pieces.shape)] + [whole(count, width)] * len(blocks),
            out_specs=[whole(count, width)] * 2,
        ),
        out_shape=(out, out),
        compiler_params=params(),
        cost_estimate=cost(12 * count * count * width * len(blocks), 4 * pieces.size),
        name="off_parts",
    )(order, pieces, *blocks)


def diag_kernel(member_ref, *refs):
    count = (len(refs) - 3) // 2
    strips, blocks, (own_ref, other_ref, total) = refs[:count], refs[count : 2 * count], refs[2 * count :]
    half = own_ref.shape[0]
    for step in range(count):
        strip = split(strips[step][...].T)
        term = dot3(strip, split(blocks[step][...]))
        total[...] = term if step == 0 else total[...] + term
    mine = pl.multiple_of(member_ref[0] * half, 8)
    own_ref[...] = total[pl.ds(mine, half), :]
    other_ref[...] = total[pl.ds(pl.multiple_of(half - mine, 8), half), :]


def diag_parts(member, strips, blocks):
    (count, strip_width), width = strips[0].shape, blocks[0].shape[1]
    half = strip_width // MEMBERS
    out = jax.ShapeDtypeStruct((half, width), F32)
    return pl.pallas_call(
        diag_kernel,
        grid_spec=pltpu.PrefetchScalarGridSpec(
            num_scalar_prefetch=1,
            grid=(1,),
            in_specs=[whole(count, strip_width)] * len(strips) + [whole(count, width)] * len(blocks),
            out_specs=[whole(half, width)] * 2,
            scratch_shapes=[pltpu.VMEM((strip_width, width), F32)],
        ),
        out_shape=(out, out),
        compiler_params=params(),
        cost_estimate=cost(6 * count * strip_width * width * len(blocks), 4 * count * strip_width * len(blocks)),
        name="diag_parts",
    )(member, *strips, *blocks)


def shards(planes, cols, anc_inverse, panel, local_rows, inv_diag):
    axes = ("row", "col")
    row, col = lax.axis_index("row"), lax.axis_index("col")
    plane, member = row // MEMBERS, row % MEMBERS
    grid = [(z, y, c) for z in range(planes) for y in range(MEMBERS) for c in range(cols)]

    def place(z, y, c):
        return (z * MEMBERS + y) * cols + c

    def move(x, target, some=lambda z, y, c: True):
        return lax.ppermute(x, axes, [(place(*d), place(*target(*d))) for d in grid if some(*d)])

    def to_partner(x):
        return move(x, lambda z, y, c: (z, 1 - y, c))

    def round_planes(x):
        out = [x]
        for _ in range(planes - 1):
            out.append(move(out[-1], lambda z, y, c: ((z + 1) % planes, y, c)))
        return out

    def broadcast_strip(x):
        holders, apart = [0], cols // 2
        while apart:
            come = move(x, lambda z, y, c: (z, y, c ^ apart), lambda z, y, c: (c ^ z) in holders)
            has = functools.reduce(jnp.logical_or, [(col ^ plane) == h for h in holders])
            x = jnp.where(has, x, come)
            holders, apart = holders + [h ^ apart for h in holders], apart // 2
        return x

    width = panel.shape[1]
    cut = max(1, round(0.6 * width / 128)) * 128
    cuts = [(0, cut), (cut, width)] if cut < width else [(0, width)]

    lists = jnp.stack([local_rows, to_partner(local_rows)])
    lists = move(lists, lambda z, y, c: (c, y, z))
    keep, send = pick(anc_inverse, local_rows, member[None], lists)
    pieces = jnp.concatenate([keep, to_partner(send)])[None]
    apart, order = cols // 2, [0]
    while apart:
        pieces = jnp.concatenate([pieces, move(pieces, lambda z, y, c: (z, y, c ^ apart))])
        order, apart = order + [k ^ apart for k in order], apart // 2
    where = jnp.zeros((cols,), jnp.int32).at[jnp.array(order)].set(jnp.arange(cols, dtype=jnp.int32))
    wanted = where[col ^ ((plane - jnp.arange(planes, dtype=jnp.int32)) % planes)]

    panels = [round_planes(panel[:, a:b]) for a, b in cuts]
    strips = [broadcast_strip(panel)]
    for step in range(1, planes):
        strips.append(broadcast_strip(jnp.concatenate([part[step] for part in panels], axis=1)))
    off, diag = [], []
    for part in panels:
        own, other = off_parts(wanted, pieces, part)
        off.append(own + to_partner(other))
    for part in off:
        own, other = diag_parts(member[None], strips, round_planes(part))
        diag.append(own + to_partner(other))
    return jnp.concatenate(off, axis=1), inv_diag - jnp.concatenate(diag, axis=1)


def solution(mesh):
    rows, cols = mesh.shape["row"], mesh.shape["col"]
    placed = (P("row", "col"), P("row", "col"), P("row"), P("row", "col"))
    return jax.shard_map(
        functools.partial(shards, rows // MEMBERS, cols),
        mesh=mesh,
        in_specs=placed,
        out_specs=(P("row", "col"), P("row", "col")),
        check_vma=False,
    )
```

time: 407 us -> 155 us (0.38)
  waiting for transfers between devices: 316 us -> 92.4 us
  starting transfers between devices: 0.34 us -> 42.8 us
  local copies, waits for them, and re-layouts: 38.8 us -> 2.31 us
  matrix products: 16.7 us -> 0 us
  blocking collectives: 13.1 us -> 0 us
  between operations: 13.8 us -> 1.1 us
  Pallas kernels: 0 us -> 12.1 us
    psum x1 -> x0, waiting for transfers between devices: 133 us -> none  [broadcast(): return lax.psum(kept, axis)]
    unnamed x5 -> x0, waiting for transfers between devices: 121 us -> none
    ppermute x0 -> x29, waiting for transfers between devices: none -> 92.4 us  [move(): lax.ppermute(x, axes, [(place(*d), place(*target(*d))) for d in grid if s...]
    ppermute x0 -> x29, starting transfers between devices: none -> 42.8 us  [move(): lax.ppermute(x, axes, [(place(*d), place(*target(*d))) for d in grid if s...]
    reduce_scatter x1 -> x0, waiting for transfers between devices: 32.6 us -> none  [shards(): lax.psum_scatter(partial_sum, 'col', scatter_dimension=1, tiled=True)]
    all_gather x1 -> x0, waiting for transfers between devices: 29 us -> none  [shards(): widened = lax.all_gather(panel, 'col', axis=1, tiled=True)]
    gather x3 -> x1, local copies, waits for them, and re-layouts: 20.5 us -> 0.64 us  [shards(): wanted = where[col ^ (plane - jnp.arange(planes, dtype=jnp.int32)) % planes]]
    dot_general x3 -> x0, matrix products: 16.7 us -> none  [the longest x1 8.45 us: shards(): lax.dot_general(widened, sigma_off, (((0,), (0,)), ((), ())), precision=l...]
  transfers between devices with their start and end apart: 4 -> 29, of which waited for: 4 -> 12; matrix products, arithmetic and copies ran while one was open for 7% -> 4% of each run, Pallas kernels for 0% -> 5%
where the time goes in v1:
time: 155 us; the launch traced here: 156 us
  waiting for transfers between devices  92.4 us (60%)
  starting transfers between devices  42.8 us (28%)
  Pallas kernels  12.1 us (8%)
  other arithmetic  5.67 us (4%)
  local copies, waits for them, and re-layouts  2.31 us (1%)
    ppermute x29, waiting for transfers between devices, move(): lax.ppermute(x, axes, [(place(*d), place(*target(*d))) for d in grid if s...  92.4 us
    ppermute x29, starting transfers between devices, move(): lax.ppermute(x, axes, [(place(*d), place(*target(*d))) for d in grid if s...  42.8 us
    pallas_call x1, Pallas kernels, pick(): pl.pallas_call(pick_kernel, grid_spec=pltpu.PrefetchScalarGridSpec(num_sc...  4.51 us
    pallas_call x2, Pallas kernels, diag_parts(): pl.pallas_call(diag_kernel, grid_spec=pltpu.PrefetchScalarGridSpec(num_sc...  3.81 us
    pallas_call x2, Pallas kernels, off_parts(): pl.pallas_call(off_kernel, grid_spec=pltpu.PrefetchScalarGridSpec(num_sca...  3.78 us
  transfers between devices with their start and end apart: 29, of which 12 were waited for; matrix products, arithmetic and copies ran while one was open for 4% of the time, Pallas kernels for 5%

profile of v1, /device:TPU:0, one launch (start us, length us, event | category | flops | bytes accessed | tf_op | source)
XLA Modules:
  0.0 156.4 jit_solution(15779944312517282300)
XLA Ops:
  0.6 3.0 %collective-permute-start = (s32[240]{0:T(256)}, s32[240]{0:T(256)S(1)}, u32[]{:S(2)}, u32[]{:S(2)}) collective-permute-start(s32[240]{0:T(256)} %rows_ref.1), channel_id=1, source_target_pairs={{0,4},{1,5},{2,6},{3,7},{4,0},{5,1},{6,2},{7,3},{8,12},{9,13},{10,... | collective-permute-start | bytes 2888 | tf_op jit(solution)/shard_map/ppermute | solution.py:151
  3.7 1.8 %collective-permute-done = s32[240]{0:T(256)S(1)} collective-permute-done((s32[240]{0:T(256)}, s32[240]{0:T(256)S(1)}, u32[]{:S(2)}, u32[]{:S(2)}) %collective-permute-start) | collective-permute-done | bytes 992 | tf_op jit(solution)/shard_map/ppermute | solution.py:151
  5.4 0.7 pad_add_fusion
  6.1 0.6 collective-permute-start.1
  6.8 0.8 copy.7.own_ref
  7.6 0.0 collective-permute-done.1.lists_ref
  7.6 0.0 copy-start
  7.6 0.7 copy-done
  8.3 4.5 %pick_compact.1 = (f32[240,240]{1,0:T(8,128)S(1)}, f32[240,240]{1,0:T(8,128)S(1)}) custom-call(s32[240]{0:T(256)S(1)} %copy-done, s32[1]{0:T(128)} %bitcast.1.member_ref, f32[2048,4096]{1,0:T(8,128)} %anc.1, s32[240,1]{1,0:T(8,128)S(1)} %copy.7.own_ref, s32[2,240]{1,0:T(2,128)S(1)} %collective-permute-done.1.lists_ref), custom_call_target="tpu_custom_call" | custom-call | flops 943718400 | bytes 3932160 | tf_op jit(solution)/shard_map/pick_compact/pallas_call | solution.py:63
  12.8 9.9 %collective-permute-start.2 = (f32[240,240]{1,0:T(8,128)S(1)}, f32[240,240]{1,0:T(8,128)S(1)}, u32[]{:S(2)}, u32[]{:S(2)}) collective-permute-start(f32[240,240]{1,0:T(8,128)S(1)} %get-tuple-element.13), channel_id=1, source_target_pairs={{0,4},{1,5},{2,6},{3,7},{4,0},{5,1},{6,2},{7,3},{8,12},{9,13},{10,... | collective-permute-start | bytes 691208 | tf_op jit(solution)/shard_map/ppermute | solution.py:151
  22.7 4.2 %collective-permute-done.2 = f32[240,240]{1,0:T(8,128)S(1)} collective-permute-done((f32[240,240]{1,0:T(8,128)S(1)}, f32[240,240]{1,0:T(8,128)S(1)}, u32[]{:S(2)}, u32[]{:S(2)}) %collective-permute-start.2) | collective-permute-done | bytes 230432 | tf_op jit(solution)/shard_map/ppermute | solution.py:151
  26.9 8.8 %collective-permute-start.3 = (f32[1,480,240]{2,1,0:T(8,128)S(1)}, f32[1,480,240]{2,1,0:T(8,128)S(1)}, u32[]{:S(2)}, u32[]{:S(2)}) collective-permute-start(f32[1,480,240]{2,1,0:T(8,128)S(1)} %maximum_bitcast_fusion), channel_id=1, source_target_pairs={{0,2},{1,3},{2,0},{3,1},{4,6},{5,7},{6,4},{7,5},{8,10},{9,11},{10,... | collective-permute-start | bytes 1382408 | tf_op jit(solution)/shard_map/ppermute | solution.py:151
  35.8 0.1 collective-permute-start.5
  35.8 11.0 %collective-permute-done.5.refs_1_ = f32[240,384]{1,0:T(8,128)S(1)} collective-permute-done((f32[240,384]{1,0:T(8,128)S(1)}, f32[240,384]{1,0:T(8,128)S(1)}, u32[]{:S(2)}, u32[]{:S(2)}) %collective-permute-start.5) | collective-permute-done | bytes 368672 | tf_op jit(solution)/shard_map/ppermute | solution.py:151
  46.8 3.0 %collective-permute-start.13 = (f32[240,640]{1,0:T(8,128)S(1)}, f32[240,640]{1,0:T(8,128)}, u32[]{:S(2)}, u32[]{:S(2)}) collective-permute-start(f32[240,640]{1,0:T(8,128)S(1)} %copy-done.2), channel_id=1, source_target_pairs={{0,2},{4,6},{9,11},{13,15},{18,16},{22,20},{27,25},{31,29}} | collective-permute-start | bytes 1843208 | tf_op jit(solution)/shard_map/ppermute | solution.py:151
  49.9 0.1 collective-permute-start.9
  50.0 1.0 pad_maximum_fusion.1
  51.0 0.0 collective-permute-start.4
  51.0 11.2 %collective-permute-done.9.refs_1_ = f32[240,256]{1,0:T(8,128)S(1)} collective-permute-done((f32[240,256]{1,0:T(8,128)S(1)}, f32[240,256]{1,0:T(8,128)S(1)}, u32[]{:S(2)}, u32[]{:S(2)}) %collective-permute-start.9) | collective-permute-done | bytes 245792 | tf_op jit(solution)/shard_map/ppermute | solution.py:151
  62.2 0.6 gather_fusion
  62.9 0.0 collective-permute-done.6.refs_2_
  62.9 0.0 collective-permute-start.7
  63.0 2.5 %collective-permute-start.15 = (f32[240,640]{1,0:T(8,128)S(1)}, f32[240,640]{1,0:T(8,128)S(1)}, u32[]{:S(2)}, u32[]{:S(2)}) collective-permute-start(f32[240,640]{1,0:T(8,128)S(1)} %constant_dynamic-update-slice_fusion), channel_id=1, source_target_pairs={{0,2},{4,6},{9,11},{13,15},{18,16},{22,20},{27,25},{31,29}} | collective-permute-start | bytes 1843208 | tf_op jit(solution)/shard_map/ppermute | solution.py:151
  65.5 7.4 %collective-permute-done.10.refs_2_ = f32[240,256]{1,0:T(8,128)S(1)} collective-permute-done((f32[240,256]{1,0:T(8,128)S(1)}, f32[240,256]{1,0:T(8,128)S(1)}, u32[]{:S(2)}, u32[]{:S(2)}) %collective-permute-start.10) | collective-permute-done | bytes 245792 | tf_op jit(solution)/shard_map/ppermute | solution.py:151
  72.9 6.3 %collective-permute-done.7.refs_3_ = f32[240,384]{1,0:T(8,128)S(1)} collective-permute-done((f32[240,384]{1,0:T(8,128)S(1)}, f32[240,384]{1,0:T(8,128)S(1)}, u32[]{:S(2)}, u32[]{:S(2)}) %collective-permute-start.7) | collective-permute-done | bytes 368672 | tf_op jit(solution)/shard_map/ppermute | solution.py:151
  79.2 2.8 %collective-permute-start.17 = (f32[240,640]{1,0:T(8,128)S(1)}, f32[240,640]{1,0:T(8,128)S(1)}, u32[]{:S(2)}, u32[]{:S(2)}) collective-permute-start(f32[240,640]{1,0:T(8,128)S(1)} %constant_dynamic-update-slice_fusion.2), channel_id=1, source_target_pairs={{0,2},{4,6},{9,11},{13,15},{18,16},{22,20},{27,25},{31,29}} | collective-permute-start | bytes 1843208 | tf_op jit(solution)/shard_map/ppermute | solution.py:151
  82.1 0.0 collective-permute-done.11.refs_3_
  82.1 2.6 %collective-permute-start.19 = (f32[240,640]{1,0:T(8,128)S(1)}, f32[240,640]{1,0:T(8,128)S(1)}, u32[]{:S(2)}, u32[]{:S(2)}) collective-permute-start(f32[240,640]{1,0:T(8,128)S(1)} %constant_dynamic-update-slice_fusion.4), channel_id=1, source_target_pairs={{0,2},{4,6},{9,11},{13,15},{18,16},{22,20},{27,25},{31,29}} | collective-permute-start | bytes 1843208 | tf_op jit(solution)/shard_map/ppermute | solution.py:151
  84.7 1.3 pad_maximum_fusion.pieces_ref
  86.1 2.2 %off_parts.2 = (f32[240,384]{1,0:T(8,128)S(1)}, f32[240,384]{1,0:T(8,128)S(1)}) custom-call(s32[4]{0:T(128)S(1)} %gather_fusion, f32[4,480,240]{2,1,0:T(8,128)S(1)} %pad_maximum_fusion.pieces_ref, f32[240,384]{1,0:T(8,128)S(1)} %slice.6.refs_0_, f32[240,384]{1,0:T(8,128)S(1)} %collective-permute-done.5.refs_1_, ...), custom_call_target="tpu_custom_call" | custom-call | flops 1061683200 | bytes 1843200 | tf_op jit(solution)/shard_map/off_parts/pallas_call | solution.py:93
  88.3 0.9 collective-permute-start.8
  89.2 0.1 broadcast_select_fusion.3
  89.2 1.3 collective-permute-start.14
  90.6 0.0 collective-permute-done.15
  90.6 0.1 broadcast_select_fusion.2
  90.7 1.3 collective-permute-start.16
  92.0 3.9 %collective-permute-done.8 = f32[240,384]{1,0:T(8,128)S(1)} collective-permute-done((f32[240,384]{1,0:T(8,128)S(1)}, f32[240,384]{1,0:T(8,128)S(1)}, u32[]{:S(2)}, u32[]{:S(2)}) %collective-permute-start.8) | collective-permute-done | bytes 368672 | tf_op jit(solution)/shard_map/ppermute | solution.py:151
  95.9 0.1 collective-permute-start.21
  96.0 0.1 broadcast_select_fusion.1
  96.1 1.3 collective-permute-start.18
  97.4 1.5 off_parts.3
  99.0 0.8 collective-permute-start.12
  99.8 0.1 broadcast_select_fusion
  99.9 1.3 collective-permute-start.20
  101.2 4.1 %collective-permute-done.21.refs_5_ = f32[240,384]{1,0:T(8,128)S(1)} collective-permute-done((f32[240,384]{1,0:T(8,128)S(1)}, f32[240,384]{1,0:T(8,128)S(1)}, u32[]{:S(2)}, u32[]{:S(2)}) %collective-permute-start.21) | collective-permute-done | bytes 368672 | tf_op jit(solution)/shard_map/ppermute | solution.py:151
  105.3 0.0 collective-permute-start.22
  105.3 0.1 broadcast_select_fusion.7.refs_0_
  105.4 0.1 collective-permute-start.25
  105.5 0.0 collective-permute-done.16
  105.5 0.1 broadcast_select_fusion.6.refs_1_
  105.6 14.6 %collective-permute-done.25.refs_5_ = f32[240,256]{1,0:T(8,128)S(1)} collective-permute-done((f32[240,256]{1,0:T(8,128)S(1)}, f32[240,256]{1,0:T(8,128)S(1)}, u32[]{:S(2)}, u32[]{:S(2)}) %collective-permute-start.25) | collective-permute-done | bytes 245792 | tf_op jit(solution)/shard_map/ppermute | solution.py:151
  120.2 0.1 broadcast_select_fusion.5.refs_2_
  120.3 10.6 %collective-permute-done.26.refs_6_ = f32[240,256]{1,0:T(8,128)S(1)} collective-permute-done((f32[240,256]{1,0:T(8,128)S(1)}, f32[240,256]{1,0:T(8,128)S(1)}, u32[]{:S(2)}, u32[]{:S(2)}) %collective-permute-start.26) | collective-permute-done | bytes 245792 | tf_op jit(solution)/shard_map/ppermute | solution.py:151
  130.9 0.1 broadcast_select_fusion.4.refs_3_
  131.0 7.3 %collective-permute-done.23.refs_7_ = f32[240,384]{1,0:T(8,128)S(1)} collective-permute-done((f32[240,384]{1,0:T(8,128)S(1)}, f32[240,384]{1,0:T(8,128)S(1)}, u32[]{:S(2)}, u32[]{:S(2)}) %collective-permute-start.23) | collective-permute-done | bytes 368672 | tf_op jit(solution)/shard_map/ppermute | solution.py:151
  138.3 2.3 %diag_parts.2 = (f32[320,384]{1,0:T(8,128)S(1)}, f32[320,384]{1,0:T(8,128)S(1)}) custom-call(s32[1]{0:T(128)} %bitcast.1.member_ref, f32[240,640]{1,0:T(8,128)S(1)} %broadcast_select_fusion.7.refs_0_, f32[240,640]{1,0:T(8,128)S(1)} %broadcast_select_fusion.6.refs_1_, f32[240,640]{1,0:T(8,128)S(1)} %broadcast_select_fusion.5.refs_2_, ...), custom_call_target="tpu_custom_call" | custom-call | flops 1415577600 | bytes 2457600 | tf_op jit(solution)/shard_map/diag_parts/pallas_call | solution.py:125
  140.7 1.3 collective-permute-start.24
  142.0 1.5 diag_parts.3
  143.5 0.0 copy-start.3
  143.5 0.9 collective-permute-start.28
  144.3 0.9 pad_maximum_fusion.2
  145.2 10.1 %collective-permute-done.28 = f32[320,256]{1,0:T(8,128)S(1)} collective-permute-done((f32[320,256]{1,0:T(8,128)S(1)}, f32[320,256]{1,0:T(8,128)S(1)}, u32[]{:S(2)}, u32[]{:S(2)}) %collective-permute-start.28) | collective-permute-done | bytes 327712 | tf_op jit(solution)/shard_map/ppermute | solution.py:151
  155.3 0.1 add.49
  155.4 1.0 maximum_subtract_fusion
  (37 shorter events, 0.4 us)
Async XLA Ops:
  0.6 4.8 %collective-permute-start = (s32[240]{0:T(256)}, s32[240]{0:T(256)S(1)}, u32[]{:S(2)}, u32[]{:S(2)}) collective-permute-start(s32[240]{0:T(256)} %rows_ref.1), channel_id=1, source_target_pairs={{0,4},{1,5},{2,6},{3,7},{4,0},{5,1},{6,2},{7,3},{8,12},{9,13},{10,... | collective-permute-start | bytes 2888 | tf_op jit(solution)/shard_map/ppermute | solution.py:151
  6.1 1.5 collective-permute-start.1
  7.6 0.7 copy-start
  8.3 27.4 %copy-start.2 = (f32[240,640]{1,0:T(8,128)S(1)}, f32[240,640]{1,0:T(8,128)}, u32[]{:S(2)}) copy-start(f32[240,640]{1,0:T(8,128)} %param.6) | copy-start | bytes 1843204
  12.8 14.0 %collective-permute-start.2 = (f32[240,240]{1,0:T(8,128)S(1)}, f32[240,240]{1,0:T(8,128)S(1)}, u32[]{:S(2)}, u32[]{:S(2)}) collective-permute-start(f32[240,240]{1,0:T(8,128)S(1)} %get-tuple-element.13), channel_id=1, source_target_pairs={{0,4},{1,5},{2,6},{3,7},{4,0},{5,1},{6,2},{7,3},{8,12},{9,13},{10,... | collective-permute-start | bytes 691208 | tf_op jit(solution)/shard_map/ppermute | solution.py:151
  26.9 35.4 %copy-start.1 = (s32[4]{0:T(128)S(1)}, s32[4]{0:T(128)}, u32[]{:S(2)}) copy-start(s32[4]{0:T(128)} %constant.57) | copy-start | bytes 52
  26.9 23.1 %collective-permute-start.3 = (f32[1,480,240]{2,1,0:T(8,128)S(1)}, f32[1,480,240]{2,1,0:T(8,128)S(1)}, u32[]{:S(2)}, u32[]{:S(2)}) collective-permute-start(f32[1,480,240]{2,1,0:T(8,128)S(1)} %maximum_bitcast_fusion), channel_id=1, source_target_pairs={{0,2},{1,3},{2,0},{3,1},{4,6},{5,7},{6,4},{7,5},{8,10},{9,11},{10,... | collective-permute-start | bytes 1382408 | tf_op jit(solution)/shard_map/ppermute | solution.py:151
  35.8 11.1 %collective-permute-start.5 = (f32[240,384]{1,0:T(8,128)S(1)}, f32[240,384]{1,0:T(8,128)S(1)}, u32[]{:S(2)}, u32[]{:S(2)}) collective-permute-start(f32[240,384]{1,0:T(8,128)S(1)} %slice.6.refs_0_), channel_id=1, source_target_pairs={{0,8},{1,9},{2,10},{3,11},{4,12},{5,13},{6,14},{7,15},{8,16},{9,17... | collective-permute-start | bytes 1105928 | tf_op jit(solution)/shard_map/ppermute | solution.py:151
  46.8 16.0 %collective-permute-start.6 = (f32[240,384]{1,0:T(8,128)S(1)}, f32[240,384]{1,0:T(8,128)S(1)}, u32[]{:S(2)}, u32[]{:S(2)}) collective-permute-start(f32[240,384]{1,0:T(8,128)S(1)} %collective-permute-done.5.refs_1_), channel_id=1, source_target_pairs={{0,8},{1,9},{2,10},{3,11},{4,12},{5,13},{6,14},{7,15},{8,16},{9,17... | collective-permute-start | bytes 1105928 | tf_op jit(solution)/shard_map/ppermute | solution.py:151
  46.8 42.3 %collective-permute-start.13 = (f32[240,640]{1,0:T(8,128)S(1)}, f32[240,640]{1,0:T(8,128)}, u32[]{:S(2)}, u32[]{:S(2)}) collective-permute-start(f32[240,640]{1,0:T(8,128)S(1)} %copy-done.2), channel_id=1, source_target_pairs={{0,2},{4,6},{9,11},{13,15},{18,16},{22,20},{27,25},{31,29}} | collective-permute-start | bytes 1843208 | tf_op jit(solution)/shard_map/ppermute | solution.py:151
  49.9 12.3 %collective-permute-start.9 = (f32[240,256]{1,0:T(8,128)S(1)}, f32[240,256]{1,0:T(8,128)S(1)}, u32[]{:S(2)}, u32[]{:S(2)}) collective-permute-start(f32[240,256]{1,0:T(8,128)S(1)} %slice.7.refs_0_), channel_id=1, source_target_pairs={{0,8},{1,9},{2,10},{3,11},{4,12},{5,13},{6,14},{7,15},{8,16},{9,17... | collective-permute-start | bytes 737288 | tf_op jit(solution)/shard_map/ppermute | solution.py:151
  51.0 33.7 %collective-permute-start.4 = (f32[2,480,240]{2,1,0:T(8,128)}, f32[2,480,240]{2,1,0:T(8,128)}, u32[]{:S(2)}, u32[]{:S(2)}) collective-permute-start(f32[2,480,240]{2,1,0:T(8,128)} %pad_maximum_fusion.1), channel_id=1, source_target_pairs={{0,1},{1,0},{2,3},{3,2},{4,5},{5,4},{6,7},{7,6},{8,9},{9,8},{10,11... | collective-permute-start | bytes 2764808 | tf_op jit(solution)/shard_map/ppermute | solution.py:151
  62.2 10.7 %collective-permute-start.10 = (f32[240,256]{1,0:T(8,128)S(1)}, f32[240,256]{1,0:T(8,128)S(1)}, u32[]{:S(2)}, u32[]{:S(2)}) collective-permute-start(f32[240,256]{1,0:T(8,128)S(1)} %collective-permute-done.9.refs_1_), channel_id=1, source_target_pairs={{0,8},{1,9},{2,10},{3,11},{4,12},{5,13},{6,14},{7,15},{8,16},{9,17... | collective-permute-start | bytes 737288 | tf_op jit(solution)/shard_map/ppermute | solution.py:151
  62.9 16.4 %collective-permute-start.7 = (f32[240,384]{1,0:T(8,128)S(1)}, f32[240,384]{1,0:T(8,128)S(1)}, u32[]{:S(2)}, u32[]{:S(2)}) collective-permute-start(f32[240,384]{1,0:T(8,128)S(1)} %collective-permute-done.6.refs_2_), channel_id=1, source_target_pairs={{0,8},{1,9},{2,10},{3,11},{4,12},{5,13},{6,14},{7,15},{8,16},{9,17... | collective-permute-start | bytes 1105928 | tf_op jit(solution)/shard_map/ppermute | solution.py:151
  63.0 27.6 %collective-permute-start.15 = (f32[240,640]{1,0:T(8,128)S(1)}, f32[240,640]{1,0:T(8,128)S(1)}, u32[]{:S(2)}, u32[]{:S(2)}) collective-permute-start(f32[240,640]{1,0:T(8,128)S(1)} %constant_dynamic-update-slice_fusion), channel_id=1, source_target_pairs={{0,2},{4,6},{9,11},{13,15},{18,16},{22,20},{27,25},{31,29}} | collective-permute-start | bytes 1843208 | tf_op jit(solution)/shard_map/ppermute | solution.py:151
  72.9 9.2 %collective-permute-start.11 = (f32[240,256]{1,0:T(8,128)S(1)}, f32[240,256]{1,0:T(8,128)S(1)}, u32[]{:S(2)}, u32[]{:S(2)}) collective-permute-start(f32[240,256]{1,0:T(8,128)S(1)} %collective-permute-done.10.refs_2_), channel_id=1, source_target_pairs={{0,8},{1,9},{2,10},{3,11},{4,12},{5,13},{6,14},{7,15},{8,16},{9,17... | collective-permute-start | bytes 737288 | tf_op jit(solution)/shard_map/ppermute | solution.py:151
  79.2 16.8 %collective-permute-start.17 = (f32[240,640]{1,0:T(8,128)S(1)}, f32[240,640]{1,0:T(8,128)S(1)}, u32[]{:S(2)}, u32[]{:S(2)}) collective-permute-start(f32[240,640]{1,0:T(8,128)S(1)} %constant_dynamic-update-slice_fusion.2), channel_id=1, source_target_pairs={{0,2},{4,6},{9,11},{13,15},{18,16},{22,20},{27,25},{31,29}} | collective-permute-start | bytes 1843208 | tf_op jit(solution)/shard_map/ppermute | solution.py:151
  82.1 16.9 %collective-permute-start.19 = (f32[240,640]{1,0:T(8,128)S(1)}, f32[240,640]{1,0:T(8,128)S(1)}, u32[]{:S(2)}, u32[]{:S(2)}) collective-permute-start(f32[240,640]{1,0:T(8,128)S(1)} %constant_dynamic-update-slice_fusion.4), channel_id=1, source_target_pairs={{0,2},{4,6},{9,11},{13,15},{18,16},{22,20},{27,25},{31,29}} | collective-permute-start | bytes 1843208 | tf_op jit(solution)/shard_map/ppermute | solution.py:151
  88.3 7.6 %collective-permute-start.8 = (f32[240,384]{1,0:T(8,128)S(1)}, f32[240,384]{1,0:T(8,128)S(1)}, u32[]{:S(2)}, u32[]{:S(2)}) collective-permute-start(f32[240,384]{1,0:T(8,128)S(1)} %get-tuple-element.15), channel_id=1, source_target_pairs={{0,4},{1,5},{2,6},{3,7},{4,0},{5,1},{6,2},{7,3},{8,12},{9,13},{10,... | collective-permute-start | bytes 1105928 | tf_op jit(solution)/shard_map/ppermute | solution.py:151
  89.2 10.7 %collective-permute-start.14 = (f32[240,640]{1,0:T(8,128)S(1)}, f32[240,640]{1,0:T(8,128)S(1)}, u32[]{:S(2)}, u32[]{:S(2)}) collective-permute-start(f32[240,640]{1,0:T(8,128)S(1)} %broadcast_select_fusion.3), channel_id=1, source_target_pairs={{0,1},{2,3},{4,5},{6,7},{9,8},{11,10},{13,12},{15,14},{16,17},{18,... | collective-permute-start | bytes 1843208 | tf_op jit(solution)/shard_map/ppermute | solution.py:151
  90.7 14.8 %collective-permute-start.16 = (f32[240,640]{1,0:T(8,128)S(1)}, f32[240,640]{1,0:T(8,128)S(1)}, u32[]{:S(2)}, u32[]{:S(2)}) collective-permute-start(f32[240,640]{1,0:T(8,128)S(1)} %broadcast_select_fusion.2), channel_id=1, source_target_pairs={{0,1},{2,3},{4,5},{6,7},{9,8},{11,10},{13,12},{15,14},{16,17},{18,... | collective-permute-start | bytes 1843208 | tf_op jit(solution)/shard_map/ppermute | solution.py:151
  95.9 9.4 %collective-permute-start.21 = (f32[240,384]{1,0:T(8,128)S(1)}, f32[240,384]{1,0:T(8,128)S(1)}, u32[]{:S(2)}, u32[]{:S(2)}) collective-permute-start(f32[240,384]{1,0:T(8,128)S(1)} %add.47.refs_4_), channel_id=1, source_target_pairs={{0,8},{1,9},{2,10},{3,11},{4,12},{5,13},{6,14},{7,15},{8,16},{9,17... | collective-permute-start | bytes 1105928 | tf_op jit(solution)/shard_map/ppermute | solution.py:151
  96.1 24.1 %collective-permute-start.18 = (f32[240,640]{1,0:T(8,128)S(1)}, f32[240,640]{1,0:T(8,128)S(1)}, u32[]{:S(2)}, u32[]{:S(2)}) collective-permute-start(f32[240,640]{1,0:T(8,128)S(1)} %broadcast_select_fusion.1), channel_id=1, source_target_pairs={{0,1},{2,3},{4,5},{6,7},{9,8},{11,10},{13,12},{15,14},{16,17},{18,... | collective-permute-start | bytes 1843208 | tf_op jit(solution)/shard_map/ppermute | solution.py:151
  99.0 6.4 %collective-permute-start.12 = (f32[240,256]{1,0:T(8,128)S(1)}, f32[240,256]{1,0:T(8,128)S(1)}, u32[]{:S(2)}, u32[]{:S(2)}) collective-permute-start(f32[240,256]{1,0:T(8,128)S(1)} %get-tuple-element.17), channel_id=1, source_target_pairs={{0,4},{1,5},{2,6},{3,7},{4,0},{5,1},{6,2},{7,3},{8,12},{9,13},{10,... | collective-permute-start | bytes 737288 | tf_op jit(solution)/shard_map/ppermute | solution.py:151
  99.9 31.0 %collective-permute-start.20 = (f32[240,640]{1,0:T(8,128)S(1)}, f32[240,640]{1,0:T(8,128)S(1)}, u32[]{:S(2)}, u32[]{:S(2)}) collective-permute-start(f32[240,640]{1,0:T(8,128)S(1)} %broadcast_select_fusion), channel_id=1, source_target_pairs={{0,1},{2,3},{4,5},{6,7},{9,8},{11,10},{13,12},{15,14},{16,17},{18,... | collective-permute-start | bytes 1843208 | tf_op jit(solution)/shard_map/ppermute | solution.py:151
  105.3 14.9 %collective-permute-start.22 = (f32[240,384]{1,0:T(8,128)S(1)}, f32[240,384]{1,0:T(8,128)S(1)}, u32[]{:S(2)}, u32[]{:S(2)}) collective-permute-start(f32[240,384]{1,0:T(8,128)S(1)} %collective-permute-done.21.refs_5_), channel_id=1, source_target_pairs={{0,8},{1,9},{2,10},{3,11},{4,12},{5,13},{6,14},{7,15},{8,16},{9,17... | collective-permute-start | bytes 1105928 | tf_op jit(solution)/shard_map/ppermute | solution.py:151
  105.4 14.8 %collective-permute-start.25 = (f32[240,256]{1,0:T(8,128)S(1)}, f32[240,256]{1,0:T(8,128)S(1)}, u32[]{:S(2)}, u32[]{:S(2)}) collective-permute-start(f32[240,256]{1,0:T(8,128)S(1)} %add.48.refs_4_), channel_id=1, source_target_pairs={{0,8},{1,9},{2,10},{3,11},{4,12},{5,13},{6,14},{7,15},{8,16},{9,17... | collective-permute-start | bytes 737288 | tf_op jit(solution)/shard_map/ppermute | solution.py:151
  120.2 10.7 %collective-permute-start.26 = (f32[240,256]{1,0:T(8,128)S(1)}, f32[240,256]{1,0:T(8,128)S(1)}, u32[]{:S(2)}, u32[]{:S(2)}) collective-permute-start(f32[240,256]{1,0:T(8,128)S(1)} %collective-permute-done.25.refs_5_), channel_id=1, source_target_pairs={{0,8},{1,9},{2,10},{3,11},{4,12},{5,13},{6,14},{7,15},{8,16},{9,17... | collective-permute-start | bytes 737288 | tf_op jit(solution)/shard_map/ppermute | solution.py:151
  120.2 18.1 %collective-permute-start.23 = (f32[240,384]{1,0:T(8,128)S(1)}, f32[240,384]{1,0:T(8,128)S(1)}, u32[]{:S(2)}, u32[]{:S(2)}) collective-permute-start(f32[240,384]{1,0:T(8,128)S(1)} %collective-permute-done.22.refs_6_), channel_id=1, source_target_pairs={{0,8},{1,9},{2,10},{3,11},{4,12},{5,13},{6,14},{7,15},{8,16},{9,17... | collective-permute-start | bytes 1105928 | tf_op jit(solution)/shard_map/ppermute | solution.py:151
  130.9 11.1 %collective-permute-start.27 = (f32[240,256]{1,0:T(8,128)S(1)}, f32[240,256]{1,0:T(8,128)S(1)}, u32[]{:S(2)}, u32[]{:S(2)}) collective-permute-start(f32[240,256]{1,0:T(8,128)S(1)} %collective-permute-done.26.refs_6_), channel_id=1, source_target_pairs={{0,8},{1,9},{2,10},{3,11},{4,12},{5,13},{6,14},{7,15},{8,16},{9,17... | collective-permute-start | bytes 737288 | tf_op jit(solution)/shard_map/ppermute | solution.py:151
  140.7 14.7 %collective-permute-start.24 = (f32[320,384]{1,0:T(8,128)S(1)}, f32[320,384]{1,0:T(8,128)S(1)}, u32[]{:S(2)}, u32[]{:S(2)}) collective-permute-start(f32[320,384]{1,0:T(8,128)S(1)} %get-tuple-element.19), channel_id=1, source_target_pairs={{0,4},{1,5},{2,6},{3,7},{4,0},{5,1},{6,2},{7,3},{8,12},{9,13},{10,... | collective-permute-start | bytes 1474568 | tf_op jit(solution)/shard_map/ppermute | solution.py:151
  143.5 11.9 %copy-start.3 = (f32[320,640]{1,0:T(8,128)S(1)}, f32[320,640]{1,0:T(8,128)}, u32[]{:S(2)}) copy-start(f32[320,640]{1,0:T(8,128)} %param.8) | copy-start | bytes 2457604
  143.5 11.8 %collective-permute-start.28 = (f32[320,256]{1,0:T(8,128)S(1)}, f32[320,256]{1,0:T(8,128)S(1)}, u32[]{:S(2)}, u32[]{:S(2)}) collective-permute-start(f32[320,256]{1,0:T(8,128)S(1)} %get-tuple-element.21), channel_id=1, source_target_pairs={{0,4},{1,5},{2,6},{3,7},{4,0},{5,1},{6,2},{7,3},{8,12},{9,13},{10,... | collective-permute-start | bytes 983048 | tf_op jit(solution)/shard_map/ppermute | solution.py:151

commit v2 on v1

v2 whole, which is shorter than its diff:
```python
import functools

import jax
import jax.numpy as jnp
from jax import lax
from jax.experimental import pallas as pl
from jax.experimental.pallas import tpu as pltpu
from jax.sharding import PartitionSpec as P

MEMBERS = 2
CUT = 0.6
GATED = 3
BF16 = jnp.bfloat16
F32 = jnp.float32


def split(x):
    high = x.astype(BF16)
    return high, (x - high.astype(F32)).astype(BF16)


def dot(a, b):
    return jnp.dot(a, b, preferred_element_type=F32)


def dot3(a, b):
    return dot(a[0], b[0]) + (dot(a[0], b[1]) + dot(a[1], b[0]))


def whole(*shape):
    return pl.BlockSpec(shape, lambda *_: (0,) * len(shape))


def params():
    return pltpu.CompilerParams(vmem_limit_bytes=48 * 2**20)


def cost(flops, moved):
    return pl.CostEstimate(flops=flops, bytes_accessed=moved, transcendentals=0)


def pick_kernel(rows_ref, member_ref, anc, own_ref, lists_ref, keep_ref, send_ref, picked, sem):
    count, width = picked.shape[0], picked.shape[1] // MEMBERS

    def fetch(i, carry):
        row = jnp.where(rows_ref[i] < 0, i, rows_ref[i])
        pltpu.make_async_copy(anc.at[pl.ds(row, 1), :], picked.at[pl.ds(i, 1), :], sem).start()
        return carry

    lax.fori_loop(0, count, fetch, 0, unroll=8)
    live = own_ref[...] >= 0
    ancestor = lax.broadcasted_iota(jnp.int32, (width, count), 0)
    chosen = [(ancestor == lists_ref[k : k + 1, :]).astype(BF16) for k in range(MEMBERS)]
    pltpu.make_async_copy(anc.at[pl.ds(0, count), :], picked, sem).wait()
    for k, out in enumerate((keep_ref, send_ref)):
        member = jnp.bitwise_xor(member_ref[0], k)
        high, low = split(picked[:, pl.ds(pl.multiple_of(member * width, 128), width)])
        out[...] = jnp.where(live, dot(high, chosen[k]) + dot(low, chosen[k]), 0.0)


def pick(anc, rows, member, lists):
    count, width = rows.shape[0], anc.shape[1]
    square = jax.ShapeDtypeStruct((count, count), F32)
    return pl.pallas_call(
        pick_kernel,
        grid_spec=pltpu.PrefetchScalarGridSpec(
            num_scalar_prefetch=2,
            grid=(1,),
            in_specs=[pl.BlockSpec(memory_space=pl.ANY), whole(count, 1), whole(MEMBERS, count)],
            out_specs=[whole(count, count)] * 2,
            scratch_shapes=[pltpu.VMEM((count, width), F32), pltpu.SemaphoreType.DMA],
        ),
        out_shape=(square, square),
        compiler_params=params(),
        cost_estimate=cost(4 * count * count * width, 16 * count * width),
        name="pick_compact",
    )(rows, member, anc, rows[:, None], lists)


def off_kernel(count, order_ref, *refs):
    own, other, blocks, (own_ref, other_ref) = refs[:count], refs[count : 2 * count], refs[2 * count : -2], refs[-2:]
    rows = own_ref.shape[0]
    total = None
    for step, block in enumerate(blocks):
        piece = jnp.concatenate([own[0][...], other[0][...]])
        for k in range(1, count):
            piece = jnp.where(order_ref[step] == k, jnp.concatenate([own[k][...], other[k][...]]), piece)
        term = dot3(split(piece), split(block[...]))
        total = term if total is None else total + term
    own_ref[...] = -total[:rows]
    other_ref[...] = -total[rows:]


def off_parts(order, own, other, blocks):
    count, width = blocks[0].shape
    out = jax.ShapeDtypeStruct((count, width), F32)
    return pl.pallas_call(
        functools.partial(off_kernel, len(own)),
        grid_spec=pltpu.PrefetchScalarGridSpec(
            num_scalar_prefetch=1,
            grid=(1,),
            in_specs=[whole(*x.shape) for x in (*own, *other, *blocks)],
            out_specs=[whole(count, width)] * 2,
        ),
        out_shape=(out, out),
        compiler_params=params(),
        cost_estimate=cost(12 * count * count * width * len(blocks), 8 * count * count * len(blocks)),
        name="off_parts",
    )(order, *own, *other, *blocks)


def turn_kernel(flag_ref, held, come, high_ref, low_ref):
    strip = jnp.where(flag_ref[0] > 0, held[...], come[...]).T
    high_ref[...], low_ref[...] = split(strip)


def turn(flag, held, come):
    count, width = held.shape
    out = jax.ShapeDtypeStruct((width, count), BF16)
    return pl.pallas_call(
        turn_kernel,
        grid_spec=pltpu.PrefetchScalarGridSpec(
            num_scalar_prefetch=1,
            grid=(1,),
            in_specs=[whole(count, width)] * 2,
            out_specs=[whole(width, count)] * 2,
        ),
        out_shape=(out, out),
        compiler_params=params(),
        cost_estimate=cost(0, 12 * count * width),
        name="turn_strip",
    )(flag, held, come)


def diag_kernel(start, member_ref, base_ref, *refs):
    count = (len(refs) - 3) // 3
    highs, lows, blocks = refs[:count], refs[count : 2 * count], refs[2 * count : -3]
    own_ref, other_ref, total = refs[-3:]
    half, width = own_ref.shape
    for step in range(count):
        term = dot3((highs[step][...], lows[step][...]), split(blocks[step][...]))
        total[...] = term if step == 0 else total[...] + term
    mine = pl.multiple_of(member_ref[0] * half, 8)
    own_ref[...] = base_ref[:, start : start + width] - total[pl.ds(mine, half), :]
    other_ref[...] = total[pl.ds(pl.multiple_of(half - mine, 8), half), :]


def diag_parts(member, base, start, strips, blocks):
    (strip_width, count), width = strips[0][0].shape, blocks[0].shape[1]
    half = strip_width // MEMBERS
    flat = [base, *(high for high, _ in strips), *(low for _, low in strips), *blocks]
    out = jax.ShapeDtypeStruct((half, width), F32)
    return pl.pallas_call(
        functools.partial(diag_kernel, start),
        grid_spec=pltpu.PrefetchScalarGridSpec(
            num_scalar_prefetch=1,
            grid=(1,),
            in_specs=[whole(*x.shape) for x in flat],
            out_specs=[whole(half, width)] * 2,
            scratch_shapes=[pltpu.VMEM((strip_width, width), F32)],
        ),
        out_shape=(out, out),
        compiler_params=params(),
        cost_estimate=cost(6 * count * strip_width * width * len(blocks), 4 * count * strip_width * len(blocks)),
        name="diag_parts",
    )(member, *flat)


def shards(planes, cols, anc_inverse, panel, local_rows, inv_diag):
    axes = ("row", "col")
    row, col = lax.axis_index("row"), lax.axis_index("col")
    plane, member = row // MEMBERS, row % MEMBERS
    grid = [(z, y, c) for z in range(planes) for y in range(MEMBERS) for c in range(cols)]

    def place(z, y, c):
        return (z * MEMBERS + y) * cols + c

    def move(x, target, some=lambda z, y, c: True):
        return lax.ppermute(x, axes, [(place(*d), place(*target(*d))) for d in grid if some(*d)])

    def to_partner(x):
        return move(x, lambda z, y, c: (z, 1 - y, c))

    def onward(x):
        return move(x, lambda z, y, c: ((z + 1) % planes, y, c))

    def sync(*values):
        return list(lax.optimization_barrier(values))

    class Strip:
        def __init__(self, block):
            self.block, self.holders, self.apart = block, [0], cols // 2

        def hop(self):
            apart, holders = self.apart, self.holders
            self.come = move(self.block, lambda z, y, c: (z, y, c ^ apart), lambda z, y, c: (c ^ z) in holders)

        def keep(self):
            has = functools.reduce(jnp.logical_or, [(col ^ plane) == h for h in self.holders])
            if self.apart == 1:
                return turn(has.astype(jnp.int32)[None], self.block, self.come)
            self.block = jnp.where(has, self.block, self.come)
            self.holders = self.holders + [h ^ self.apart for h in self.holders]
            self.apart //= 2

        def rest(self):
            while True:
                self.hop()
                if done := self.keep():
                    return done

    width = panel.shape[1]
    cut = max(1, round(CUT * width / 128)) * 128
    cuts = [(0, cut), (cut, width)] if cut < width else [(0, width)]
    panels = [[panel[:, a:b]] for a, b in cuts]
    panels[0].append(onward(panels[0][0]))
    lists = jnp.stack([move(local_rows, lambda z, y, c: (c, y, z)), move(local_rows, lambda z, y, c: (c, 1 - y, z))])
    keep, send = pick(anc_inverse, local_rows, member[None], lists)
    send, panels[0][1] = sync(send, panels[0][1])
    apart, order = cols // 2, [0, cols // 2]
    own = [keep, move(keep, lambda z, y, c: (z, y, c ^ apart))]
    other = [to_partner(send), move(send, lambda z, y, c: (z, 1 - y, c ^ apart))]
    while apart > 1:
        apart //= 2
        for held in (own, other):
            held += [move(piece, lambda z, y, c: (z, y, c ^ apart)) for piece in held]
        order = order + [k ^ apart for k in order]
    wanted = col ^ ((plane - jnp.arange(planes, dtype=jnp.int32)) % planes)
    wanted = sum(jnp.where(wanted == k, i, 0) for i, k in enumerate(order))
    for part in panels:
        while len(part) < planes:
            part.append(onward(part[-1]))

    kept, sent = off_parts(wanted, own, other, panels[0])
    blocks = [panel] + [jnp.concatenate([part[k] for part in panels], axis=1) for k in range(1, planes)]
    strips = [Strip(block) for block in sync(*blocks, sent)[:-1]]
    early, late = strips[:GATED], strips[GATED:]
    for strip in early:
        strip.hop()
    offs = [[kept + to_partner(sent)]]
    offs[0].append(onward(offs[0][0]))
    offs[0][1], *values = sync(offs[0][1], *(strip.come for strip in early))
    for strip, value in zip(early, values):
        strip.come = value
        strip.keep()
    for part in panels[1:]:
        kept, sent = off_parts(wanted, own, other, part)
        offs.append([kept + to_partner(sent)])
    for part in offs:
        while len(part) < planes:
            part.append(onward(part[-1]))
    turned = [strip.rest() for strip in strips]
    diag, gate = [], None
    for (start, _), part in zip(cuts, offs):
        if gate is not None:
            part[-1], _ = sync(part[-1], gate)
        kept, sent = diag_parts(member[None], inv_diag, start, turned, part)
        gate = sent
        diag.append(kept - to_partner(sent))
    return jnp.concatenate([part[0] for part in offs], axis=1), jnp.concatenate(diag, axis=1)


def solution(mesh):
    rows, cols = mesh.shape["row"], mesh.shape["col"]
    placed = (P("row", "col"), P("row", "col"), P("row"), P("row", "col"))
    return jax.shard_map(
        functools.partial(shards, rows // MEMBERS, cols),
        mesh=mesh,
        in_specs=placed,
        out_specs=(P("row", "col"), P("row", "col")),
        check_vma=False,
    )
```

time: 155 us -> 142 us (0.916); the launches traced: 156 us -> 141 us
  waiting for transfers between devices: 92.4 us -> 60.4 us
  Pallas kernels: 12.1 us -> 18.9 us
  local copies, waits for them, and re-layouts: 2.31 us -> 6.49 us
  other arithmetic: 5.67 us -> 9.41 us
  starting transfers between devices: 42.8 us -> 44.6 us
    ppermute x29 -> x33, waiting for transfers between devices: 92.4 us -> 60.4 us  [move(): lax.ppermute(x, axes, [(place(*d), place(*target(*d))) for d in grid if s...]
    pallas_call x4 -> x8, Pallas kernels: 7.59 us -> 14 us  [the longest x2 5.77 us: diag_parts(): pl.pallas_call(functools.partial(diag_kernel, start), grid_spec=pltpu.Pre...]
    select_n x9 -> x4, other arithmetic: 0.57 us -> 4.78 us  [keep(): self.block = jnp.where(has, self.block, self.come)]
    unnamed x11 -> x10, local copies, waits for them, and re-layouts: 0.76 us -> 3.72 us
    slice x2, local copies, waits for them, and re-layouts: 0.04 us -> 1.97 us  [shards(): panels = [[panel[:, a:b]] for a, b in cuts]]
    ppermute x29 -> x33, starting transfers between devices: 42.8 us -> 44.6 us  [move(): lax.ppermute(x, axes, [(place(*d), place(*target(*d))) for d in grid if s...]
    concatenate x3 -> x5, other arithmetic: 3.21 us -> 4.43 us  [the longest x3 2.62 us: shards(): jnp.concatenate([part[k] for part in panels], axis=1)]
  transfers between devices with their start and end apart: 29 -> 33, of which waited for: 12 -> 14; matrix products, arithmetic and copies ran while one was open for 4% -> 7% of each run, Pallas kernels for 5% -> 13%
where the time goes in v2:
time: 142 us; the launch traced here: 141 us
  waiting for transfers between devices  60.4 us (43%)
  starting transfers between devices  44.6 us (31%)
  Pallas kernels  18.9 us (13%)
  other arithmetic  9.41 us (7%)
  local copies, waits for them, and re-layouts  6.49 us (5%)
    ppermute x33, waiting for transfers between devices, move(): lax.ppermute(x, axes, [(place(*d), place(*target(*d))) for d in grid if s...  60.4 us
    ppermute x33, starting transfers between devices, move(): lax.ppermute(x, axes, [(place(*d), place(*target(*d))) for d in grid if s...  44.6 us
    pallas_call x2, Pallas kernels, diag_parts(): pl.pallas_call(functools.partial(diag_kernel, start), grid_spec=pltpu.Pre...  5.77 us
    pallas_call x1, Pallas kernels, pick(): pl.pallas_call(pick_kernel, grid_spec=pltpu.PrefetchScalarGridSpec(num_sc...  4.92 us
    select_n x4, other arithmetic, keep(): self.block = jnp.where(has, self.block, self.come)  4.78 us
    pallas_call x4, Pallas kernels, turn(): pl.pallas_call(turn_kernel, grid_spec=pltpu.PrefetchScalarGridSpec(num_sc...  4.21 us
    pallas_call x2, Pallas kernels, off_parts(): pl.pallas_call(functools.partial(off_kernel, len(own)), grid_spec=pltpu.P...  4 us
    unnamed x10, local copies, waits for them, and re-layouts  3.72 us
  transfers between devices with their start and end apart: 33, of which 14 were waited for; matrix products, arithmetic and copies ran while one was open for 7% of the time, Pallas kernels for 13%

profile of v2, /device:TPU:0, one launch (start us, length us, event | category | flops | bytes accessed | tf_op | source)
XLA Modules:
  0.0 140.8 jit_solution(11472141977819252776)
XLA Ops:
  0.6 1.0 slice.6.refs_8_
  1.6 3.1 %collective-permute-start.5 = (f32[240,384]{1,0:T(8,128)S(1)}, f32[240,384]{1,0:T(8,128)S(1)}, u32[]{:S(2)}, u32[]{:S(2)}) collective-permute-start(f32[240,384]{1,0:T(8,128)S(1)} %slice.6.refs_8_), channel_id=1, source_target_pairs={{0,8},{1,9},{2,10},{3,11},{4,12},{5,13},{6,14},{7,15},{8,16},{9,17... | collective-permute-start | bytes 1105928 | tf_op jit(solution)/shard_map/ppermute | solution.py:179
  4.7 1.5 %collective-permute-start.1 = (s32[240]{0:T(256)}, s32[240]{0:T(256)S(1)}, u32[]{:S(2)}, u32[]{:S(2)}) collective-permute-start(s32[240]{0:T(256)} %rows_ref.1), channel_id=1, source_target_pairs={{0,4},{1,12},{2,20},{3,28},{4,0},{5,8},{6,16},{7,24},{8,5},{9,13},... | collective-permute-start | bytes 2888 | tf_op jit(solution)/shard_map/ppermute | solution.py:179
  6.2 1.3 collective-permute-start
  7.6 1.0 slice.7.refs_8_
  8.5 3.4 %collective-permute-start.13 = (f32[240,256]{1,0:T(8,128)S(1)}, f32[240,256]{1,0:T(8,128)S(1)}, u32[]{:S(2)}, u32[]{:S(2)}) collective-permute-start(f32[240,256]{1,0:T(8,128)S(1)} %slice.7.refs_8_), channel_id=1, source_target_pairs={{0,8},{1,9},{2,10},{3,11},{4,12},{5,13},{6,14},{7,15},{8,16},{9,17... | collective-permute-start | bytes 737288 | tf_op jit(solution)/shard_map/ppermute | solution.py:179
  11.9 0.8 copy.6.own_ref
  12.8 0.7 copy-done.3
  13.5 4.9 %pick_compact.1 = (f32[240,240]{1,0:T(8,128)S(1)}, f32[240,240]{1,0:T(8,128)}) custom-call(s32[240]{0:T(256)S(1)} %copy-done.3, s32[1]{0:T(128)} %bitcast.member_ref, f32[2048,4096]{1,0:T(8,128)} %anc.1, s32[240,1]{1,0:T(8,128)S(1)} %copy.6.own_ref, s32[2,240]{1,0:T(2,128)S(1)} %pad_add_fusion.lists_ref), custom_call_target="tpu_custom_call" | custom-call | flops 943718400 | bytes 15728640 | tf_op jit(solution)/shard_map/pick_compact/pallas_call | solution.py:64
  18.4 3.7 %collective-permute-start.10 = (f32[240,384]{1,0:T(8,128)S(1)}, f32[240,384]{1,0:T(8,128)S(1)}, u32[]{:S(2)}, u32[]{:S(2)}) collective-permute-start(f32[240,384]{1,0:T(8,128)S(1)} %collective-permute-done.5.refs_9_), channel_id=1, source_target_pairs={{0,8},{1,9},{2,10},{3,11},{4,12},{5,13},{6,14},{7,15},{8,16},{9,17... | collective-permute-start | bytes 1105928 | tf_op jit(solution)/shard_map/ppermute | solution.py:179
  22.1 0.9 collective-permute-start.2
  23.0 1.6 %collective-permute-start.14 = (f32[240,256]{1,0:T(8,128)S(1)}, f32[240,256]{1,0:T(8,128)S(1)}, u32[]{:S(2)}, u32[]{:S(2)}) collective-permute-start(f32[240,256]{1,0:T(8,128)S(1)} %collective-permute-done.13.refs_9_), channel_id=1, source_target_pairs={{0,8},{1,9},{2,10},{3,11},{4,12},{5,13},{6,14},{7,15},{8,16},{9,17... | collective-permute-start | bytes 737288 | tf_op jit(solution)/shard_map/ppermute | solution.py:179
  24.6 0.1 collective-permute-start.3
  24.7 0.6 collective-permute-start.6
  25.3 5.3 %collective-permute-done.2.refs_1_ = f32[240,240]{1,0:T(8,128)S(1)} collective-permute-done((f32[240,240]{1,0:T(8,128)S(1)}, f32[240,240]{1,0:T(8,128)S(1)}, u32[]{:S(2)}, u32[]{:S(2)}) %collective-permute-start.2) | collective-permute-done | bytes 230432 | tf_op jit(solution)/shard_map/ppermute | solution.py:179
  30.6 1.7 %collective-permute-start.7 = (f32[240,240]{1,0:T(8,128)}, f32[240,240]{1,0:T(8,128)S(1)}, u32[]{:S(2)}, u32[]{:S(2)}) collective-permute-start(f32[240,240]{1,0:T(8,128)} %get-tuple-element.33), channel_id=1, source_target_pairs={{0,6},{1,7},{2,4},{3,5},{4,2},{5,3},{6,0},{7,1},{8,14},{9,15},{10,... | collective-permute-start | bytes 691208 | tf_op jit(solution)/shard_map/ppermute | solution.py:179
  32.3 0.4 collective-permute-done.10.refs_10_
  32.7 0.8 collective-permute-start.11
  33.6 0.1 collective-permute-start.4
  33.6 4.3 %collective-permute-done.14.refs_10_ = f32[240,256]{1,0:T(8,128)S(1)} collective-permute-done((f32[240,256]{1,0:T(8,128)S(1)}, f32[240,256]{1,0:T(8,128)S(1)}, u32[]{:S(2)}, u32[]{:S(2)}) %collective-permute-start.14) | collective-permute-done | bytes 245792 | tf_op jit(solution)/shard_map/ppermute | solution.py:179
  38.0 0.8 collective-permute-start.15
  38.8 0.5 collective-permute-done.7.refs_5_
  39.3 0.9 pad_maximum_fusion.2
  40.2 0.9 pad_maximum_fusion.3
  41.1 4.9 %collective-permute-done.11.refs_11_ = f32[240,384]{1,0:T(8,128)S(1)} collective-permute-done((f32[240,384]{1,0:T(8,128)S(1)}, f32[240,384]{1,0:T(8,128)S(1)}, u32[]{:S(2)}, u32[]{:S(2)}) %collective-permute-start.11) | collective-permute-done | bytes 368672 | tf_op jit(solution)/shard_map/ppermute | solution.py:179
  46.0 2.3 %off_parts.2 = (f32[240,384]{1,0:T(8,128)S(1)}, f32[240,384]{1,0:T(8,128)S(1)}) custom-call(s32[4]{0:T(128)S(1)} %fusion.2.order_ref, f32[240,240]{1,0:T(8,128)S(1)} %get-tuple-element.31.refs_0_, f32[240,240]{1,0:T(8,128)S(1)} %collective-permute-done.2.refs_1_, f32[240,240]{1,0:T(8,128)S(1)} %collective-permute-done.3.refs_2_, ...), custom_call_target="tpu_custom_call" | custom-call | flops 1061683200 | bytes 1843200 | tf_op jit(solution)/shard_map/off_parts/pallas_call | solution.py:97
  48.4 0.6 collective-permute-start.12
  48.9 1.7 %collective-permute-done.15.refs_11_ = f32[240,256]{1,0:T(8,128)S(1)} collective-permute-done((f32[240,256]{1,0:T(8,128)S(1)}, f32[240,256]{1,0:T(8,128)S(1)}, u32[]{:S(2)}, u32[]{:S(2)}) %collective-permute-start.15) | collective-permute-done | bytes 245792 | tf_op jit(solution)/shard_map/ppermute | solution.py:179
  50.6 0.9 pad_maximum_fusion.4
  51.5 6.5 %collective-permute-start.24 = (f32[240,640]{1,0:T(8,128)}, f32[240,640]{1,0:T(8,128)}, u32[]{:S(2)}, u32[]{:S(2)}) collective-permute-start(f32[240,640]{1,0:T(8,128)} %pad_maximum_fusion.4), channel_id=1, source_target_pairs={{0,2},{4,6},{9,11},{13,15},{18,16},{22,20},{27,25},{31,29}} | collective-permute-start | bytes 1843208 | tf_op jit(solution)/shard_map/ppermute | solution.py:179
  58.0 1.7 %off_parts.3 = (f32[240,256]{1,0:T(8,128)S(1)}, f32[240,256]{1,0:T(8,128)S(1)}) custom-call(s32[4]{0:T(128)S(1)} %fusion.2.order_ref, f32[240,240]{1,0:T(8,128)S(1)} %get-tuple-element.31.refs_0_, f32[240,240]{1,0:T(8,128)S(1)} %collective-permute-done.2.refs_1_, f32[240,240]{1,0:T(8,128)S(1)} %collective-permute-done.3.refs_2_, ...), custom_call_target="tpu_custom_call" | custom-call | flops 707788800 | bytes 1843200 | tf_op jit(solution)/shard_map/off_parts/pallas_call | solution.py:97
  59.6 0.5 collective-permute-start.16
  60.1 5.8 %collective-permute-done.16 = f32[240,256]{1,0:T(8,128)S(1)} collective-permute-done((f32[240,256]{1,0:T(8,128)S(1)}, f32[240,256]{1,0:T(8,128)S(1)}, u32[]{:S(2)}, u32[]{:S(2)}) %collective-permute-start.16) | collective-permute-done | bytes 245792 | tf_op jit(solution)/shard_map/ppermute | solution.py:179
  66.0 4.7 %collective-permute-start.18 = (f32[240,640]{1,0:T(8,128)}, f32[240,640]{1,0:T(8,128)}, u32[]{:S(2)}, u32[]{:S(2)}) collective-permute-start(f32[240,640]{1,0:T(8,128)} %param.5), channel_id=1, source_target_pairs={{0,2},{4,6},{9,11},{13,15},{18,16},{22,20},{27,25},{31,29}} | collective-permute-start | bytes 1843208 | tf_op jit(solution)/shard_map/ppermute | solution.py:179
  70.8 1.3 collective-permute-start.19
  72.1 1.3 collective-permute-start.20
  73.5 1.1 collective-permute-done.29.refs_9_
  74.6 1.1 broadcast_select_fusion.held
  75.7 2.2 %collective-permute-done.18 = f32[240,640]{1,0:T(8,128)} collective-permute-done((f32[240,640]{1,0:T(8,128)}, f32[240,640]{1,0:T(8,128)}, u32[]{:S(2)}, u32[]{:S(2)}) %collective-permute-start.18) | collective-permute-done | bytes 614432 | tf_op jit(solution)/shard_map/ppermute | solution.py:179
  77.9 1.3 collective-permute-start.25
  79.2 5.3 %collective-permute-done.19 = f32[240,640]{1,0:T(8,128)S(1)} collective-permute-done((f32[240,640]{1,0:T(8,128)}, f32[240,640]{1,0:T(8,128)S(1)}, u32[]{:S(2)}, u32[]{:S(2)}) %collective-permute-start.19) | collective-permute-done | bytes 614432 | tf_op jit(solution)/shard_map/ppermute | solution.py:179
  84.5 6.6 %collective-permute-done.20 = f32[240,640]{1,0:T(8,128)S(1)} collective-permute-done((f32[240,640]{1,0:T(8,128)}, f32[240,640]{1,0:T(8,128)S(1)}, u32[]{:S(2)}, u32[]{:S(2)}) %collective-permute-start.20) | collective-permute-done | bytes 614432 | tf_op jit(solution)/shard_map/ppermute | solution.py:179
  91.1 1.4 broadcast_select_fusion.3.held
  92.4 2.1 %collective-permute-start.21 = (f32[240,640]{1,0:T(8,128)S(1)}, f32[240,640]{1,0:T(8,128)}, u32[]{:S(2)}, u32[]{:S(2)}) collective-permute-start(f32[240,640]{1,0:T(8,128)S(1)} %broadcast_select_fusion.3.held), channel_id=1, source_target_pairs={{0,1},{2,3},{4,5},{6,7},{9,8},{11,10},{13,12},{15,14},{16,17},{18,... | collective-permute-start | bytes 1843208 | tf_op jit(solution)/shard_map/ppermute | solution.py:179
  94.6 1.1 broadcast_select_fusion.2.held
  95.7 2.2 %collective-permute-start.22 = (f32[240,640]{1,0:T(8,128)S(1)}, f32[240,640]{1,0:T(8,128)}, u32[]{:S(2)}, u32[]{:S(2)}) collective-permute-start(f32[240,640]{1,0:T(8,128)S(1)} %broadcast_select_fusion.2.held), channel_id=1, source_target_pairs={{0,1},{2,3},{4,5},{6,7},{9,8},{11,10},{13,12},{15,14},{16,17},{18,... | collective-permute-start | bytes 1843208 | tf_op jit(solution)/shard_map/ppermute | solution.py:179
  97.9 1.1 broadcast_select_fusion.1.held
  99.0 2.1 %collective-permute-start.23 = (f32[240,640]{1,0:T(8,128)S(1)}, f32[240,640]{1,0:T(8,128)}, u32[]{:S(2)}, u32[]{:S(2)}) collective-permute-start(f32[240,640]{1,0:T(8,128)S(1)} %broadcast_select_fusion.1.held), channel_id=1, source_target_pairs={{0,1},{2,3},{4,5},{6,7},{9,8},{11,10},{13,12},{15,14},{16,17},{18,... | collective-permute-start | bytes 1843208 | tf_op jit(solution)/shard_map/ppermute | solution.py:179
  101.2 6.9 %collective-permute-done.26.refs_10_ = f32[240,384]{1,0:T(8,128)} collective-permute-done((f32[240,384]{1,0:T(8,128)}, f32[240,384]{1,0:T(8,128)}, u32[]{:S(2)}, u32[]{:S(2)}) %collective-permute-start.26) | collective-permute-done | bytes 368672 | tf_op jit(solution)/shard_map/ppermute | solution.py:179
  108.1 0.8 copy-done.1
  108.9 1.1 copy-done.2
  110.0 0.2 turn_strip.7
  110.2 1.3 turn_strip.4
  111.6 1.3 turn_strip.5
  112.9 1.3 turn_strip.6
  114.2 6.6 %collective-permute-done.27.refs_11_ = f32[240,384]{1,0:T(8,128)} collective-permute-done((f32[240,384]{1,0:T(8,128)}, f32[240,384]{1,0:T(8,128)}, u32[]{:S(2)}, u32[]{:S(2)}) %collective-permute-start.27) | collective-permute-done | bytes 368672 | tf_op jit(solution)/shard_map/ppermute | solution.py:179
  120.9 1.1 copy-done
  122.0 3.5 %diag_parts.2 = (f32[320,384]{1,0:T(8,128)S(1)}, f32[320,384]{1,0:T(8,128)S(1)}) custom-call(s32[1]{0:T(128)} %bitcast.member_ref, f32[320,640]{1,0:T(8,128)S(1)} %copy-done, bf16[640,240]{1,0:T(8,128)(2,1)S(1)} %get-tuple-element.43.refs_0_, bf16[640,240]{1,0:T(8,128)(2,1)S(1)} %get-tuple-element.45.refs_1_, ...), custom_call_target="tpu_custom_call" | custom-call | flops 1415577600 | bytes 2457600 | tf_op jit(solution)/shard_map/diag_parts/pallas_call | solution.py:153
  125.5 0.7 collective-permute-start.28
  126.1 2.3 %diag_parts.3 = (f32[320,256]{1,0:T(8,128)S(1)}, f32[320,256]{1,0:T(8,128)S(1)}) custom-call(s32[1]{0:T(128)} %bitcast.member_ref, f32[320,640]{1,0:T(8,128)S(1)} %copy-done, bf16[640,240]{1,0:T(8,128)(2,1)S(1)} %get-tuple-element.43.refs_0_, bf16[640,240]{1,0:T(8,128)(2,1)S(1)} %get-tuple-element.45.refs_1_, ...), custom_call_target="tpu_custom_call" | custom-call | flops 943718400 | bytes 2457600 | tf_op jit(solution)/shard_map/diag_parts/pallas_call | solution.py:153
  128.4 1.5 %collective-permute-start.32 = (f32[320,256]{1,0:T(8,128)S(1)}, f32[320,256]{1,0:T(8,128)S(1)}, u32[]{:S(2)}, u32[]{:S(2)}) collective-permute-start(f32[320,256]{1,0:T(8,128)S(1)} %get-tuple-element.59), channel_id=1, source_target_pairs={{0,4},{1,5},{2,6},{3,7},{4,0},{5,1},{6,2},{7,3},{8,12},{9,13},{10,... | collective-permute-start | bytes 983048 | tf_op jit(solution)/shard_map/ppermute | solution.py:179
  130.0 0.9 pad_maximum_fusion.1
  130.8 8.9 %collective-permute-done.32 = f32[320,256]{1,0:T(8,128)S(1)} collective-permute-done((f32[320,256]{1,0:T(8,128)S(1)}, f32[320,256]{1,0:T(8,128)S(1)}, u32[]{:S(2)}, u32[]{:S(2)}) %collective-permute-start.32) | collective-permute-done | bytes 327712 | tf_op jit(solution)/shard_map/ppermute | solution.py:179
  139.8 0.9 pad_maximum_fusion
  (39 shorter events, 0.3 us)
Async XLA Ops:
  1.6 16.8 %collective-permute-start.5 = (f32[240,384]{1,0:T(8,128)S(1)}, f32[240,384]{1,0:T(8,128)S(1)}, u32[]{:S(2)}, u32[]{:S(2)}) collective-permute-start(f32[240,384]{1,0:T(8,128)S(1)} %slice.6.refs_8_), channel_id=1, source_target_pairs={{0,8},{1,9},{2,10},{3,11},{4,12},{5,13},{6,14},{7,15},{8,16},{9,17... | collective-permute-start | bytes 1105928 | tf_op jit(solution)/shard_map/ppermute | solution.py:179
  4.7 8.0 %collective-permute-start.1 = (s32[240]{0:T(256)}, s32[240]{0:T(256)S(1)}, u32[]{:S(2)}, u32[]{:S(2)}) collective-permute-start(s32[240]{0:T(256)} %rows_ref.1), channel_id=1, source_target_pairs={{0,4},{1,12},{2,20},{3,28},{4,0},{5,8},{6,16},{7,24},{8,5},{9,13},... | collective-permute-start | bytes 2888 | tf_op jit(solution)/shard_map/ppermute | solution.py:179
  6.2 6.5 %collective-permute-start = (s32[240]{0:T(256)}, s32[240]{0:T(256)S(1)}, u32[]{:S(2)}, u32[]{:S(2)}) collective-permute-start(s32[240]{0:T(256)} %rows_ref.1), channel_id=1, source_target_pairs={{0,0},{1,8},{2,16},{3,24},{4,4},{5,12},{6,20},{7,28},{8,1},{9,9},{... | collective-permute-start | bytes 2888 | tf_op jit(solution)/shard_map/ppermute | solution.py:179
  8.5 14.5 %collective-permute-start.13 = (f32[240,256]{1,0:T(8,128)S(1)}, f32[240,256]{1,0:T(8,128)S(1)}, u32[]{:S(2)}, u32[]{:S(2)}) collective-permute-start(f32[240,256]{1,0:T(8,128)S(1)} %slice.7.refs_8_), channel_id=1, source_target_pairs={{0,8},{1,9},{2,10},{3,11},{4,12},{5,13},{6,14},{7,15},{8,16},{9,17... | collective-permute-start | bytes 737288 | tf_op jit(solution)/shard_map/ppermute | solution.py:179
  12.8 0.7 copy-start.3
  18.4 14.3 %collective-permute-start.10 = (f32[240,384]{1,0:T(8,128)S(1)}, f32[240,384]{1,0:T(8,128)S(1)}, u32[]{:S(2)}, u32[]{:S(2)}) collective-permute-start(f32[240,384]{1,0:T(8,128)S(1)} %collective-permute-done.5.refs_9_), channel_id=1, source_target_pairs={{0,8},{1,9},{2,10},{3,11},{4,12},{5,13},{6,14},{7,15},{8,16},{9,17... | collective-permute-start | bytes 1105928 | tf_op jit(solution)/shard_map/ppermute | solution.py:179
  22.1 8.5 %collective-permute-start.2 = (f32[240,240]{1,0:T(8,128)S(1)}, f32[240,240]{1,0:T(8,128)S(1)}, u32[]{:S(2)}, u32[]{:S(2)}) collective-permute-start(f32[240,240]{1,0:T(8,128)S(1)} %get-tuple-element.31.refs_0_), channel_id=1, source_target_pairs={{0,2},{1,3},{2,0},{3,1},{4,6},{5,7},{6,4},{7,5},{8,10},{9,11},{10,... | collective-permute-start | bytes 691208 | tf_op jit(solution)/shard_map/ppermute | solution.py:179
  23.0 14.9 %collective-permute-start.14 = (f32[240,256]{1,0:T(8,128)S(1)}, f32[240,256]{1,0:T(8,128)S(1)}, u32[]{:S(2)}, u32[]{:S(2)}) collective-permute-start(f32[240,256]{1,0:T(8,128)S(1)} %collective-permute-done.13.refs_9_), channel_id=1, source_target_pairs={{0,8},{1,9},{2,10},{3,11},{4,12},{5,13},{6,14},{7,15},{8,16},{9,17... | collective-permute-start | bytes 737288 | tf_op jit(solution)/shard_map/ppermute | solution.py:179
  24.6 9.0 %collective-permute-start.3 = (f32[240,240]{1,0:T(8,128)S(1)}, f32[240,240]{1,0:T(8,128)S(1)}, u32[]{:S(2)}, u32[]{:S(2)}) collective-permute-start(f32[240,240]{1,0:T(8,128)S(1)} %get-tuple-element.31.refs_0_), channel_id=1, source_target_pairs={{0,1},{1,0},{2,3},{3,2},{4,5},{5,4},{6,7},{7,6},{8,9},{9,8},{10,11... | collective-permute-start | bytes 691208 | tf_op jit(solution)/shard_map/ppermute | solution.py:179
  24.7 14.1 %collective-permute-start.6 = (f32[240,240]{1,0:T(8,128)}, f32[240,240]{1,0:T(8,128)S(1)}, u32[]{:S(2)}, u32[]{:S(2)}) collective-permute-start(f32[240,240]{1,0:T(8,128)} %get-tuple-element.33), channel_id=1, source_target_pairs={{0,4},{1,5},{2,6},{3,7},{4,0},{5,1},{6,2},{7,3},{8,12},{9,13},{10,... | collective-permute-start | bytes 691208 | tf_op jit(solution)/shard_map/ppermute | solution.py:179
  30.6 8.7 %collective-permute-start.7 = (f32[240,240]{1,0:T(8,128)}, f32[240,240]{1,0:T(8,128)S(1)}, u32[]{:S(2)}, u32[]{:S(2)}) collective-permute-start(f32[240,240]{1,0:T(8,128)} %get-tuple-element.33), channel_id=1, source_target_pairs={{0,6},{1,7},{2,4},{3,5},{4,2},{5,3},{6,0},{7,1},{8,14},{9,15},{10,... | collective-permute-start | bytes 691208 | tf_op jit(solution)/shard_map/ppermute | solution.py:179
  32.7 13.3 %collective-permute-start.11 = (f32[240,384]{1,0:T(8,128)S(1)}, f32[240,384]{1,0:T(8,128)S(1)}, u32[]{:S(2)}, u32[]{:S(2)}) collective-permute-start(f32[240,384]{1,0:T(8,128)S(1)} %collective-permute-done.10.refs_10_), channel_id=1, source_target_pairs={{0,8},{1,9},{2,10},{3,11},{4,12},{5,13},{6,14},{7,15},{8,16},{9,17... | collective-permute-start | bytes 1105928 | tf_op jit(solution)/shard_map/ppermute | solution.py:179
  33.6 7.5 %collective-permute-start.4 = (f32[240,240]{1,0:T(8,128)S(1)}, f32[240,240]{1,0:T(8,128)S(1)}, u32[]{:S(2)}, u32[]{:S(2)}) collective-permute-start(f32[240,240]{1,0:T(8,128)S(1)} %collective-permute-done.2.refs_1_), channel_id=1, source_target_pairs={{0,1},{1,0},{2,3},{3,2},{4,5},{5,4},{6,7},{7,6},{8,9},{9,8},{10,11... | collective-permute-start | bytes 691208 | tf_op jit(solution)/shard_map/ppermute | solution.py:179
  38.0 12.6 %collective-permute-start.15 = (f32[240,256]{1,0:T(8,128)S(1)}, f32[240,256]{1,0:T(8,128)S(1)}, u32[]{:S(2)}, u32[]{:S(2)}) collective-permute-start(f32[240,256]{1,0:T(8,128)S(1)} %collective-permute-done.14.refs_10_), channel_id=1, source_target_pairs={{0,8},{1,9},{2,10},{3,11},{4,12},{5,13},{6,14},{7,15},{8,16},{9,17... | collective-permute-start | bytes 737288 | tf_op jit(solution)/shard_map/ppermute | solution.py:179
  38.8 2.3 %collective-permute-start.8 = (f32[240,240]{1,0:T(8,128)S(1)}, f32[240,240]{1,0:T(8,128)S(1)}, u32[]{:S(2)}, u32[]{:S(2)}) collective-permute-start(f32[240,240]{1,0:T(8,128)S(1)} %collective-permute-done.6.refs_4_), channel_id=1, source_target_pairs={{0,1},{1,0},{2,3},{3,2},{4,5},{5,4},{6,7},{7,6},{8,9},{9,8},{10,11... | collective-permute-start | bytes 691208 | tf_op jit(solution)/shard_map/ppermute | solution.py:179
  39.3 1.7 %collective-permute-start.9 = (f32[240,240]{1,0:T(8,128)S(1)}, f32[240,240]{1,0:T(8,128)S(1)}, u32[]{:S(2)}, u32[]{:S(2)}) collective-permute-start(f32[240,240]{1,0:T(8,128)S(1)} %collective-permute-done.7.refs_5_), channel_id=1, source_target_pairs={{0,1},{1,0},{2,3},{3,2},{4,5},{5,4},{6,7},{7,6},{8,9},{9,8},{10,11... | collective-permute-start | bytes 691208 | tf_op jit(solution)/shard_map/ppermute | solution.py:179
  48.4 23.7 %collective-permute-start.12 = (f32[240,384]{1,0:T(8,128)S(1)}, f32[240,384]{1,0:T(8,128)S(1)}, u32[]{:S(2)}, u32[]{:S(2)}) collective-permute-start(f32[240,384]{1,0:T(8,128)S(1)} %get-tuple-element.36), channel_id=1, source_target_pairs={{0,4},{1,5},{2,6},{3,7},{4,0},{5,1},{6,2},{7,3},{8,12},{9,13},{10,... | collective-permute-start | bytes 1105928 | tf_op jit(solution)/shard_map/ppermute | solution.py:179
  51.5 23.1 %collective-permute-start.24 = (f32[240,640]{1,0:T(8,128)}, f32[240,640]{1,0:T(8,128)}, u32[]{:S(2)}, u32[]{:S(2)}) collective-permute-start(f32[240,640]{1,0:T(8,128)} %pad_maximum_fusion.4), channel_id=1, source_target_pairs={{0,2},{4,6},{9,11},{13,15},{18,16},{22,20},{27,25},{31,29}} | collective-permute-start | bytes 1843208 | tf_op jit(solution)/shard_map/ppermute | solution.py:179
  59.6 6.3 %collective-permute-start.16 = (f32[240,256]{1,0:T(8,128)S(1)}, f32[240,256]{1,0:T(8,128)S(1)}, u32[]{:S(2)}, u32[]{:S(2)}) collective-permute-start(f32[240,256]{1,0:T(8,128)S(1)} %get-tuple-element.38), channel_id=1, source_target_pairs={{0,4},{1,5},{2,6},{3,7},{4,0},{5,1},{6,2},{7,3},{8,12},{9,13},{10,... | collective-permute-start | bytes 737288 | tf_op jit(solution)/shard_map/ppermute | solution.py:179
  65.9 8.6 %collective-permute-start.29 = (f32[240,256]{1,0:T(8,128)S(1)}, f32[240,256]{1,0:T(8,128)S(1)}, u32[]{:S(2)}, u32[]{:S(2)}) collective-permute-start(f32[240,256]{1,0:T(8,128)S(1)} %add.29.refs_8_), channel_id=1, source_target_pairs={{0,8},{1,9},{2,10},{3,11},{4,12},{5,13},{6,14},{7,15},{8,16},{9,17... | collective-permute-start | bytes 737288 | tf_op jit(solution)/shard_map/ppermute | solution.py:179
  66.0 11.9 %collective-permute-start.18 = (f32[240,640]{1,0:T(8,128)}, f32[240,640]{1,0:T(8,128)}, u32[]{:S(2)}, u32[]{:S(2)}) collective-permute-start(f32[240,640]{1,0:T(8,128)} %param.5), channel_id=1, source_target_pairs={{0,2},{4,6},{9,11},{13,15},{18,16},{22,20},{27,25},{31,29}} | collective-permute-start | bytes 1843208 | tf_op jit(solution)/shard_map/ppermute | solution.py:179
  70.8 13.7 %collective-permute-start.19 = (f32[240,640]{1,0:T(8,128)}, f32[240,640]{1,0:T(8,128)S(1)}, u32[]{:S(2)}, u32[]{:S(2)}) collective-permute-start(f32[240,640]{1,0:T(8,128)} %pad_maximum_fusion.2), channel_id=1, source_target_pairs={{0,2},{4,6},{9,11},{13,15},{18,16},{22,20},{27,25},{31,29}} | collective-permute-start | bytes 1843208 | tf_op jit(solution)/shard_map/ppermute | solution.py:179
  72.1 19.0 %collective-permute-start.20 = (f32[240,640]{1,0:T(8,128)}, f32[240,640]{1,0:T(8,128)S(1)}, u32[]{:S(2)}, u32[]{:S(2)}) collective-permute-start(f32[240,640]{1,0:T(8,128)} %pad_maximum_fusion.3), channel_id=1, source_target_pairs={{0,2},{4,6},{9,11},{13,15},{18,16},{22,20},{27,25},{31,29}} | collective-permute-start | bytes 1843208 | tf_op jit(solution)/shard_map/ppermute | solution.py:179
  74.6 16.5 %collective-permute-start.17 = (f32[240,384]{1,0:T(8,128)S(1)}, f32[240,384]{1,0:T(8,128)}, u32[]{:S(2)}, u32[]{:S(2)}) collective-permute-start(f32[240,384]{1,0:T(8,128)S(1)} %add.28.refs_8_), channel_id=1, source_target_pairs={{0,8},{1,9},{2,10},{3,11},{4,12},{5,13},{6,14},{7,15},{8,16},{9,17... | collective-permute-start | bytes 1105928 | tf_op jit(solution)/shard_map/ppermute | solution.py:179
  74.6 24.4 %collective-permute-start.30 = (f32[240,256]{1,0:T(8,128)S(1)}, f32[240,256]{1,0:T(8,128)}, u32[]{:S(2)}, u32[]{:S(2)}) collective-permute-start(f32[240,256]{1,0:T(8,128)S(1)} %collective-permute-done.29.refs_9_), channel_id=1, source_target_pairs={{0,8},{1,9},{2,10},{3,11},{4,12},{5,13},{6,14},{7,15},{8,16},{9,17... | collective-permute-start | bytes 737288 | tf_op jit(solution)/shard_map/ppermute | solution.py:179
  77.9 30.2 %collective-permute-start.25 = (f32[240,640]{1,0:T(8,128)S(1)}, f32[240,640]{1,0:T(8,128)S(1)}, u32[]{:S(2)}, u32[]{:S(2)}) collective-permute-start(f32[240,640]{1,0:T(8,128)S(1)} %broadcast_select_fusion.held), channel_id=1, source_target_pairs={{0,1},{2,3},{4,5},{6,7},{9,8},{11,10},{13,12},{15,14},{16,17},{18,... | collective-permute-start | bytes 1843208 | tf_op jit(solution)/shard_map/ppermute | solution.py:179
  91.1 1.4 copy-start.4
  92.4 17.8 %collective-permute-start.21 = (f32[240,640]{1,0:T(8,128)S(1)}, f32[240,640]{1,0:T(8,128)}, u32[]{:S(2)}, u32[]{:S(2)}) collective-permute-start(f32[240,640]{1,0:T(8,128)S(1)} %broadcast_select_fusion.3.held), channel_id=1, source_target_pairs={{0,1},{2,3},{4,5},{6,7},{9,8},{11,10},{13,12},{15,14},{16,17},{18,... | collective-permute-start | bytes 1843208 | tf_op jit(solution)/shard_map/ppermute | solution.py:179
  95.7 15.9 %collective-permute-start.22 = (f32[240,640]{1,0:T(8,128)S(1)}, f32[240,640]{1,0:T(8,128)}, u32[]{:S(2)}, u32[]{:S(2)}) collective-permute-start(f32[240,640]{1,0:T(8,128)S(1)} %broadcast_select_fusion.2.held), channel_id=1, source_target_pairs={{0,1},{2,3},{4,5},{6,7},{9,8},{11,10},{13,12},{15,14},{16,17},{18,... | collective-permute-start | bytes 1843208 | tf_op jit(solution)/shard_map/ppermute | solution.py:179
  97.9 10.2 %collective-permute-start.26 = (f32[240,384]{1,0:T(8,128)}, f32[240,384]{1,0:T(8,128)}, u32[]{:S(2)}, u32[]{:S(2)}) collective-permute-start(f32[240,384]{1,0:T(8,128)} %collective-permute-done.17.refs_9_), channel_id=1, source_target_pairs={{0,8},{1,9},{2,10},{3,11},{4,12},{5,13},{6,14},{7,15},{8,16},{9,17... | collective-permute-start | bytes 1105928 | tf_op jit(solution)/shard_map/ppermute | solution.py:179
  99.0 13.9 %collective-permute-start.23 = (f32[240,640]{1,0:T(8,128)S(1)}, f32[240,640]{1,0:T(8,128)}, u32[]{:S(2)}, u32[]{:S(2)}) collective-permute-start(f32[240,640]{1,0:T(8,128)S(1)} %broadcast_select_fusion.1.held), channel_id=1, source_target_pairs={{0,1},{2,3},{4,5},{6,7},{9,8},{11,10},{13,12},{15,14},{16,17},{18,... | collective-permute-start | bytes 1843208 | tf_op jit(solution)/shard_map/ppermute | solution.py:179
  108.1 12.8 %collective-permute-start.27 = (f32[240,384]{1,0:T(8,128)}, f32[240,384]{1,0:T(8,128)}, u32[]{:S(2)}, u32[]{:S(2)}) collective-permute-start(f32[240,384]{1,0:T(8,128)} %collective-permute-done.26.refs_10_), channel_id=1, source_target_pairs={{0,8},{1,9},{2,10},{3,11},{4,12},{5,13},{6,14},{7,15},{8,16},{9,17... | collective-permute-start | bytes 1105928 | tf_op jit(solution)/shard_map/ppermute | solution.py:179
  108.1 0.8 copy-start.1
  108.9 17.2 %collective-permute-start.31 = (f32[240,256]{1,0:T(8,128)}, f32[240,256]{1,0:T(8,128)}, u32[]{:S(2)}, u32[]{:S(2)}) collective-permute-start(f32[240,256]{1,0:T(8,128)} %collective-permute-done.30.refs_10_), channel_id=1, source_target_pairs={{0,8},{1,9},{2,10},{3,11},{4,12},{5,13},{6,14},{7,15},{8,16},{9,17... | collective-permute-start | bytes 737288 | tf_op jit(solution)/shard_map/ppermute | solution.py:179
  108.9 1.1 copy-start.2
  120.9 1.1 copy-start
  125.5 14.3 %collective-permute-start.28 = (f32[320,384]{1,0:T(8,128)S(1)}, f32[320,384]{1,0:T(8,128)S(1)}, u32[]{:S(2)}, u32[]{:S(2)}) collective-permute-start(f32[320,384]{1,0:T(8,128)S(1)} %get-tuple-element.56), channel_id=1, source_target_pairs={{0,4},{1,5},{2,6},{3,7},{4,0},{5,1},{6,2},{7,3},{8,12},{9,13},{10,... | collective-permute-start | bytes 1474568 | tf_op jit(solution)/shard_map/ppermute | solution.py:179
  128.4 11.2 %collective-permute-start.32 = (f32[320,256]{1,0:T(8,128)S(1)}, f32[320,256]{1,0:T(8,128)S(1)}, u32[]{:S(2)}, u32[]{:S(2)}) collective-permute-start(f32[320,256]{1,0:T(8,128)S(1)} %get-tuple-element.59), channel_id=1, source_target_pairs={{0,4},{1,5},{2,6},{3,7},{4,0},{5,1},{6,2},{7,3},{8,12},{9,13},{10,... | collective-permute-start | bytes 983048 | tf_op jit(solution)/shard_map/ppermute | solution.py:179

commit v3 on v2

--- a/solution.py
+++ b/solution.py
@@ -9,7 +9,10 @@
 
 MEMBERS = 2
 CUT = 0.6
-GATED = 3
+FIRST, NEAR, LAST, SKEW, SPLIT, ORDER = 'a', '', False, False, True, False
+VMEM = 24
+PICK, OFF, DIAG, TURN = 1, 1, 1, 1
+PLAN = {(0, 1): ('k1a', 'y1a'), (1, 1): ('k1b', 'y2b'), (2, 1): ('k1a', 'y1a'), (3, 1): ('k1b', 'y2a'), (3, 2): ('y2b', 'y3a')}
 BF16 = jnp.bfloat16
 F32 = jnp.float32
 
@@ -32,11 +35,11 @@
 
 
 def params():
-    return pltpu.CompilerParams(vmem_limit_bytes=48 * 2**20)
-
-
-def cost(flops, moved):
-    return pl.CostEstimate(flops=flops, bytes_accessed=moved, transcendentals=0)
+    return pltpu.CompilerParams(vmem_limit_bytes=VMEM * 2**20)
+
+
+def cost(scale, flops, moved):
+    return pl.CostEstimate(flops=int(scale * flops), bytes_accessed=int(scale * moved), transcendentals=0)
 
 
 def pick_kernel(rows_ref, member_ref, anc, own_ref, lists_ref, keep_ref, send_ref, picked, sem):
@@ -72,7 +75,7 @@
         ),
         out_shape=(square, square),
         compiler_params=params(),
-        cost_estimate=cost(4 * count * count * width, 16 * count * width),
+        cost_estimate=cost(PICK, 4 * count * count * width, 16 * count * width),
         name="pick_compact",
     )(rows, member, anc, rows[:, None], lists)
 
@@ -104,7 +107,7 @@
         ),
         out_shape=(out, out),
         compiler_params=params(),
-        cost_estimate=cost(12 * count * count * width * len(blocks), 8 * count * count * len(blocks)),
+        cost_estimate=cost(OFF, 12 * count * count * width * len(blocks), 8 * count * count * len(blocks)),
         name="off_parts",
     )(order, *own, *other, *blocks)
 
@@ -127,7 +130,7 @@
         ),
         out_shape=(out, out),
         compiler_params=params(),
-        cost_estimate=cost(0, 12 * count * width),
+        cost_estimate=cost(TURN, 0, 12 * count * width),
         name="turn_strip",
     )(flag, held, come)
 
@@ -161,9 +164,60 @@
         ),
         out_shape=(out, out),
         compiler_params=params(),
-        cost_estimate=cost(6 * count * strip_width * width * len(blocks), 4 * count * strip_width * len(blocks)),
+        cost_estimate=cost(DIAG, 6 * count * strip_width * width * len(blocks), 4 * count * strip_width * len(blocks)),
         name="diag_parts",
     )(member, *flat)
+
+
+def diag_first_kernel(*refs):
+    count, total = len(refs) // 3, refs[-1]
+    for step in range(count):
+        high, low, block = refs[step::count][:3]
+        term = dot3((high[...], low[...]), split(block[...]))
+        total[...] = term if step == 0 else total[...] + term
+
+
+def diag_first(strips, blocks):
+    (strip_width, count), width = strips[0][0].shape, blocks[0].shape[1]
+    flat = [*(high for high, _ in strips), *(low for _, low in strips), *blocks]
+    return pl.pallas_call(
+        diag_first_kernel,
+        grid=(1,),
+        in_specs=[whole(*x.shape) for x in flat],
+        out_specs=whole(strip_width, width),
+        out_shape=jax.ShapeDtypeStruct((strip_width, width), F32),
+        compiler_params=params(),
+        cost_estimate=cost(DIAG, 6 * count * strip_width * width * len(blocks), 4 * count * strip_width * len(blocks)),
+        name="diag_first",
+    )(*flat)
+
+
+def diag_last_kernel(start, member_ref, first, base_ref, high, low, block, own_ref, other_ref, total):
+    half, width = own_ref.shape
+    total[...] = first[...] + dot3((high[...], low[...]), split(block[...]))
+    mine = pl.multiple_of(member_ref[0] * half, 8)
+    own_ref[...] = base_ref[:, start : start + width] - total[pl.ds(mine, half), :]
+    other_ref[...] = total[pl.ds(pl.multiple_of(half - mine, 8), half), :]
+
+
+def diag_last(member, first, base, start, strip, block):
+    (strip_width, count), width = strip[0].shape, block.shape[1]
+    half = strip_width // MEMBERS
+    out = jax.ShapeDtypeStruct((half, width), F32)
+    return pl.pallas_call(
+        functools.partial(diag_last_kernel, start),
+        grid_spec=pltpu.PrefetchScalarGridSpec(
+            num_scalar_prefetch=1,
+            grid=(1,),
+            in_specs=[whole(*x.shape) for x in (first, base, *strip, block)],
+            out_specs=[whole(half, width)] * 2,
+            scratch_shapes=[pltpu.VMEM((strip_width, width), F32)],
+        ),
+        out_shape=(out, out),
+        compiler_params=params(),
+        cost_estimate=cost(DIAG, 6 * count * strip_width * width, 8 * count * strip_width),
+        name="diag_last",
+    )(member, first, base, *strip, block)
 
 
 def shards(planes, cols, anc_inverse, panel, local_rows, inv_diag):
@@ -189,37 +243,76 @@
 
     class Strip:
         def __init__(self, block):
-            self.block, self.holders, self.apart = block, [0], cols // 2
+            self.block, self.holders, self.apart, self.made = block, [0], cols // 2, 0
 
         def hop(self):
             apart, holders = self.apart, self.holders
+            self.made += 1
             self.come = move(self.block, lambda z, y, c: (z, y, c ^ apart), lambda z, y, c: (c ^ z) in holders)
 
+        def has(self):
+            return functools.reduce(jnp.logical_or, [(col ^ plane) == h for h in self.holders])
+
         def keep(self):
-            has = functools.reduce(jnp.logical_or, [(col ^ plane) == h for h in self.holders])
-            if self.apart == 1:
-                return turn(has.astype(jnp.int32)[None], self.block, self.come)
-            self.block = jnp.where(has, self.block, self.come)
+            self.block = jnp.where(self.has(), self.block, self.come)
             self.holders = self.holders + [h ^ self.apart for h in self.holders]
             self.apart //= 2
-
-        def rest(self):
-            while True:
+            self.come = None
+
+        def finish(self):
+            if not self.made:
                 self.hop()
-                if done := self.keep():
-                    return done
+            while self.apart > 1:
+                self.keep()
+                self.hop()
+            return turn(self.has().astype(jnp.int32)[None], self.block, self.come)
 
     width = panel.shape[1]
     cut = max(1, round(CUT * width / 128)) * 128
     cuts = [(0, cut), (cut, width)] if cut < width else [(0, width)]
+    def at(event, value):
+        nonlocal strips
+        due = [k for (k, hop), (_, hold) in PLAN.items() if hold == event and k < len(strips) and strips[k].made == hop]
+        if due:
+            value, *comes = sync(value, *(strips[k].come for k in due))
+            for k, come in zip(due, comes):
+                strips[k].come = come
+        for (k, hop), (start, _) in PLAN.items():
+            if start == event and k < planes:
+                while len(strips) <= k:
+                    strips.append(Strip(joined_panel(len(strips))))
+                if hop == 2:
+                    strips[k].keep()
+                if event != "begin":
+                    strips[k].block, _ = sync(strips[k].block, value)
+                strips[k].hop()
+        return value
+
+    def joined_panel(k):
+        return jnp.concatenate([part[k] for part in panels], axis=1) if k else panel
+
+    strips = []
+    at("begin", None)
     panels = [[panel[:, a:b]] for a, b in cuts]
-    panels[0].append(onward(panels[0][0]))
+    for part in panels:
+        part.append(onward(part[0]))
     lists = jnp.stack([move(local_rows, lambda z, y, c: (c, y, z)), move(local_rows, lambda z, y, c: (c, 1 - y, z))])
     keep, send = pick(anc_inverse, local_rows, member[None], lists)
-    send, panels[0][1] = sync(send, panels[0][1])
+    if FIRST == "a":
+        send, panels[0][1] = sync(send, panels[0][1])
+    elif FIRST == "ab":
+        send, *firsts = sync(send, *(part[1] for part in panels))
+        for part, value in zip(panels, firsts):
+            part[1] = value
+    send = at("pick", send)
     apart, order = cols // 2, [0, cols // 2]
     own = [keep, move(keep, lambda z, y, c: (z, y, c ^ apart))]
     other = [to_partner(send), move(send, lambda z, y, c: (z, 1 - y, c ^ apart))]
+    for k, part in enumerate(panels):
+        part.append(onward(part[1]))
+        if NEAR == "ab"[k]:
+            part[2], own[1], *other = sync(part[2], own[1], *other)
+        part[2] = at("ab"[k] + "2", part[2])
     while apart > 1:
         apart //= 2
         for held in (own, other):
@@ -227,35 +320,43 @@
         order = order + [k ^ apart for k in order]
     wanted = col ^ ((plane - jnp.arange(planes, dtype=jnp.int32)) % planes)
     wanted = sum(jnp.where(wanted == k, i, 0) for i, k in enumerate(order))
-    for part in panels:
+    for k, part in enumerate(panels):
         while len(part) < planes:
             part.append(onward(part[-1]))
+        part[-1] = at("ab"[k] + "3", part[-1])
 
     kept, sent = off_parts(wanted, own, other, panels[0])
-    blocks = [panel] + [jnp.concatenate([part[k] for part in panels], axis=1) for k in range(1, planes)]
-    strips = [Strip(block) for block in sync(*blocks, sent)[:-1]]
-    early, late = strips[:GATED], strips[GATED:]
-    for strip in early:
-        strip.hop()
-    offs = [[kept + to_partner(sent)]]
-    offs[0].append(onward(offs[0][0]))
-    offs[0][1], *values = sync(offs[0][1], *(strip.come for strip in early))
-    for strip, value in zip(early, values):
-        strip.come = value
-        strip.keep()
+    sent = at("k1a", sent)
+    value = kept + to_partner(sent)
+    if LAST and len(panels) > 1:
+        value, panels[1][-1] = sync(value, panels[1][-1])
+    offs = [[at("xa", value)]]
+    offs[0].append(at("y1a", onward(offs[0][0])))
     for part in panels[1:]:
         kept, sent = off_parts(wanted, own, other, part)
-        offs.append([kept + to_partner(sent)])
-    for part in offs:
-        while len(part) < planes:
-            part.append(onward(part[-1]))
-    turned = [strip.rest() for strip in strips]
+        sent = at("k1b", sent)
+        value = kept + to_partner(sent)
+        if SKEW:
+            value, offs[0][1] = sync(value, offs[0][1])
+        offs.append([at("xb", value)])
+        offs[-1].append(at("y1b", onward(offs[-1][0])))
+    for step in range(2, planes):
+        for k, part in enumerate(offs):
+            part.append(at(f"y{step}" + "ab"[k], onward(part[-1])))
+    while len(strips) < planes:
+        strips.append(Strip(joined_panel(len(strips))))
+    turned = [strip.finish() for strip in strips]
     diag, gate = [], None
     for (start, _), part in zip(cuts, offs):
         if gate is not None:
             part[-1], _ = sync(part[-1], gate)
-        kept, sent = diag_parts(member[None], inv_diag, start, turned, part)
-        gate = sent
+        if SPLIT:
+            total = diag_first(turned[:-1], part[:-1])
+            kept, sent = diag_last(member[None], total, inv_diag, start, turned[-1], part[-1])
+        else:
+            kept, sent = diag_parts(member[None], inv_diag, start, turned, part)
+        if ORDER:
+            gate = sent
         diag.append(kept - to_partner(sent))
     return jnp.concatenate([part[0] for part in offs], axis=1), jnp.concatenate(diag, axis=1)
 

time: 142 us -> 134 us (0.944)
  waiting for transfers between devices: 60.4 us -> 50.9 us
  Pallas kernels: 18.9 us -> 23.3 us
  starting transfers between devices: 44.6 us -> 41 us
    ppermute x33, waiting for transfers between devices: 60.4 us -> 50.9 us  [move(): lax.ppermute(x, axes, [(place(*d), place(*target(*d))) for d in grid if s...]
    ppermute x33, starting transfers between devices: 44.6 us -> 41 us  [move(): lax.ppermute(x, axes, [(place(*d), place(*target(*d))) for d in grid if s...]
    pallas_call x2, Pallas kernels: 4 us -> 6.85 us  [off_parts(): pl.pallas_call(functools.partial(off_kernel, len(own)), grid_spec=pltpu.P...]
    unnamed x10 -> x18, local copies, waits for them, and re-layouts: 3.72 us -> 4.94 us
    pallas_call x2 -> x4, Pallas kernels: 5.77 us -> 6.75 us  [the longest x2 4.54 us: diag_first(): pl.pallas_call(diag_first_kernel, grid=(1,), in_specs=[whole(*x.shape) fo...]
  transfers between devices with their start and end apart: 33 -> 33, of which waited for: 14 -> 10; matrix products, arithmetic and copies ran while one was open for 7% -> 8% of each run, Pallas kernels for 13% -> 18%
where the time goes in v3:
time: 134 us; the launch traced here: 133 us
  waiting for transfers between devices  50.9 us (38%)
  starting transfers between devices  41 us (31%)
  Pallas kernels  23.3 us (17%)
  other arithmetic  9.33 us (7%)
  local copies, waits for them, and re-layouts  7.79 us (6%)
    ppermute x33, waiting for transfers between devices, move(): lax.ppermute(x, axes, [(place(*d), place(*target(*d))) for d in grid if s...  50.9 us
    ppermute x33, starting transfers between devices, move(): lax.ppermute(x, axes, [(place(*d), place(*target(*d))) for d in grid if s...  41 us
    pallas_call x2, Pallas kernels, off_parts(): pl.pallas_call(functools.partial(off_kernel, len(own)), grid_spec=pltpu.P...  6.85 us
    pallas_call x4, Pallas kernels, turn(): pl.pallas_call(turn_kernel, grid_spec=pltpu.PrefetchScalarGridSpec(num_sc...  5.47 us
    unnamed x18, local copies, waits for them, and re-layouts  4.94 us
    pallas_call x2, Pallas kernels, diag_first(): pl.pallas_call(diag_first_kernel, grid=(1,), in_specs=[whole(*x.shape) fo...  4.54 us
    select_n x4, other arithmetic, keep(): self.block = jnp.where(self.has(), self.block, self.come)  4.45 us
    pallas_call x1, Pallas kernels, pick(): pl.pallas_call(pick_kernel, grid_spec=pltpu.PrefetchScalarGridSpec(num_sc...  4.27 us
  transfers between devices with their start and end apart: 33, of which 10 were waited for; matrix products, arithmetic and copies ran while one was open for 8% of the time, Pallas kernels for 18%

profile of v3, /device:TPU:0, one launch (start us, length us, event | category | flops | bytes accessed | tf_op | source)
XLA Modules:
  0.0 133.4 jit_solution(14604460040258073437)
XLA Ops:
  0.6 1.1 slice.6.refs_8_
  1.7 3.1 %collective-permute-start.5 = (f32[240,384]{1,0:T(8,128)S(1)}, f32[240,384]{1,0:T(8,128)S(1)}, u32[]{:S(2)}, u32[]{:S(2)}) collective-permute-start(f32[240,384]{1,0:T(8,128)S(1)} %slice.6.refs_8_), channel_id=1, source_target_pairs={{0,8},{1,9},{2,10},{3,11},{4,12},{5,13},{6,14},{7,15},{8,16},{9,17... | collective-permute-start | bytes 1105928 | tf_op jit(solution)/shard_map/ppermute | solution.py:233
  4.8 1.5 %collective-permute-start.1 = (s32[240]{0:T(256)}, s32[240]{0:T(256)S(1)}, u32[]{:S(2)}, u32[]{:S(2)}) collective-permute-start(s32[240]{0:T(256)} %rows_ref.1), channel_id=1, source_target_pairs={{0,4},{1,12},{2,20},{3,28},{4,0},{5,8},{6,16},{7,24},{8,5},{9,13},... | collective-permute-start | bytes 2888 | tf_op jit(solution)/shard_map/ppermute | solution.py:233
  6.3 1.3 collective-permute-start
  7.7 1.0 slice.7.refs_8_
  8.6 3.4 %collective-permute-start.13 = (f32[240,256]{1,0:T(8,128)S(1)}, f32[240,256]{1,0:T(8,128)S(1)}, u32[]{:S(2)}, u32[]{:S(2)}) collective-permute-start(f32[240,256]{1,0:T(8,128)S(1)} %slice.7.refs_8_), channel_id=1, source_target_pairs={{0,8},{1,9},{2,10},{3,11},{4,12},{5,13},{6,14},{7,15},{8,16},{9,17... | collective-permute-start | bytes 737288 | tf_op jit(solution)/shard_map/ppermute | solution.py:233
  12.0 0.8 copy.6.own_ref
  12.9 0.7 copy-done.8
  13.5 4.3 %pick_compact.1 = (f32[240,240]{1,0:T(8,128)S(1)}, f32[240,240]{1,0:T(8,128)S(1)}) custom-call(s32[240]{0:T(256)S(1)} %copy-done.8, s32[1]{0:T(128)} %bitcast.member_ref, f32[2048,4096]{1,0:T(8,128)} %anc.1, s32[240,1]{1,0:T(8,128)S(1)} %copy.6.own_ref, s32[2,240]{1,0:T(2,128)S(1)} %pad_add_fusion.lists_ref), custom_call_target="tpu_custom_call" | custom-call | flops 943718400 | bytes 15728640 | tf_op jit(solution)/shard_map/pick_compact/pallas_call | solution.py:67
  17.8 4.5 %collective-permute-start.2 = (f32[240,240]{1,0:T(8,128)S(1)}, f32[240,240]{1,0:T(8,128)}, u32[]{:S(2)}, u32[]{:S(2)}) collective-permute-start(f32[240,240]{1,0:T(8,128)S(1)} %get-tuple-element.36.refs_0_), channel_id=1, source_target_pairs={{0,2},{1,3},{2,0},{3,1},{4,6},{5,7},{6,4},{7,5},{8,10},{9,11},{10,... | collective-permute-start | bytes 691208 | tf_op jit(solution)/shard_map/ppermute | solution.py:233
  22.4 1.7 %collective-permute-start.14 = (f32[240,256]{1,0:T(8,128)S(1)}, f32[240,256]{1,0:T(8,128)S(1)}, u32[]{:S(2)}, u32[]{:S(2)}) collective-permute-start(f32[240,256]{1,0:T(8,128)S(1)} %collective-permute-done.13.refs_9_), channel_id=1, source_target_pairs={{0,8},{1,9},{2,10},{3,11},{4,12},{5,13},{6,14},{7,15},{8,16},{9,17... | collective-permute-start | bytes 737288 | tf_op jit(solution)/shard_map/ppermute | solution.py:233
  24.0 0.1 collective-permute-start.3
  24.2 0.7 copy-done.4
  24.9 0.6 collective-permute-start.6
  25.5 3.0 %collective-permute-done.2.refs_1_ = f32[240,240]{1,0:T(8,128)} collective-permute-done((f32[240,240]{1,0:T(8,128)S(1)}, f32[240,240]{1,0:T(8,128)}, u32[]{:S(2)}, u32[]{:S(2)}) %collective-permute-start.2) | collective-permute-done | bytes 230432 | tf_op jit(solution)/shard_map/ppermute | solution.py:233
  28.5 2.2 %collective-permute-start.7 = (f32[240,240]{1,0:T(8,128)S(1)}, f32[240,240]{1,0:T(8,128)}, u32[]{:S(2)}, u32[]{:S(2)}) collective-permute-start(f32[240,240]{1,0:T(8,128)S(1)} %get-tuple-element.38), channel_id=1, source_target_pairs={{0,6},{1,7},{2,4},{3,5},{4,2},{5,3},{6,0},{7,1},{8,14},{9,15},{10,... | collective-permute-start | bytes 691208 | tf_op jit(solution)/shard_map/ppermute | solution.py:233
  30.7 10.0 %collective-permute-done.14.refs_10_ = f32[240,256]{1,0:T(8,128)S(1)} collective-permute-done((f32[240,256]{1,0:T(8,128)S(1)}, f32[240,256]{1,0:T(8,128)S(1)}, u32[]{:S(2)}, u32[]{:S(2)}) %collective-permute-start.14) | collective-permute-done | bytes 245792 | tf_op jit(solution)/shard_map/ppermute | solution.py:233
  40.7 0.7 copy-done.6
  41.4 0.1 collective-permute-start.4
  41.5 0.4 collective-permute-start.8
  41.9 0.1 collective-permute-start.9
  42.0 1.2 collective-permute-done.4.refs_3_
  43.2 8.0 %collective-permute-done.15.refs_11_ = f32[240,256]{1,0:T(8,128)S(1)} collective-permute-done((f32[240,256]{1,0:T(8,128)S(1)}, f32[240,256]{1,0:T(8,128)S(1)}, u32[]{:S(2)}, u32[]{:S(2)}) %collective-permute-start.15) | collective-permute-done | bytes 245792 | tf_op jit(solution)/shard_map/ppermute | solution.py:233
  51.3 0.9 copy-done.5
  52.2 0.9 copy-done.7
  53.2 3.1 %off_parts.3 = (f32[240,256]{1,0:T(8,128)S(1)}, f32[240,256]{1,0:T(8,128)S(1)}) custom-call(s32[4]{0:T(128)S(1)} %fusion.2.order_ref, f32[240,240]{1,0:T(8,128)S(1)} %copy-done.5, f32[240,240]{1,0:T(8,128)} %collective-permute-done.2.refs_1_, f32[240,240]{1,0:T(8,128)S(1)} %copy-done.7, f32[240,240]{1,0:T(8,128)} %collective-permute-done.4.refs_3_, ...), custom_call_target="tpu_custom_call" | custom-call | flops 707788800 | bytes 1843200 | tf_op jit(solution)/shard_map/off_parts/pallas_call | solution.py:100
  56.3 0.5 collective-permute-start.16
  56.8 0.9 pad_maximum_fusion.3
  57.6 2.6 %collective-permute-start.23 = (f32[240,640]{1,0:T(8,128)}, f32[240,640]{1,0:T(8,128)}, u32[]{:S(2)}, u32[]{:S(2)}) collective-permute-start(f32[240,640]{1,0:T(8,128)} %pad_maximum_fusion.3), channel_id=1, source_target_pairs={{0,2},{4,6},{9,11},{13,15},{18,16},{22,20},{27,25},{31,29}} | collective-permute-start | bytes 1843208 | tf_op jit(solution)/shard_map/ppermute | solution.py:233
  60.2 3.8 %off_parts.2 = (f32[240,384]{1,0:T(8,128)S(1)}, f32[240,384]{1,0:T(8,128)S(1)}) custom-call(s32[4]{0:T(128)S(1)} %fusion.2.order_ref, f32[240,240]{1,0:T(8,128)S(1)} %copy-done.5, f32[240,240]{1,0:T(8,128)} %collective-permute-done.2.refs_1_, f32[240,240]{1,0:T(8,128)S(1)} %copy-done.7, f32[240,240]{1,0:T(8,128)} %collective-permute-done.4.refs_3_, ...), custom_call_target="tpu_custom_call" | custom-call | flops 1061683200 | bytes 1843200 | tf_op jit(solution)/shard_map/off_parts/pallas_call | solution.py:100
  63.9 1.7 %collective-permute-start.12 = (f32[240,384]{1,0:T(8,128)S(1)}, f32[240,384]{1,0:T(8,128)}, u32[]{:S(2)}, u32[]{:S(2)}) collective-permute-start(f32[240,384]{1,0:T(8,128)S(1)} %get-tuple-element.41), channel_id=1, source_target_pairs={{0,4},{1,5},{2,6},{3,7},{4,0},{5,1},{6,2},{7,3},{8,12},{9,13},{10,... | collective-permute-start | bytes 1105928 | tf_op jit(solution)/shard_map/ppermute | solution.py:233
  65.7 0.9 pad_maximum_fusion.2
  66.6 2.1 %collective-permute-start.18 = (f32[240,640]{1,0:T(8,128)}, f32[240,640]{1,0:T(8,128)}, u32[]{:S(2)}, u32[]{:S(2)}) collective-permute-start(f32[240,640]{1,0:T(8,128)} %param.5), channel_id=1, source_target_pairs={{0,2},{4,6},{9,11},{13,15},{18,16},{22,20},{27,25},{31,29}} | collective-permute-start | bytes 1843208 | tf_op jit(solution)/shard_map/ppermute | solution.py:233
  68.7 2.1 %collective-permute-start.19 = (f32[240,640]{1,0:T(8,128)}, f32[240,640]{1,0:T(8,128)}, u32[]{:S(2)}, u32[]{:S(2)}) collective-permute-start(f32[240,640]{1,0:T(8,128)} %pad_maximum_fusion.2), channel_id=1, source_target_pairs={{0,2},{4,6},{9,11},{13,15},{18,16},{22,20},{27,25},{31,29}} | collective-permute-start | bytes 1843208 | tf_op jit(solution)/shard_map/ppermute | solution.py:233
  70.9 2.9 %collective-permute-done.21.refs_7_ = f32[240,256]{1,0:T(8,128)S(1)} collective-permute-done((f32[240,256]{1,0:T(8,128)S(1)}, f32[240,256]{1,0:T(8,128)S(1)}, u32[]{:S(2)}, u32[]{:S(2)}) %collective-permute-start.21) | collective-permute-done | bytes 245792 | tf_op jit(solution)/shard_map/ppermute | solution.py:233
  73.7 1.1 add.28.refs_6_
  75.0 1.3 collective-permute-start.27
  76.3 6.8 %collective-permute-done.22.refs_8_ = f32[240,256]{1,0:T(8,128)} collective-permute-done((f32[240,256]{1,0:T(8,128)S(1)}, f32[240,256]{1,0:T(8,128)}, u32[]{:S(2)}, u32[]{:S(2)}) %collective-permute-start.22) | collective-permute-done | bytes 245792 | tf_op jit(solution)/shard_map/ppermute | solution.py:233
  83.1 1.1 broadcast_select_fusion.2.held
  84.2 2.1 %collective-permute-start.24 = (f32[240,640]{1,0:T(8,128)S(1)}, f32[240,640]{1,0:T(8,128)}, u32[]{:S(2)}, u32[]{:S(2)}) collective-permute-start(f32[240,640]{1,0:T(8,128)S(1)} %broadcast_select_fusion.2.held), channel_id=1, source_target_pairs={{0,1},{2,3},{4,5},{6,7},{9,8},{11,10},{13,12},{15,14},{16,17},{18,... | collective-permute-start | bytes 1843208 | tf_op jit(solution)/shard_map/ppermute | solution.py:233
  86.4 0.6 collective-permute-done.17.refs_7_
  86.9 2.1 %broadcast_select_fusion.3.held = f32[240,640]{1,0:T(8,128)} fusion(f32[240,640]{1,0:T(8,128)} %param.5, f32[240,640]{1,0:T(8,128)} %collective-permute-done.18, pred[]{:T(512)S(6)} %eq.17), kind=kLoop, calls=%fused_computation.8 | loop fusion | flops 153600 | bytes 1843201 | tf_op jit(solution)/shard_map/jit(_where)/select_n | solution.py:257
  89.0 2.1 %collective-permute-start.20 = (f32[240,640]{1,0:T(8,128)}, f32[240,640]{1,0:T(8,128)}, u32[]{:S(2)}, u32[]{:S(2)}) collective-permute-start(f32[240,640]{1,0:T(8,128)} %broadcast_select_fusion.3.held), channel_id=1, source_target_pairs={{0,1},{2,3},{4,5},{6,7},{9,8},{11,10},{13,12},{15,14},{16,17},{18,... | collective-permute-start | bytes 1843208 | tf_op jit(solution)/shard_map/ppermute | solution.py:233
  91.2 1.1 broadcast_select_fusion.1.held
  92.3 2.1 %collective-permute-start.25 = (f32[240,640]{1,0:T(8,128)S(1)}, f32[240,640]{1,0:T(8,128)}, u32[]{:S(2)}, u32[]{:S(2)}) collective-permute-start(f32[240,640]{1,0:T(8,128)S(1)} %broadcast_select_fusion.1.held), channel_id=1, source_target_pairs={{0,1},{2,3},{4,5},{6,7},{9,8},{11,10},{13,12},{15,14},{16,17},{18,... | collective-permute-start | bytes 1843208 | tf_op jit(solution)/shard_map/ppermute | solution.py:233
  94.4 1.9 %collective-permute-done.26.refs_8_ = f32[240,384]{1,0:T(8,128)} collective-permute-done((f32[240,384]{1,0:T(8,128)S(1)}, f32[240,384]{1,0:T(8,128)}, u32[]{:S(2)}, u32[]{:S(2)}) %collective-permute-start.26) | collective-permute-done | bytes 368672 | tf_op jit(solution)/shard_map/ppermute | solution.py:233
  96.4 0.1 broadcast_select_fusion.held
  96.4 2.1 %collective-permute-start.29 = (f32[240,640]{1,0:T(8,128)S(1)}, f32[240,640]{1,0:T(8,128)}, u32[]{:S(2)}, u32[]{:S(2)}) collective-permute-start(f32[240,640]{1,0:T(8,128)S(1)} %broadcast_select_fusion.held), channel_id=1, source_target_pairs={{0,1},{2,3},{4,5},{6,7},{9,8},{11,10},{13,12},{15,14},{16,17},{18,... | collective-permute-start | bytes 1843208 | tf_op jit(solution)/shard_map/ppermute | solution.py:233
  98.6 0.8 collective-permute-start.31
  99.4 1.3 turn_strip.5
  100.8 1.5 %turn_strip.4 = (bf16[640,240]{1,0:T(8,128)(2,1)S(1)}, bf16[640,240]{1,0:T(8,128)(2,1)S(1)}) custom-call(s32[1]{0:T(128)} %bitcast.4.flag_ref, f32[240,640]{1,0:T(8,128)} %broadcast_select_fusion.3.held, f32[240,640]{1,0:T(8,128)} %collective-permute-done.20.come), custom_call_target="tpu_custom_call" | custom-call | bytes 1843200 | tf_op jit(solution)/shard_map/turn_strip/pallas_call | solution.py:123
  102.3 1.3 turn_strip.6
  103.6 1.0 copy-done.3
  104.6 2.7 %diag_first.2.first = f32[640,384]{1,0:T(8,128)S(1)} custom-call(bf16[640,240]{1,0:T(8,128)(2,1)S(1)} %get-tuple-element.47.refs_0_, bf16[640,240]{1,0:T(8,128)(2,1)S(1)} %get-tuple-element.50.refs_1_, bf16[640,240]{1,0:T(8,128)(2,1)S(1)} %get-tuple-element.52.refs_2_, bf16[640,240]{1,0:T(8,128)(2,1)S(1)} %get-tuple-element.53.refs_3_, ...), custom_call_target="tpu_custom_call" | custom-call | flops 1061683200 | bytes 1843200 | tf_op jit(solution)/shard_map/diag_first/pallas_call | solution.py:183
  107.3 5.0 %collective-permute-done.28.block = f32[240,384]{1,0:T(8,128)} collective-permute-done((f32[240,384]{1,0:T(8,128)}, f32[240,384]{1,0:T(8,128)}, u32[]{:S(2)}, u32[]{:S(2)}) %collective-permute-start.28) | collective-permute-done | bytes 368672 | tf_op jit(solution)/shard_map/ppermute | solution.py:233
  112.2 1.3 turn_strip.7
  113.6 1.7 %diag_last.2 = (f32[320,384]{1,0:T(8,128)S(1)}, f32[320,384]{1,0:T(8,128)S(1)}) custom-call(s32[1]{0:T(128)} %bitcast.member_ref, f32[640,384]{1,0:T(8,128)S(1)} %diag_first.2.first, f32[320,640]{1,0:T(8,128)S(1)} %copy-done, bf16[640,240]{1,0:T(8,128)(2,1)S(1)} %get-tuple-element.63.high, bf16[640,240]{1,0:T(8,128)(2,1)S(1)} %get-tuple-element.64.low, ...), custom_call_target="tpu_custom_call" | custom-call | flops 353894400 | bytes 1228800 | tf_op jit(solution)/shard_map/diag_last/pallas_call | solution.py:207
  115.3 0.8 collective-permute-start.30
  116.1 1.9 %diag_first.3.first = f32[640,256]{1,0:T(8,128)S(1)} custom-call(bf16[640,240]{1,0:T(8,128)(2,1)S(1)} %get-tuple-element.47.refs_0_, bf16[640,240]{1,0:T(8,128)(2,1)S(1)} %get-tuple-element.50.refs_1_, bf16[640,240]{1,0:T(8,128)(2,1)S(1)} %get-tuple-element.52.refs_2_, bf16[640,240]{1,0:T(8,128)(2,1)S(1)} %get-tuple-element.53.refs_3_, ...), custom_call_target="tpu_custom_call" | custom-call | flops 707788800 | bytes 1843200 | tf_op jit(solution)/shard_map/diag_first/pallas_call | solution.py:183
  118.0 0.5 diag_last.3
  118.5 1.3 %collective-permute-start.32 = (f32[320,256]{1,0:T(8,128)S(1)}, f32[320,256]{1,0:T(8,128)S(1)}, u32[]{:S(2)}, u32[]{:S(2)}) collective-permute-start(f32[320,256]{1,0:T(8,128)S(1)} %get-tuple-element.69), channel_id=1, source_target_pairs={{0,4},{1,5},{2,6},{3,7},{4,0},{5,1},{6,2},{7,3},{8,12},{9,13},{10,... | collective-permute-start | bytes 983048 | tf_op jit(solution)/shard_map/ppermute | solution.py:233
  119.9 0.9 pad_maximum_fusion.1
  120.7 11.6 %collective-permute-done.32 = f32[320,256]{1,0:T(8,128)S(1)} collective-permute-done((f32[320,256]{1,0:T(8,128)S(1)}, f32[320,256]{1,0:T(8,128)S(1)}, u32[]{:S(2)}, u32[]{:S(2)}) %collective-permute-start.32) | collective-permute-done | bytes 327712 | tf_op jit(solution)/shard_map/ppermute | solution.py:233
  132.4 0.9 pad_maximum_fusion
  (49 shorter events, 0.4 us)
Async XLA Ops:
  0.6 112.9 %copy-start = (f32[320,640]{1,0:T(8,128)S(1)}, f32[320,640]{1,0:T(8,128)}, u32[]{:S(2)}) copy-start(f32[320,640]{1,0:T(8,128)} %base_ref.3) | copy-start | bytes 2457604
  1.7 20.6 %collective-permute-start.5 = (f32[240,384]{1,0:T(8,128)S(1)}, f32[240,384]{1,0:T(8,128)S(1)}, u32[]{:S(2)}, u32[]{:S(2)}) collective-permute-start(f32[240,384]{1,0:T(8,128)S(1)} %slice.6.refs_8_), channel_id=1, source_target_pairs={{0,8},{1,9},{2,10},{3,11},{4,12},{5,13},{6,14},{7,15},{8,16},{9,17... | collective-permute-start | bytes 1105928 | tf_op jit(solution)/shard_map/ppermute | solution.py:233
  4.8 8.0 %collective-permute-start.1 = (s32[240]{0:T(256)}, s32[240]{0:T(256)S(1)}, u32[]{:S(2)}, u32[]{:S(2)}) collective-permute-start(s32[240]{0:T(256)} %rows_ref.1), channel_id=1, source_target_pairs={{0,4},{1,12},{2,20},{3,28},{4,0},{5,8},{6,16},{7,24},{8,5},{9,13},... | collective-permute-start | bytes 2888 | tf_op jit(solution)/shard_map/ppermute | solution.py:233
  6.3 6.5 %collective-permute-start = (s32[240]{0:T(256)}, s32[240]{0:T(256)S(1)}, u32[]{:S(2)}, u32[]{:S(2)}) collective-permute-start(s32[240]{0:T(256)} %rows_ref.1), channel_id=1, source_target_pairs={{0,0},{1,8},{2,16},{3,24},{4,4},{5,12},{6,20},{7,28},{8,1},{9,9},{... | collective-permute-start | bytes 2888 | tf_op jit(solution)/shard_map/ppermute | solution.py:233
  8.6 13.7 %collective-permute-start.13 = (f32[240,256]{1,0:T(8,128)S(1)}, f32[240,256]{1,0:T(8,128)S(1)}, u32[]{:S(2)}, u32[]{:S(2)}) collective-permute-start(f32[240,256]{1,0:T(8,128)S(1)} %slice.7.refs_8_), channel_id=1, source_target_pairs={{0,8},{1,9},{2,10},{3,11},{4,12},{5,13},{6,14},{7,15},{8,16},{9,17... | collective-permute-start | bytes 737288 | tf_op jit(solution)/shard_map/ppermute | solution.py:233
  12.9 0.7 copy-start.8
  17.8 10.7 %collective-permute-start.2 = (f32[240,240]{1,0:T(8,128)S(1)}, f32[240,240]{1,0:T(8,128)}, u32[]{:S(2)}, u32[]{:S(2)}) collective-permute-start(f32[240,240]{1,0:T(8,128)S(1)} %get-tuple-element.36.refs_0_), channel_id=1, source_target_pairs={{0,2},{1,3},{2,0},{3,1},{4,6},{5,7},{6,4},{7,5},{8,10},{9,11},{10,... | collective-permute-start | bytes 691208 | tf_op jit(solution)/shard_map/ppermute | solution.py:233
  22.4 19.6 %collective-permute-start.10 = (f32[240,384]{1,0:T(8,128)S(1)}, f32[240,384]{1,0:T(8,128)S(1)}, u32[]{:S(2)}, u32[]{:S(2)}) collective-permute-start(f32[240,384]{1,0:T(8,128)S(1)} %collective-permute-done.5.refs_9_), channel_id=1, source_target_pairs={{0,8},{1,9},{2,10},{3,11},{4,12},{5,13},{6,14},{7,15},{8,16},{9,17... | collective-permute-start | bytes 1105928 | tf_op jit(solution)/shard_map/ppermute | solution.py:233
  22.4 18.3 %collective-permute-start.14 = (f32[240,256]{1,0:T(8,128)S(1)}, f32[240,256]{1,0:T(8,128)S(1)}, u32[]{:S(2)}, u32[]{:S(2)}) collective-permute-start(f32[240,256]{1,0:T(8,128)S(1)} %collective-permute-done.13.refs_9_), channel_id=1, source_target_pairs={{0,8},{1,9},{2,10},{3,11},{4,12},{5,13},{6,14},{7,15},{8,16},{9,17... | collective-permute-start | bytes 737288 | tf_op jit(solution)/shard_map/ppermute | solution.py:233
  24.0 16.6 %collective-permute-start.3 = (f32[240,240]{1,0:T(8,128)S(1)}, f32[240,240]{1,0:T(8,128)S(1)}, u32[]{:S(2)}, u32[]{:S(2)}) collective-permute-start(f32[240,240]{1,0:T(8,128)S(1)} %get-tuple-element.36.refs_0_), channel_id=1, source_target_pairs={{0,1},{1,0},{2,3},{3,2},{4,5},{5,4},{6,7},{7,6},{8,9},{9,8},{10,11... | collective-permute-start | bytes 691208 | tf_op jit(solution)/shard_map/ppermute | solution.py:233
  24.2 0.7 copy-start.4
  24.9 16.6 %collective-permute-start.6 = (f32[240,240]{1,0:T(8,128)S(1)}, f32[240,240]{1,0:T(8,128)}, u32[]{:S(2)}, u32[]{:S(2)}) collective-permute-start(f32[240,240]{1,0:T(8,128)S(1)} %get-tuple-element.38), channel_id=1, source_target_pairs={{0,4},{1,5},{2,6},{3,7},{4,0},{5,1},{6,2},{7,3},{8,12},{9,13},{10,... | collective-permute-start | bytes 691208 | tf_op jit(solution)/shard_map/ppermute | solution.py:233
  28.5 13.4 %collective-permute-start.7 = (f32[240,240]{1,0:T(8,128)S(1)}, f32[240,240]{1,0:T(8,128)}, u32[]{:S(2)}, u32[]{:S(2)}) collective-permute-start(f32[240,240]{1,0:T(8,128)S(1)} %get-tuple-element.38), channel_id=1, source_target_pairs={{0,6},{1,7},{2,4},{3,5},{4,2},{5,3},{6,0},{7,1},{8,14},{9,15},{10,... | collective-permute-start | bytes 691208 | tf_op jit(solution)/shard_map/ppermute | solution.py:233
  40.7 10.6 %collective-permute-start.15 = (f32[240,256]{1,0:T(8,128)S(1)}, f32[240,256]{1,0:T(8,128)S(1)}, u32[]{:S(2)}, u32[]{:S(2)}) collective-permute-start(f32[240,256]{1,0:T(8,128)S(1)} %collective-permute-done.14.refs_10_), channel_id=1, source_target_pairs={{0,8},{1,9},{2,10},{3,11},{4,12},{5,13},{6,14},{7,15},{8,16},{9,17... | collective-permute-start | bytes 737288 | tf_op jit(solution)/shard_map/ppermute | solution.py:233
  40.7 0.7 copy-start.6
  41.4 1.9 %collective-permute-start.4 = (f32[240,240]{1,0:T(8,128)}, f32[240,240]{1,0:T(8,128)}, u32[]{:S(2)}, u32[]{:S(2)}) collective-permute-start(f32[240,240]{1,0:T(8,128)} %collective-permute-done.2.refs_1_), channel_id=1, source_target_pairs={{0,1},{1,0},{2,3},{3,2},{4,5},{5,4},{6,7},{7,6},{8,9},{9,8},{10,11... | collective-permute-start | bytes 691208 | tf_op jit(solution)/shard_map/ppermute | solution.py:233
  41.5 9.8 %collective-permute-start.8 = (f32[240,240]{1,0:T(8,128)}, f32[240,240]{1,0:T(8,128)}, u32[]{:S(2)}, u32[]{:S(2)}) collective-permute-start(f32[240,240]{1,0:T(8,128)} %collective-permute-done.6.refs_4_), channel_id=1, source_target_pairs={{0,1},{1,0},{2,3},{3,2},{4,5},{5,4},{6,7},{7,6},{8,9},{9,8},{10,11... | collective-permute-start | bytes 691208 | tf_op jit(solution)/shard_map/ppermute | solution.py:233
  41.9 9.4 %collective-permute-start.9 = (f32[240,240]{1,0:T(8,128)}, f32[240,240]{1,0:T(8,128)}, u32[]{:S(2)}, u32[]{:S(2)}) collective-permute-start(f32[240,240]{1,0:T(8,128)} %collective-permute-done.7.refs_5_), channel_id=1, source_target_pairs={{0,1},{1,0},{2,3},{3,2},{4,5},{5,4},{6,7},{7,6},{8,9},{9,8},{10,11... | collective-permute-start | bytes 691208 | tf_op jit(solution)/shard_map/ppermute | solution.py:233
  42.0 18.2 %collective-permute-start.11 = (f32[240,384]{1,0:T(8,128)S(1)}, f32[240,384]{1,0:T(8,128)S(1)}, u32[]{:S(2)}, u32[]{:S(2)}) collective-permute-start(f32[240,384]{1,0:T(8,128)S(1)} %collective-permute-done.10.refs_10_), channel_id=1, source_target_pairs={{0,8},{1,9},{2,10},{3,11},{4,12},{5,13},{6,14},{7,15},{8,16},{9,17... | collective-permute-start | bytes 1105928 | tf_op jit(solution)/shard_map/ppermute | solution.py:233
  51.3 0.9 copy-start.5
  52.2 0.9 copy-start.7
  56.3 9.4 %collective-permute-start.16 = (f32[240,256]{1,0:T(8,128)S(1)}, f32[240,256]{1,0:T(8,128)S(1)}, u32[]{:S(2)}, u32[]{:S(2)}) collective-permute-start(f32[240,256]{1,0:T(8,128)S(1)} %get-tuple-element.43), channel_id=1, source_target_pairs={{0,4},{1,5},{2,6},{3,7},{4,0},{5,1},{6,2},{7,3},{8,12},{9,13},{10,... | collective-permute-start | bytes 737288 | tf_op jit(solution)/shard_map/ppermute | solution.py:233
  57.6 17.4 %collective-permute-start.23 = (f32[240,640]{1,0:T(8,128)}, f32[240,640]{1,0:T(8,128)}, u32[]{:S(2)}, u32[]{:S(2)}) collective-permute-start(f32[240,640]{1,0:T(8,128)} %pad_maximum_fusion.3), channel_id=1, source_target_pairs={{0,2},{4,6},{9,11},{13,15},{18,16},{22,20},{27,25},{31,29}} | collective-permute-start | bytes 1843208 | tf_op jit(solution)/shard_map/ppermute | solution.py:233
  63.9 9.8 %copy-start.1 = (f32[240,384]{1,0:T(8,128)}, f32[240,384]{1,0:T(8,128)S(1)}, u32[]{:S(2)}) copy-start(f32[240,384]{1,0:T(8,128)S(1)} %get-tuple-element.40) | copy-start | bytes 1105924
  63.9 9.8 %collective-permute-start.12 = (f32[240,384]{1,0:T(8,128)S(1)}, f32[240,384]{1,0:T(8,128)}, u32[]{:S(2)}, u32[]{:S(2)}) collective-permute-start(f32[240,384]{1,0:T(8,128)S(1)} %get-tuple-element.41), channel_id=1, source_target_pairs={{0,4},{1,5},{2,6},{3,7},{4,0},{5,1},{6,2},{7,3},{8,12},{9,13},{10,... | collective-permute-start | bytes 1105928 | tf_op jit(solution)/shard_map/ppermute | solution.py:233
  65.7 8.0 %collective-permute-start.21 = (f32[240,256]{1,0:T(8,128)S(1)}, f32[240,256]{1,0:T(8,128)S(1)}, u32[]{:S(2)}, u32[]{:S(2)}) collective-permute-start(f32[240,256]{1,0:T(8,128)S(1)} %add.29.refs_6_), channel_id=1, source_target_pairs={{0,8},{1,9},{2,10},{3,11},{4,12},{5,13},{6,14},{7,15},{8,16},{9,17... | collective-permute-start | bytes 737288 | tf_op jit(solution)/shard_map/ppermute | solution.py:233
  66.6 19.8 %collective-permute-start.18 = (f32[240,640]{1,0:T(8,128)}, f32[240,640]{1,0:T(8,128)}, u32[]{:S(2)}, u32[]{:S(2)}) collective-permute-start(f32[240,640]{1,0:T(8,128)} %param.5), channel_id=1, source_target_pairs={{0,2},{4,6},{9,11},{13,15},{18,16},{22,20},{27,25},{31,29}} | collective-permute-start | bytes 1843208 | tf_op jit(solution)/shard_map/ppermute | solution.py:233
  68.7 17.6 %collective-permute-start.19 = (f32[240,640]{1,0:T(8,128)}, f32[240,640]{1,0:T(8,128)}, u32[]{:S(2)}, u32[]{:S(2)}) collective-permute-start(f32[240,640]{1,0:T(8,128)} %pad_maximum_fusion.2), channel_id=1, source_target_pairs={{0,2},{4,6},{9,11},{13,15},{18,16},{22,20},{27,25},{31,29}} | collective-permute-start | bytes 1843208 | tf_op jit(solution)/shard_map/ppermute | solution.py:233
  73.7 9.4 %collective-permute-start.22 = (f32[240,256]{1,0:T(8,128)S(1)}, f32[240,256]{1,0:T(8,128)}, u32[]{:S(2)}, u32[]{:S(2)}) collective-permute-start(f32[240,256]{1,0:T(8,128)S(1)} %collective-permute-done.21.refs_7_), channel_id=1, source_target_pairs={{0,8},{1,9},{2,10},{3,11},{4,12},{5,13},{6,14},{7,15},{8,16},{9,17... | collective-permute-start | bytes 737288 | tf_op jit(solution)/shard_map/ppermute | solution.py:233
  74.9 12.1 %collective-permute-start.17 = (f32[240,384]{1,0:T(8,128)S(1)}, f32[240,384]{1,0:T(8,128)S(1)}, u32[]{:S(2)}, u32[]{:S(2)}) collective-permute-start(f32[240,384]{1,0:T(8,128)S(1)} %add.28.refs_6_), channel_id=1, source_target_pairs={{0,8},{1,9},{2,10},{3,11},{4,12},{5,13},{6,14},{7,15},{8,16},{9,17... | collective-permute-start | bytes 1105928 | tf_op jit(solution)/shard_map/ppermute | solution.py:233
  75.0 19.4 %collective-permute-start.27 = (f32[240,640]{1,0:T(8,128)S(1)}, f32[240,640]{1,0:T(8,128)S(1)}, u32[]{:S(2)}, u32[]{:S(2)}) collective-permute-start(f32[240,640]{1,0:T(8,128)S(1)} %pad_maximum_fusion.4), channel_id=1, source_target_pairs={{0,2},{4,6},{9,11},{13,15},{18,16},{22,20},{27,25},{31,29}} | collective-permute-start | bytes 1843208 | tf_op jit(solution)/shard_map/ppermute | solution.py:233
  84.2 14.4 %collective-permute-start.24 = (f32[240,640]{1,0:T(8,128)S(1)}, f32[240,640]{1,0:T(8,128)}, u32[]{:S(2)}, u32[]{:S(2)}) collective-permute-start(f32[240,640]{1,0:T(8,128)S(1)} %broadcast_select_fusion.2.held), channel_id=1, source_target_pairs={{0,1},{2,3},{4,5},{6,7},{9,8},{11,10},{13,12},{15,14},{16,17},{18,... | collective-permute-start | bytes 1843208 | tf_op jit(solution)/shard_map/ppermute | solution.py:233
  86.9 7.5 %copy-start.2 = (f32[240,384]{1,0:T(8,128)}, f32[240,384]{1,0:T(8,128)S(1)}, u32[]{:S(2)}) copy-start(f32[240,384]{1,0:T(8,128)S(1)} %collective-permute-done.17.refs_7_) | copy-start | bytes 1105924
  86.9 9.4 %collective-permute-start.26 = (f32[240,384]{1,0:T(8,128)S(1)}, f32[240,384]{1,0:T(8,128)}, u32[]{:S(2)}, u32[]{:S(2)}) collective-permute-start(f32[240,384]{1,0:T(8,128)S(1)} %collective-permute-done.17.refs_7_), channel_id=1, source_target_pairs={{0,8},{1,9},{2,10},{3,11},{4,12},{5,13},{6,14},{7,15},{8,16},{9,17... | collective-permute-start | bytes 1105928 | tf_op jit(solution)/shard_map/ppermute | solution.py:233
  89.0 11.7 %collective-permute-start.20 = (f32[240,640]{1,0:T(8,128)}, f32[240,640]{1,0:T(8,128)}, u32[]{:S(2)}, u32[]{:S(2)}) collective-permute-start(f32[240,640]{1,0:T(8,128)} %broadcast_select_fusion.3.held), channel_id=1, source_target_pairs={{0,1},{2,3},{4,5},{6,7},{9,8},{11,10},{13,12},{15,14},{16,17},{18,... | collective-permute-start | bytes 1843208 | tf_op jit(solution)/shard_map/ppermute | solution.py:233
  92.3 10.0 %collective-permute-start.25 = (f32[240,640]{1,0:T(8,128)S(1)}, f32[240,640]{1,0:T(8,128)}, u32[]{:S(2)}, u32[]{:S(2)}) collective-permute-start(f32[240,640]{1,0:T(8,128)S(1)} %broadcast_select_fusion.1.held), channel_id=1, source_target_pairs={{0,1},{2,3},{4,5},{6,7},{9,8},{11,10},{13,12},{15,14},{16,17},{18,... | collective-permute-start | bytes 1843208 | tf_op jit(solution)/shard_map/ppermute | solution.py:233
  96.4 15.8 %collective-permute-start.29 = (f32[240,640]{1,0:T(8,128)S(1)}, f32[240,640]{1,0:T(8,128)}, u32[]{:S(2)}, u32[]{:S(2)}) collective-permute-start(f32[240,640]{1,0:T(8,128)S(1)} %broadcast_select_fusion.held), channel_id=1, source_target_pairs={{0,1},{2,3},{4,5},{6,7},{9,8},{11,10},{13,12},{15,14},{16,17},{18,... | collective-permute-start | bytes 1843208 | tf_op jit(solution)/shard_map/ppermute | solution.py:233
  98.6 13.6 %collective-permute-start.28 = (f32[240,384]{1,0:T(8,128)}, f32[240,384]{1,0:T(8,128)}, u32[]{:S(2)}, u32[]{:S(2)}) collective-permute-start(f32[240,384]{1,0:T(8,128)} %collective-permute-done.26.refs_8_), channel_id=1, source_target_pairs={{0,8},{1,9},{2,10},{3,11},{4,12},{5,13},{6,14},{7,15},{8,16},{9,17... | collective-permute-start | bytes 1105928 | tf_op jit(solution)/shard_map/ppermute | solution.py:233
  98.6 19.4 %collective-permute-start.31 = (f32[240,256]{1,0:T(8,128)}, f32[240,256]{1,0:T(8,128)S(1)}, u32[]{:S(2)}, u32[]{:S(2)}) collective-permute-start(f32[240,256]{1,0:T(8,128)} %collective-permute-done.22.refs_8_), channel_id=1, source_target_pairs={{0,8},{1,9},{2,10},{3,11},{4,12},{5,13},{6,14},{7,15},{8,16},{9,17... | collective-permute-start | bytes 737288 | tf_op jit(solution)/shard_map/ppermute | solution.py:233
  103.6 1.0 copy-start.3
  115.3 17.0 %collective-permute-start.30 = (f32[320,384]{1,0:T(8,128)S(1)}, f32[320,384]{1,0:T(8,128)S(1)}, u32[]{:S(2)}, u32[]{:S(2)}) collective-permute-start(f32[320,384]{1,0:T(8,128)S(1)} %get-tuple-element.67), channel_id=1, source_target_pairs={{0,4},{1,5},{2,6},{3,7},{4,0},{5,1},{6,2},{7,3},{8,12},{9,13},{10,... | collective-permute-start | bytes 1474568 | tf_op jit(solution)/shard_map/ppermute | solution.py:233
  118.5 13.8 %collective-permute-start.32 = (f32[320,256]{1,0:T(8,128)S(1)}, f32[320,256]{1,0:T(8,128)S(1)}, u32[]{:S(2)}, u32[]{:S(2)}) collective-permute-start(f32[320,256]{1,0:T(8,128)S(1)} %get-tuple-element.69), channel_id=1, source_target_pairs={{0,4},{1,5},{2,6},{3,7},{4,0},{5,1},{6,2},{7,3},{8,12},{9,13},{10,... | collective-permute-start | bytes 983048 | tf_op jit(solution)/shard_map/ppermute | solution.py:233

commit v4 on v3

--- a/solution.py
+++ b/solution.py
@@ -9,16 +9,20 @@
 
 MEMBERS = 2
 CUT = 0.6
-FIRST, NEAR, LAST, SKEW, SPLIT, ORDER = 'a', '', False, False, True, False
-VMEM = 24
-PICK, OFF, DIAG, TURN = 1, 1, 1, 1
-PLAN = {(0, 1): ('k1a', 'y1a'), (1, 1): ('k1b', 'y2b'), (2, 1): ('k1a', 'y1a'), (3, 1): ('k1b', 'y2a'), (3, 2): ('y2b', 'y3a')}
+PLAN = {
+    (0, 1): ("k1a", "y1a"),
+    (1, 1): ("k1b", "y2b"),
+    (2, 1): ("k1a", "y1a"),
+    (3, 1): ("y1a", None),
+    (3, 2): ("y2b", "y3a"),
+}
 BF16 = jnp.bfloat16
 F32 = jnp.float32
 
 
 def split(x):
-    high = x.astype(BF16)
+    limit = float(jnp.finfo(BF16).max)
+    high = jnp.clip(x, -limit, limit).astype(BF16)
     return high, (x - high.astype(F32)).astype(BF16)
 
 
@@ -35,11 +39,11 @@
 
 
 def params():
-    return pltpu.CompilerParams(vmem_limit_bytes=VMEM * 2**20)
-
-
-def cost(scale, flops, moved):
-    return pl.CostEstimate(flops=int(scale * flops), bytes_accessed=int(scale * moved), transcendentals=0)
+    return pltpu.CompilerParams(vmem_limit_bytes=24 * 2**20)
+
+
+def cost(flops, moved):
+    return pl.CostEstimate(flops=flops, bytes_accessed=moved, transcendentals=0)
 
 
 def pick_kernel(rows_ref, member_ref, anc, own_ref, lists_ref, keep_ref, send_ref, picked, sem):
@@ -75,41 +79,64 @@
         ),
         out_shape=(square, square),
         compiler_params=params(),
-        cost_estimate=cost(PICK, 4 * count * count * width, 16 * count * width),
+        cost_estimate=cost(4 * count * count * width, 16 * count * width),
         name="pick_compact",
     )(rows, member, anc, rows[:, None], lists)
 
 
-def off_kernel(count, order_ref, *refs):
-    own, other, blocks, (own_ref, other_ref) = refs[:count], refs[count : 2 * count], refs[2 * count : -2], refs[-2:]
+def pack_kernel(count, order_ref, *refs):
+    own, other, (high_ref, low_ref) = refs[:count], refs[count : 2 * count], refs[2 * count :]
+    for step in range(high_ref.shape[0]):
+        for k in range(count):
+
+            @pl.when(order_ref[step] == k)
+            def _():
+                piece = jnp.concatenate([own[k][...], other[k][...]])
+                high_ref[step], low_ref[step] = split(piece)
+
+
+def pack(order, own, other):
+    count, steps = own[0].shape[0], order.shape[0]
+    out = jax.ShapeDtypeStruct((steps, 2 * count, count), BF16)
+    return pl.pallas_call(
+        functools.partial(pack_kernel, len(own)),
+        grid_spec=pltpu.PrefetchScalarGridSpec(
+            num_scalar_prefetch=1,
+            grid=(1,),
+            in_specs=[whole(count, count)] * (2 * len(own)),
+            out_specs=[whole(*out.shape)] * 2,
+        ),
+        out_shape=(out, out),
+        compiler_params=params(),
+        cost_estimate=cost(0, 16 * count * count * steps),
+        name="pack_pieces",
+    )(order, *own, *other)
+
+
+def off_kernel(high, low, *refs):
+    blocks, (own_ref, other_ref) = refs[:-2], refs[-2:]
     rows = own_ref.shape[0]
     total = None
     for step, block in enumerate(blocks):
-        piece = jnp.concatenate([own[0][...], other[0][...]])
-        for k in range(1, count):
-            piece = jnp.where(order_ref[step] == k, jnp.concatenate([own[k][...], other[k][...]]), piece)
-        term = dot3(split(piece), split(block[...]))
+        term = dot3((high[step], low[step]), split(block[...]))
         total = term if total is None else total + term
     own_ref[...] = -total[:rows]
     other_ref[...] = -total[rows:]
 
 
-def off_parts(order, own, other, blocks):
+def off_parts(pieces, blocks):
     count, width = blocks[0].shape
     out = jax.ShapeDtypeStruct((count, width), F32)
     return pl.pallas_call(
-        functools.partial(off_kernel, len(own)),
-        grid_spec=pltpu.PrefetchScalarGridSpec(
-            num_scalar_prefetch=1,
-            grid=(1,),
-            in_specs=[whole(*x.shape) for x in (*own, *other, *blocks)],
-            out_specs=[whole(count, width)] * 2,
-        ),
+        off_kernel,
+        grid=(1,),
+        in_specs=[whole(*x.shape) for x in (*pieces, *blocks)],
+        out_specs=[whole(count, width)] * 2,
         out_shape=(out, out),
         compiler_params=params(),
-        cost_estimate=cost(OFF, 12 * count * count * width * len(blocks), 8 * count * count * len(blocks)),
+        cost_estimate=cost(12 * count * count * width * len(blocks), 8 * count * count * len(blocks)),
         name="off_parts",
-    )(order, *own, *other, *blocks)
+    )(*pieces, *blocks)
 
 
 def turn_kernel(flag_ref, held, come, high_ref, low_ref):
@@ -130,43 +157,9 @@
         ),
         out_shape=(out, out),
         compiler_params=params(),
-        cost_estimate=cost(TURN, 0, 12 * count * width),
+        cost_estimate=cost(0, 12 * count * width),
         name="turn_strip",
     )(flag, held, come)
-
-
-def diag_kernel(start, member_ref, base_ref, *refs):
-    count = (len(refs) - 3) // 3
-    highs, lows, blocks = refs[:count], refs[count : 2 * count], refs[2 * count : -3]
-    own_ref, other_ref, total = refs[-3:]
-    half, width = own_ref.shape
-    for step in range(count):
-        term = dot3((highs[step][...], lows[step][...]), split(blocks[step][...]))
-        total[...] = term if step == 0 else total[...] + term
-    mine = pl.multiple_of(member_ref[0] * half, 8)
-    own_ref[...] = base_ref[:, start : start + width] - total[pl.ds(mine, half), :]
-    other_ref[...] = total[pl.ds(pl.multiple_of(half - mine, 8), half), :]
-
-
-def diag_parts(member, base, start, strips, blocks):
-    (strip_width, count), width = strips[0][0].shape, blocks[0].shape[1]
-    half = strip_width // MEMBERS
-    flat = [base, *(high for high, _ in strips), *(low for _, low in strips), *blocks]
-    out = jax.ShapeDtypeStruct((half, width), F32)
-    return pl.pallas_call(
-        functools.partial(diag_kernel, start),
-        grid_spec=pltpu.PrefetchScalarGridSpec(
-            num_scalar_prefetch=1,
-            grid=(1,),
-            in_specs=[whole(*x.shape) for x in flat],
-            out_specs=[whole(half, width)] * 2,
-            scratch_shapes=[pltpu.VMEM((strip_width, width), F32)],
-        ),
-        out_shape=(out, out),
-        compiler_params=params(),
-        cost_estimate=cost(DIAG, 6 * count * strip_width * width * len(blocks), 4 * count * strip_width * len(blocks)),
-        name="diag_parts",
-    )(member, *flat)
 
 
 def diag_first_kernel(*refs):
@@ -187,7 +180,7 @@
         out_specs=whole(strip_width, width),
         out_shape=jax.ShapeDtypeStruct((strip_width, width), F32),
         compiler_params=params(),
-        cost_estimate=cost(DIAG, 6 * count * strip_width * width * len(blocks), 4 * count * strip_width * len(blocks)),
+        cost_estimate=cost(6 * count * strip_width * width * len(blocks), 4 * count * strip_width * len(blocks)),
         name="diag_first",
     )(*flat)
 
@@ -215,7 +208,7 @@
         ),
         out_shape=(out, out),
         compiler_params=params(),
-        cost_estimate=cost(DIAG, 6 * count * strip_width * width, 8 * count * strip_width),
+        cost_estimate=cost(6 * count * strip_width * width, 8 * count * strip_width),
         name="diag_last",
     )(member, first, base, *strip, block)
 
@@ -270,8 +263,8 @@
     width = panel.shape[1]
     cut = max(1, round(CUT * width / 128)) * 128
     cuts = [(0, cut), (cut, width)] if cut < width else [(0, width)]
+
     def at(event, value):
-        nonlocal strips
         due = [k for (k, hop), (_, hold) in PLAN.items() if hold == event and k < len(strips) and strips[k].made == hop]
         if due:
             value, *comes = sync(value, *(strips[k].come for k in due))
@@ -283,8 +276,7 @@
                     strips.append(Strip(joined_panel(len(strips))))
                 if hop == 2:
                     strips[k].keep()
-                if event != "begin":
-                    strips[k].block, _ = sync(strips[k].block, value)
+                strips[k].block, _ = sync(strips[k].block, value)
                 strips[k].hop()
         return value
 
@@ -292,27 +284,17 @@
         return jnp.concatenate([part[k] for part in panels], axis=1) if k else panel
 
     strips = []
-    at("begin", None)
     panels = [[panel[:, a:b]] for a, b in cuts]
     for part in panels:
         part.append(onward(part[0]))
     lists = jnp.stack([move(local_rows, lambda z, y, c: (c, y, z)), move(local_rows, lambda z, y, c: (c, 1 - y, z))])
     keep, send = pick(anc_inverse, local_rows, member[None], lists)
-    if FIRST == "a":
-        send, panels[0][1] = sync(send, panels[0][1])
-    elif FIRST == "ab":
-        send, *firsts = sync(send, *(part[1] for part in panels))
-        for part, value in zip(panels, firsts):
-            part[1] = value
-    send = at("pick", send)
+    send, panels[0][1] = sync(send, panels[0][1])
     apart, order = cols // 2, [0, cols // 2]
     own = [keep, move(keep, lambda z, y, c: (z, y, c ^ apart))]
     other = [to_partner(send), move(send, lambda z, y, c: (z, 1 - y, c ^ apart))]
-    for k, part in enumerate(panels):
+    for part in panels:
         part.append(onward(part[1]))
-        if NEAR == "ab"[k]:
-            part[2], own[1], *other = sync(part[2], own[1], *other)
-        part[2] = at("ab"[k] + "2", part[2])
     while apart > 1:
         apart //= 2
         for held in (own, other):
@@ -321,42 +303,27 @@
     wanted = col ^ ((plane - jnp.arange(planes, dtype=jnp.int32)) % planes)
     wanted = sum(jnp.where(wanted == k, i, 0) for i, k in enumerate(order))
     for k, part in enumerate(panels):
+        if k:
+            part[2], panels[0][3] = sync(part[2], panels[0][3])
         while len(part) < planes:
             part.append(onward(part[-1]))
-        part[-1] = at("ab"[k] + "3", part[-1])
-
-    kept, sent = off_parts(wanted, own, other, panels[0])
-    sent = at("k1a", sent)
-    value = kept + to_partner(sent)
-    if LAST and len(panels) > 1:
-        value, panels[1][-1] = sync(value, panels[1][-1])
-    offs = [[at("xa", value)]]
-    offs[0].append(at("y1a", onward(offs[0][0])))
-    for part in panels[1:]:
-        kept, sent = off_parts(wanted, own, other, part)
-        sent = at("k1b", sent)
-        value = kept + to_partner(sent)
-        if SKEW:
-            value, offs[0][1] = sync(value, offs[0][1])
-        offs.append([at("xb", value)])
-        offs[-1].append(at("y1b", onward(offs[-1][0])))
-    for step in range(2, planes):
+
+    pieces = pack(wanted, own, other)
+    offs = []
+    for k, part in enumerate(panels):
+        kept, sent = off_parts(pieces, part)
+        sent = at("k1" + "ab"[k], sent)
+        offs.append([kept + to_partner(sent)])
+    for step in range(1, planes):
         for k, part in enumerate(offs):
             part.append(at(f"y{step}" + "ab"[k], onward(part[-1])))
     while len(strips) < planes:
         strips.append(Strip(joined_panel(len(strips))))
     turned = [strip.finish() for strip in strips]
-    diag, gate = [], None
+    diag = []
     for (start, _), part in zip(cuts, offs):
-        if gate is not None:
-            part[-1], _ = sync(part[-1], gate)
-        if SPLIT:
-            total = diag_first(turned[:-1], part[:-1])
-            kept, sent = diag_last(member[None], total, inv_diag, start, turned[-1], part[-1])
-        else:
-            kept, sent = diag_parts(member[None], inv_diag, start, turned, part)
-        if ORDER:
-            gate = sent
+        total = diag_first(turned[:-1], part[:-1])
+        kept, sent = diag_last(member[None], total, inv_diag, start, turned[-1], part[-1])
         diag.append(kept - to_partner(sent))
     return jnp.concatenate([part[0] for part in offs], axis=1), jnp.concatenate(diag, axis=1)
 

time: 134 us -> 129 us (0.963)
  starting transfers between devices: 41 us -> 50.6 us
  waiting for transfers between devices: 50.9 us -> 42.6 us
  other arithmetic: 9.33 us -> 6.21 us
  Pallas kernels: 23.3 us -> 20.9 us
  local copies, waits for them, and re-layouts: 7.79 us -> 6.15 us
    ppermute x33, starting transfers between devices: 41 us -> 50.6 us  [move(): lax.ppermute(x, axes, [(place(*d), place(*target(*d))) for d in grid if s...]
    ppermute x33, waiting for transfers between devices: 50.9 us -> 42.6 us  [move(): lax.ppermute(x, axes, [(place(*d), place(*target(*d))) for d in grid if s...]
    pallas_call x2 -> x3, Pallas kernels: 6.85 us -> 5.12 us  [the longest x2 2.64 us: off_parts(): pl.pallas_call(off_kernel, grid=(1,), in_specs=[whole(*x.shape) for x in...]
    unnamed x18 -> x12, local copies, waits for them, and re-layouts: 4.94 us -> 3.26 us
  transfers between devices with their start and end apart: 33 -> 33, of which waited for: 10 -> 13; matrix products, arithmetic and copies ran while one was open for 8% -> 6% of each run, Pallas kernels for 18% -> 16%
where the time goes in v4:
time: 129 us; the launch traced here: 127 us
  starting transfers between devices  50.6 us (39%)
  waiting for transfers between devices  42.6 us (33%)
  Pallas kernels  20.9 us (16%)
  other arithmetic  6.21 us (5%)
  local copies, waits for them, and re-layouts  6.15 us (5%)
    ppermute x33, starting transfers between devices, move(): lax.ppermute(x, axes, [(place(*d), place(*target(*d))) for d in grid if s...  50.6 us
    ppermute x33, waiting for transfers between devices, move(): lax.ppermute(x, axes, [(place(*d), place(*target(*d))) for d in grid if s...  42.6 us
    pallas_call x4, Pallas kernels, turn(): pl.pallas_call(turn_kernel, grid_spec=pltpu.PrefetchScalarGridSpec(num_sc...  5.47 us
    pallas_call x1, Pallas kernels, pick(): pl.pallas_call(pick_kernel, grid_spec=pltpu.PrefetchScalarGridSpec(num_sc...  4.26 us
    pallas_call x2, Pallas kernels, diag_first(): pl.pallas_call(diag_first_kernel, grid=(1,), in_specs=[whole(*x.shape) fo...  3.75 us
    select_n x4, other arithmetic, keep(): self.block = jnp.where(self.has(), self.block, self.come)  3.27 us
    unnamed x12, local copies, waits for them, and re-layouts  3.26 us
    pallas_call x2, Pallas kernels, off_parts(): pl.pallas_call(off_kernel, grid=(1,), in_specs=[whole(*x.shape) for x in...  2.64 us
  transfers between devices with their start and end apart: 33, of which 13 were waited for; matrix products, arithmetic and copies ran while one was open for 6% of the time, Pallas kernels for 16%

profile of v4, /device:TPU:0, one launch (start us, length us, event | category | flops | bytes accessed | tf_op | source)
XLA Modules:
  0.0 127.3 jit_solution(15215832330633055490)
XLA Ops:
  0.6 1.1 slice.6.refs_0_
  1.7 3.1 %collective-permute-start.5 = (f32[240,384]{1,0:T(8,128)S(1)}, f32[240,384]{1,0:T(8,128)S(1)}, u32[]{:S(2)}, u32[]{:S(2)}) collective-permute-start(f32[240,384]{1,0:T(8,128)S(1)} %slice.6.refs_0_), channel_id=1, source_target_pairs={{0,8},{1,9},{2,10},{3,11},{4,12},{5,13},{6,14},{7,15},{8,16},{9,17... | collective-permute-start | bytes 1105928 | tf_op jit(solution)/shard_map/ppermute | solution.py:226
  4.8 1.3 %collective-permute-start = (s32[240]{0:T(256)}, s32[240]{0:T(256)S(1)}, u32[]{:S(2)}, u32[]{:S(2)}) collective-permute-start(s32[240]{0:T(256)} %rows_ref.1), channel_id=1, source_target_pairs={{0,0},{1,8},{2,16},{3,24},{4,4},{5,12},{6,20},{7,28},{8,1},{9,9},{... | collective-permute-start | bytes 2888 | tf_op jit(solution)/shard_map/ppermute | solution.py:226
  6.1 1.5 %collective-permute-start.1 = (s32[240]{0:T(256)}, s32[240]{0:T(256)S(1)}, u32[]{:S(2)}, u32[]{:S(2)}) collective-permute-start(s32[240]{0:T(256)} %rows_ref.1), channel_id=1, source_target_pairs={{0,4},{1,12},{2,20},{3,28},{4,0},{5,8},{6,16},{7,24},{8,5},{9,13},... | collective-permute-start | bytes 2888 | tf_op jit(solution)/shard_map/ppermute | solution.py:226
  7.7 0.8 copy.6.own_ref
  8.5 1.4 %collective-permute-done.1 = s32[240]{0:T(256)S(1)} collective-permute-done((s32[240]{0:T(256)}, s32[240]{0:T(256)S(1)}, u32[]{:S(2)}, u32[]{:S(2)}) %collective-permute-start.1) | collective-permute-done | bytes 992 | tf_op jit(solution)/shard_map/ppermute | solution.py:226
  9.9 0.7 copy-done.5
  10.6 4.3 %pick_compact.1 = (f32[240,240]{1,0:T(8,128)S(1)}, f32[240,240]{1,0:T(8,128)S(1)}) custom-call(s32[240]{0:T(256)S(1)} %copy-done.5, s32[1]{0:T(128)} %bitcast.member_ref, f32[2048,4096]{1,0:T(8,128)} %anc.1, s32[240,1]{1,0:T(8,128)S(1)} %copy.6.own_ref, s32[2,240]{1,0:T(2,128)S(1)} %pad_add_fusion.lists_ref), custom_call_target="tpu_custom_call" | custom-call | flops 943718400 | bytes 15728640 | tf_op jit(solution)/shard_map/pick_compact/pallas_call | solution.py:71
  14.9 0.6 collective-permute-done.5.refs_1_
  15.5 4.5 %collective-permute-start.10 = (f32[240,384]{1,0:T(8,128)S(1)}, f32[240,384]{1,0:T(8,128)S(1)}, u32[]{:S(2)}, u32[]{:S(2)}) collective-permute-start(f32[240,384]{1,0:T(8,128)S(1)} %collective-permute-done.5.refs_1_), channel_id=1, source_target_pairs={{0,8},{1,9},{2,10},{3,11},{4,12},{5,13},{6,14},{7,15},{8,16},{9,17... | collective-permute-start | bytes 1105928 | tf_op jit(solution)/shard_map/ppermute | solution.py:226
  20.0 2.5 %collective-permute-start.2 = (f32[240,240]{1,0:T(8,128)S(1)}, f32[240,240]{1,0:T(8,128)}, u32[]{:S(2)}, u32[]{:S(2)}) collective-permute-start(f32[240,240]{1,0:T(8,128)S(1)} %get-tuple-element.38.refs_0_), channel_id=1, source_target_pairs={{0,2},{1,3},{2,0},{3,1},{4,6},{5,7},{6,4},{7,5},{8,10},{9,11},{10,... | collective-permute-start | bytes 691208 | tf_op jit(solution)/shard_map/ppermute | solution.py:226
  22.5 1.0 slice.7.refs_0_
  23.5 1.2 collective-permute-start.11
  24.7 0.6 collective-permute-start.6
  25.2 3.8 %collective-permute-done.2.refs_1_ = f32[240,240]{1,0:T(8,128)} collective-permute-done((f32[240,240]{1,0:T(8,128)S(1)}, f32[240,240]{1,0:T(8,128)}, u32[]{:S(2)}, u32[]{:S(2)}) %collective-permute-start.2) | collective-permute-done | bytes 230432 | tf_op jit(solution)/shard_map/ppermute | solution.py:226
  29.1 2.4 %collective-permute-start.7 = (f32[240,240]{1,0:T(8,128)S(1)}, f32[240,240]{1,0:T(8,128)}, u32[]{:S(2)}, u32[]{:S(2)}) collective-permute-start(f32[240,240]{1,0:T(8,128)S(1)} %get-tuple-element.40), channel_id=1, source_target_pairs={{0,6},{1,7},{2,4},{3,5},{4,2},{5,3},{6,0},{7,1},{8,14},{9,15},{10,... | collective-permute-start | bytes 691208 | tf_op jit(solution)/shard_map/ppermute | solution.py:226
  31.4 0.7 collective-permute-done.10.refs_2_
  32.1 0.5 collective-permute-start.13
  32.6 4.8 %collective-permute-done.11.refs_1_ = f32[240,256]{1,0:T(8,128)S(1)} collective-permute-done((f32[240,256]{1,0:T(8,128)S(1)}, f32[240,256]{1,0:T(8,128)S(1)}, u32[]{:S(2)}, u32[]{:S(2)}) %collective-permute-start.11) | collective-permute-done | bytes 245792 | tf_op jit(solution)/shard_map/ppermute | solution.py:226
  37.4 0.5 collective-permute-start.12
  37.9 0.7 copy-done.3
  38.6 0.5 collective-permute-start.8
  39.2 1.3 collective-permute-done.4.refs_3_
  40.4 0.4 collective-permute-done.8.refs_6_
  40.8 0.4 collective-permute-done.9.refs_7_
  41.1 0.9 copy-done.4
  42.1 2.5 %pack_pieces.1 = (bf16[4,480,240]{2,1,0:T(8,128)(2,1)S(1)}, bf16[4,480,240]{2,1,0:T(8,128)(2,1)S(1)}) custom-call(s32[4]{0:T(128)S(1)} %fusion.2.order_ref, f32[240,240]{1,0:T(8,128)S(1)} %get-tuple-element.38.refs_0_, f32[240,240]{1,0:T(8,128)} %collective-permute-done.2.refs_1_, f32[240,240]{1,0:T(8,128)S(1)} %copy-done.4, ...), custom_call_target="tpu_custom_call" | custom-call | bytes 3686400 | tf_op jit(solution)/shard_map/pack_pieces/pallas_call | solution.py:101
  44.6 5.5 %collective-permute-done.12.refs_2_ = f32[240,256]{1,0:T(8,128)S(1)} collective-permute-done((f32[240,256]{1,0:T(8,128)S(1)}, f32[240,256]{1,0:T(8,128)S(1)}, u32[]{:S(2)}, u32[]{:S(2)}) %collective-permute-start.12) | collective-permute-done | bytes 245792 | tf_op jit(solution)/shard_map/ppermute | solution.py:226
  50.1 1.7 %off_parts.2 = (f32[240,384]{1,0:T(8,128)S(1)}, f32[240,384]{1,0:T(8,128)S(1)}) custom-call(bf16[4,480,240]{2,1,0:T(8,128)(2,1)S(1)} %get-tuple-element.41.high, bf16[4,480,240]{2,1,0:T(8,128)(2,1)S(1)} %get-tuple-element.42.low, f32[240,384]{1,0:T(8,128)S(1)} %slice.6.refs_0_, f32[240,384]{1,0:T(8,128)S(1)} %collective-permute-done.5.refs_1_, ...), custom_call_target="tpu_custom_call" | custom-call | flops 1061683200 | bytes 1843200 | tf_op jit(solution)/shard_map/off_parts/pallas_call | solution.py:130
  51.8 0.7 collective-permute-start.14
  52.5 0.9 pad_maximum_fusion.2
  53.4 6.6 %collective-permute-start.19 = (f32[240,640]{1,0:T(8,128)}, f32[240,640]{1,0:T(8,128)}, u32[]{:S(2)}, u32[]{:S(2)}) collective-permute-start(f32[240,640]{1,0:T(8,128)} %pad_maximum_fusion.2), channel_id=1, source_target_pairs={{0,2},{4,6},{9,11},{13,15},{18,16},{22,20},{27,25},{31,29}} | collective-permute-start | bytes 1843208 | tf_op jit(solution)/shard_map/ppermute | solution.py:226
  60.0 2.1 %collective-permute-start.18 = (f32[240,640]{1,0:T(8,128)}, f32[240,640]{1,0:T(8,128)}, u32[]{:S(2)}, u32[]{:S(2)}) collective-permute-start(f32[240,640]{1,0:T(8,128)} %param.5), channel_id=1, source_target_pairs={{0,2},{4,6},{9,11},{13,15},{18,16},{22,20},{27,25},{31,29}} | collective-permute-start | bytes 1843208 | tf_op jit(solution)/shard_map/ppermute | solution.py:226
  62.2 1.0 off_parts.3
  63.1 0.9 collective-permute-start.16
  64.1 0.3 collective-permute-start.17
  64.4 5.0 %collective-permute-done.16 = f32[240,256]{1,0:T(8,128)S(1)} collective-permute-done((f32[240,256]{1,0:T(8,128)S(1)}, f32[240,256]{1,0:T(8,128)S(1)}, u32[]{:S(2)}, u32[]{:S(2)}) %collective-permute-start.16) | collective-permute-done | bytes 245792 | tf_op jit(solution)/shard_map/ppermute | solution.py:226
  69.5 3.0 %collective-permute-start.23 = (f32[240,640]{1,0:T(8,128)S(1)}, f32[240,640]{1,0:T(8,128)S(1)}, u32[]{:S(2)}, u32[]{:S(2)}) collective-permute-start(f32[240,640]{1,0:T(8,128)S(1)} %pad_maximum_fusion.3), channel_id=1, source_target_pairs={{0,2},{4,6},{9,11},{13,15},{18,16},{22,20},{27,25},{31,29}} | collective-permute-start | bytes 1843208 | tf_op jit(solution)/shard_map/ppermute | solution.py:226
  72.6 6.1 %collective-permute-done.21.refs_7_ = f32[240,256]{1,0:T(8,128)S(1)} collective-permute-done((f32[240,256]{1,0:T(8,128)S(1)}, f32[240,256]{1,0:T(8,128)S(1)}, u32[]{:S(2)}, u32[]{:S(2)}) %collective-permute-start.21) | collective-permute-done | bytes 245792 | tf_op jit(solution)/shard_map/ppermute | solution.py:226
  78.7 0.5 collective-permute-start.26
  79.2 4.2 %collective-permute-start.27 = (f32[240,640]{1,0:T(8,128)S(1)}, f32[240,640]{1,0:T(8,128)S(1)}, u32[]{:S(2)}, u32[]{:S(2)}) collective-permute-start(f32[240,640]{1,0:T(8,128)S(1)} %pad_maximum_fusion.4), channel_id=1, source_target_pairs={{0,2},{4,6},{9,11},{13,15},{18,16},{22,20},{27,25},{31,29}} | collective-permute-start | bytes 1843208 | tf_op jit(solution)/shard_map/ppermute | solution.py:226
  83.4 1.1 broadcast_select_fusion.1.held
  84.6 2.1 %collective-permute-start.25 = (f32[240,640]{1,0:T(8,128)S(1)}, f32[240,640]{1,0:T(8,128)}, u32[]{:S(2)}, u32[]{:S(2)}) collective-permute-start(f32[240,640]{1,0:T(8,128)S(1)} %broadcast_select_fusion.1.held), channel_id=1, source_target_pairs={{0,1},{2,3},{4,5},{6,7},{9,8},{11,10},{13,12},{15,14},{16,17},{18,... | collective-permute-start | bytes 1843208 | tf_op jit(solution)/shard_map/ppermute | solution.py:226
  86.7 1.1 broadcast_select_fusion.3.held
  87.9 2.1 %collective-permute-start.20 = (f32[240,640]{1,0:T(8,128)S(1)}, f32[240,640]{1,0:T(8,128)}, u32[]{:S(2)}, u32[]{:S(2)}) collective-permute-start(f32[240,640]{1,0:T(8,128)S(1)} %broadcast_select_fusion.3.held), channel_id=1, source_target_pairs={{0,1},{2,3},{4,5},{6,7},{9,8},{11,10},{13,12},{15,14},{16,17},{18,... | collective-permute-start | bytes 1843208 | tf_op jit(solution)/shard_map/ppermute | solution.py:226
  90.0 0.9 broadcast_select_fusion.2.held
  90.9 2.1 %collective-permute-start.24 = (f32[240,640]{1,0:T(8,128)}, f32[240,640]{1,0:T(8,128)}, u32[]{:S(2)}, u32[]{:S(2)}) collective-permute-start(f32[240,640]{1,0:T(8,128)} %broadcast_select_fusion.2.held), channel_id=1, source_target_pairs={{0,1},{2,3},{4,5},{6,7},{9,8},{11,10},{13,12},{15,14},{16,17},{18,... | collective-permute-start | bytes 1843208 | tf_op jit(solution)/shard_map/ppermute | solution.py:226
  93.1 2.1 %collective-permute-start.29 = (f32[240,640]{1,0:T(8,128)S(1)}, f32[240,640]{1,0:T(8,128)}, u32[]{:S(2)}, u32[]{:S(2)}) collective-permute-start(f32[240,640]{1,0:T(8,128)S(1)} %broadcast_select_fusion.held), channel_id=1, source_target_pairs={{0,1},{2,3},{4,5},{6,7},{9,8},{11,10},{13,12},{15,14},{16,17},{18,... | collective-permute-start | bytes 1843208 | tf_op jit(solution)/shard_map/ppermute | solution.py:226
  95.3 2.8 %collective-permute-start.31 = (f32[240,256]{1,0:T(8,128)}, f32[240,256]{1,0:T(8,128)S(1)}, u32[]{:S(2)}, u32[]{:S(2)}) collective-permute-start(f32[240,256]{1,0:T(8,128)} %copy-done.1), channel_id=1, source_target_pairs={{0,8},{1,9},{2,10},{3,11},{4,12},{5,13},{6,14},{7,15},{8,16},{9,17... | collective-permute-start | bytes 737288 | tf_op jit(solution)/shard_map/ppermute | solution.py:226
  98.0 1.3 %turn_strip.6 = (bf16[640,240]{1,0:T(8,128)(2,1)S(1)}, bf16[640,240]{1,0:T(8,128)(2,1)S(1)}) custom-call(s32[1]{0:T(128)} %bitcast.4.flag_ref, f32[240,640]{1,0:T(8,128)S(1)} %broadcast_select_fusion.1.held, f32[240,640]{1,0:T(8,128)} %collective-permute-done.25.come), custom_call_target="tpu_custom_call" | custom-call | bytes 1843200 | tf_op jit(solution)/shard_map/turn_strip/pallas_call | solution.py:150
  99.4 1.3 %turn_strip.4 = (bf16[640,240]{1,0:T(8,128)(2,1)S(1)}, bf16[640,240]{1,0:T(8,128)(2,1)S(1)}) custom-call(s32[1]{0:T(128)} %bitcast.4.flag_ref, f32[240,640]{1,0:T(8,128)S(1)} %broadcast_select_fusion.3.held, f32[240,640]{1,0:T(8,128)} %collective-permute-done.20.come), custom_call_target="tpu_custom_call" | custom-call | bytes 1843200 | tf_op jit(solution)/shard_map/turn_strip/pallas_call | solution.py:150
  100.7 1.5 %turn_strip.5 = (bf16[640,240]{1,0:T(8,128)(2,1)S(1)}, bf16[640,240]{1,0:T(8,128)(2,1)S(1)}) custom-call(s32[1]{0:T(128)} %bitcast.4.flag_ref, f32[240,640]{1,0:T(8,128)} %broadcast_select_fusion.2.held, f32[240,640]{1,0:T(8,128)} %collective-permute-done.24.come), custom_call_target="tpu_custom_call" | custom-call | bytes 1843200 | tf_op jit(solution)/shard_map/turn_strip/pallas_call | solution.py:150
  102.2 2.8 %diag_first.2.first = f32[640,384]{1,0:T(8,128)S(1)} custom-call(bf16[640,240]{1,0:T(8,128)(2,1)S(1)} %get-tuple-element.53.refs_0_, bf16[640,240]{1,0:T(8,128)(2,1)S(1)} %get-tuple-element.56.refs_1_, bf16[640,240]{1,0:T(8,128)(2,1)S(1)} %get-tuple-element.58.refs_2_, bf16[640,240]{1,0:T(8,128)(2,1)S(1)} %get-tuple-element.59.refs_3_, ...), custom_call_target="tpu_custom_call" | custom-call | flops 1061683200 | bytes 1843200 | tf_op jit(solution)/shard_map/diag_first/pallas_call | solution.py:176
  105.0 3.0 %collective-permute-done.28.block = f32[240,384]{1,0:T(8,128)} collective-permute-done((f32[240,384]{1,0:T(8,128)}, f32[240,384]{1,0:T(8,128)}, u32[]{:S(2)}, u32[]{:S(2)}) %collective-permute-start.28) | collective-permute-done | bytes 368672 | tf_op jit(solution)/shard_map/ppermute | solution.py:226
  108.0 1.3 %turn_strip.7 = (bf16[640,240]{1,0:T(8,128)(2,1)S(1)}, bf16[640,240]{1,0:T(8,128)(2,1)S(1)}) custom-call(s32[1]{0:T(128)} %bitcast.4.flag_ref, f32[240,640]{1,0:T(8,128)S(1)} %broadcast_select_fusion.held, f32[240,640]{1,0:T(8,128)} %collective-permute-done.29.come), custom_call_target="tpu_custom_call" | custom-call | bytes 1843200 | tf_op jit(solution)/shard_map/turn_strip/pallas_call | solution.py:150
  109.3 1.8 %diag_last.2 = (f32[320,384]{1,0:T(8,128)S(1)}, f32[320,384]{1,0:T(8,128)S(1)}) custom-call(s32[1]{0:T(128)} %bitcast.member_ref, f32[640,384]{1,0:T(8,128)S(1)} %diag_first.2.first, f32[320,640]{1,0:T(8,128)S(1)} %copy-done, bf16[640,240]{1,0:T(8,128)(2,1)S(1)} %get-tuple-element.67.high, bf16[640,240]{1,0:T(8,128)(2,1)S(1)} %get-tuple-element.68.low, ...), custom_call_target="tpu_custom_call" | custom-call | flops 353894400 | bytes 1228800 | tf_op jit(solution)/shard_map/diag_last/pallas_call | solution.py:200
  111.1 0.6 collective-permute-start.30
  111.6 0.9 copy-done.2
  112.6 1.0 diag_first.3.first
  113.6 0.5 diag_last.3
  114.1 1.6 %collective-permute-start.32 = (f32[320,256]{1,0:T(8,128)S(1)}, f32[320,256]{1,0:T(8,128)S(1)}, u32[]{:S(2)}, u32[]{:S(2)}) collective-permute-start(f32[320,256]{1,0:T(8,128)S(1)} %get-tuple-element.73), channel_id=1, source_target_pairs={{0,4},{1,5},{2,6},{3,7},{4,0},{5,1},{6,2},{7,3},{8,12},{9,13},{10,... | collective-permute-start | bytes 983048 | tf_op jit(solution)/shard_map/ppermute | solution.py:226
  115.7 0.9 pad_maximum_fusion.1
  116.5 9.7 %collective-permute-done.32 = f32[320,256]{1,0:T(8,128)S(1)} collective-permute-done((f32[320,256]{1,0:T(8,128)S(1)}, f32[320,256]{1,0:T(8,128)S(1)}, u32[]{:S(2)}, u32[]{:S(2)}) %collective-permute-start.32) | collective-permute-done | bytes 327712 | tf_op jit(solution)/shard_map/ppermute | solution.py:226
  126.3 0.9 pad_maximum_fusion
  (44 shorter events, 0.6 us)
Async XLA Ops:
  0.6 108.7 %copy-start = (f32[320,640]{1,0:T(8,128)S(1)}, f32[320,640]{1,0:T(8,128)}, u32[]{:S(2)}) copy-start(f32[320,640]{1,0:T(8,128)} %base_ref.3) | copy-start | bytes 2457604
  1.7 13.7 %collective-permute-start.5 = (f32[240,384]{1,0:T(8,128)S(1)}, f32[240,384]{1,0:T(8,128)S(1)}, u32[]{:S(2)}, u32[]{:S(2)}) collective-permute-start(f32[240,384]{1,0:T(8,128)S(1)} %slice.6.refs_0_), channel_id=1, source_target_pairs={{0,8},{1,9},{2,10},{3,11},{4,12},{5,13},{6,14},{7,15},{8,16},{9,17... | collective-permute-start | bytes 1105928 | tf_op jit(solution)/shard_map/ppermute | solution.py:226
  4.8 3.7 %collective-permute-start = (s32[240]{0:T(256)}, s32[240]{0:T(256)S(1)}, u32[]{:S(2)}, u32[]{:S(2)}) collective-permute-start(s32[240]{0:T(256)} %rows_ref.1), channel_id=1, source_target_pairs={{0,0},{1,8},{2,16},{3,24},{4,4},{5,12},{6,20},{7,28},{8,1},{9,9},{... | collective-permute-start | bytes 2888 | tf_op jit(solution)/shard_map/ppermute | solution.py:226
  6.1 3.8 %collective-permute-start.1 = (s32[240]{0:T(256)}, s32[240]{0:T(256)S(1)}, u32[]{:S(2)}, u32[]{:S(2)}) collective-permute-start(s32[240]{0:T(256)} %rows_ref.1), channel_id=1, source_target_pairs={{0,4},{1,12},{2,20},{3,28},{4,0},{5,8},{6,16},{7,24},{8,5},{9,13},... | collective-permute-start | bytes 2888 | tf_op jit(solution)/shard_map/ppermute | solution.py:226
  9.9 0.7 copy-start.5
  15.5 16.6 %collective-permute-start.10 = (f32[240,384]{1,0:T(8,128)S(1)}, f32[240,384]{1,0:T(8,128)S(1)}, u32[]{:S(2)}, u32[]{:S(2)}) collective-permute-start(f32[240,384]{1,0:T(8,128)S(1)} %collective-permute-done.5.refs_1_), channel_id=1, source_target_pairs={{0,8},{1,9},{2,10},{3,11},{4,12},{5,13},{6,14},{7,15},{8,16},{9,17... | collective-permute-start | bytes 1105928 | tf_op jit(solution)/shard_map/ppermute | solution.py:226
  20.0 9.1 %collective-permute-start.2 = (f32[240,240]{1,0:T(8,128)S(1)}, f32[240,240]{1,0:T(8,128)}, u32[]{:S(2)}, u32[]{:S(2)}) collective-permute-start(f32[240,240]{1,0:T(8,128)S(1)} %get-tuple-element.38.refs_0_), channel_id=1, source_target_pairs={{0,2},{1,3},{2,0},{3,1},{4,6},{5,7},{6,4},{7,5},{8,10},{9,11},{10,... | collective-permute-start | bytes 691208 | tf_op jit(solution)/shard_map/ppermute | solution.py:226
  23.5 13.9 %collective-permute-start.11 = (f32[240,256]{1,0:T(8,128)S(1)}, f32[240,256]{1,0:T(8,128)S(1)}, u32[]{:S(2)}, u32[]{:S(2)}) collective-permute-start(f32[240,256]{1,0:T(8,128)S(1)} %slice.7.refs_0_), channel_id=1, source_target_pairs={{0,8},{1,9},{2,10},{3,11},{4,12},{5,13},{6,14},{7,15},{8,16},{9,17... | collective-permute-start | bytes 737288 | tf_op jit(solution)/shard_map/ppermute | solution.py:226
  24.7 13.2 %collective-permute-start.3 = (f32[240,240]{1,0:T(8,128)S(1)}, f32[240,240]{1,0:T(8,128)S(1)}, u32[]{:S(2)}, u32[]{:S(2)}) collective-permute-start(f32[240,240]{1,0:T(8,128)S(1)} %get-tuple-element.38.refs_0_), channel_id=1, source_target_pairs={{0,1},{1,0},{2,3},{3,2},{4,5},{5,4},{6,7},{7,6},{8,9},{9,8},{10,11... | collective-permute-start | bytes 691208 | tf_op jit(solution)/shard_map/ppermute | solution.py:226
  24.7 13.9 %collective-permute-start.6 = (f32[240,240]{1,0:T(8,128)S(1)}, f32[240,240]{1,0:T(8,128)}, u32[]{:S(2)}, u32[]{:S(2)}) collective-permute-start(f32[240,240]{1,0:T(8,128)S(1)} %get-tuple-element.40), channel_id=1, source_target_pairs={{0,4},{1,5},{2,6},{3,7},{4,0},{5,1},{6,2},{7,3},{8,12},{9,13},{10,... | collective-permute-start | bytes 691208 | tf_op jit(solution)/shard_map/ppermute | solution.py:226
  29.1 10.0 %collective-permute-start.7 = (f32[240,240]{1,0:T(8,128)S(1)}, f32[240,240]{1,0:T(8,128)}, u32[]{:S(2)}, u32[]{:S(2)}) collective-permute-start(f32[240,240]{1,0:T(8,128)S(1)} %get-tuple-element.40), channel_id=1, source_target_pairs={{0,6},{1,7},{2,4},{3,5},{4,2},{5,3},{6,0},{7,1},{8,14},{9,15},{10,... | collective-permute-start | bytes 691208 | tf_op jit(solution)/shard_map/ppermute | solution.py:226
  32.1 17.9 %collective-permute-start.13 = (f32[240,384]{1,0:T(8,128)S(1)}, f32[240,384]{1,0:T(8,128)S(1)}, u32[]{:S(2)}, u32[]{:S(2)}) collective-permute-start(f32[240,384]{1,0:T(8,128)S(1)} %collective-permute-done.10.refs_2_), channel_id=1, source_target_pairs={{0,8},{1,9},{2,10},{3,11},{4,12},{5,13},{6,14},{7,15},{8,16},{9,17... | collective-permute-start | bytes 1105928 | tf_op jit(solution)/shard_map/ppermute | solution.py:226
  37.4 12.7 %collective-permute-start.12 = (f32[240,256]{1,0:T(8,128)S(1)}, f32[240,256]{1,0:T(8,128)S(1)}, u32[]{:S(2)}, u32[]{:S(2)}) collective-permute-start(f32[240,256]{1,0:T(8,128)S(1)} %collective-permute-done.11.refs_1_), channel_id=1, source_target_pairs={{0,8},{1,9},{2,10},{3,11},{4,12},{5,13},{6,14},{7,15},{8,16},{9,17... | collective-permute-start | bytes 737288 | tf_op jit(solution)/shard_map/ppermute | solution.py:226
  37.9 0.7 copy-start.3
  38.6 1.9 %collective-permute-start.4 = (f32[240,240]{1,0:T(8,128)}, f32[240,240]{1,0:T(8,128)}, u32[]{:S(2)}, u32[]{:S(2)}) collective-permute-start(f32[240,240]{1,0:T(8,128)} %collective-permute-done.2.refs_1_), channel_id=1, source_target_pairs={{0,1},{1,0},{2,3},{3,2},{4,5},{5,4},{6,7},{7,6},{8,9},{9,8},{10,11... | collective-permute-start | bytes 691208 | tf_op jit(solution)/shard_map/ppermute | solution.py:226
  38.6 2.2 %collective-permute-start.8 = (f32[240,240]{1,0:T(8,128)}, f32[240,240]{1,0:T(8,128)}, u32[]{:S(2)}, u32[]{:S(2)}) collective-permute-start(f32[240,240]{1,0:T(8,128)} %collective-permute-done.6.refs_4_), channel_id=1, source_target_pairs={{0,1},{1,0},{2,3},{3,2},{4,5},{5,4},{6,7},{7,6},{8,9},{9,8},{10,11... | collective-permute-start | bytes 691208 | tf_op jit(solution)/shard_map/ppermute | solution.py:226
  39.1 2.0 %collective-permute-start.9 = (f32[240,240]{1,0:T(8,128)}, f32[240,240]{1,0:T(8,128)}, u32[]{:S(2)}, u32[]{:S(2)}) collective-permute-start(f32[240,240]{1,0:T(8,128)} %collective-permute-done.7.refs_5_), channel_id=1, source_target_pairs={{0,1},{1,0},{2,3},{3,2},{4,5},{5,4},{6,7},{7,6},{8,9},{9,8},{10,11... | collective-permute-start | bytes 691208 | tf_op jit(solution)/shard_map/ppermute | solution.py:226
  41.1 0.9 copy-start.4
  50.0 12.1 %collective-permute-start.15 = (f32[240,256]{1,0:T(8,128)S(1)}, f32[240,256]{1,0:T(8,128)S(1)}, u32[]{:S(2)}, u32[]{:S(2)}) collective-permute-start(f32[240,256]{1,0:T(8,128)S(1)} %collective-permute-done.12.refs_2_), channel_id=1, source_target_pairs={{0,8},{1,9},{2,10},{3,11},{4,12},{5,13},{6,14},{7,15},{8,16},{9,17... | collective-permute-start | bytes 737288 | tf_op jit(solution)/shard_map/ppermute | solution.py:226
  51.8 12.2 %collective-permute-start.14 = (f32[240,384]{1,0:T(8,128)S(1)}, f32[240,384]{1,0:T(8,128)S(1)}, u32[]{:S(2)}, u32[]{:S(2)}) collective-permute-start(f32[240,384]{1,0:T(8,128)S(1)} %get-tuple-element.46), channel_id=1, source_target_pairs={{0,4},{1,5},{2,6},{3,7},{4,0},{5,1},{6,2},{7,3},{8,12},{9,13},{10,... | collective-permute-start | bytes 1105928 | tf_op jit(solution)/shard_map/ppermute | solution.py:226
  53.4 25.3 %collective-permute-start.19 = (f32[240,640]{1,0:T(8,128)}, f32[240,640]{1,0:T(8,128)}, u32[]{:S(2)}, u32[]{:S(2)}) collective-permute-start(f32[240,640]{1,0:T(8,128)} %pad_maximum_fusion.2), channel_id=1, source_target_pairs={{0,2},{4,6},{9,11},{13,15},{18,16},{22,20},{27,25},{31,29}} | collective-permute-start | bytes 1843208 | tf_op jit(solution)/shard_map/ppermute | solution.py:226
  60.0 18.7 %collective-permute-start.18 = (f32[240,640]{1,0:T(8,128)}, f32[240,640]{1,0:T(8,128)}, u32[]{:S(2)}, u32[]{:S(2)}) collective-permute-start(f32[240,640]{1,0:T(8,128)} %param.5), channel_id=1, source_target_pairs={{0,2},{4,6},{9,11},{13,15},{18,16},{22,20},{27,25},{31,29}} | collective-permute-start | bytes 1843208 | tf_op jit(solution)/shard_map/ppermute | solution.py:226
  63.1 6.3 %collective-permute-start.16 = (f32[240,256]{1,0:T(8,128)S(1)}, f32[240,256]{1,0:T(8,128)S(1)}, u32[]{:S(2)}, u32[]{:S(2)}) collective-permute-start(f32[240,256]{1,0:T(8,128)S(1)} %get-tuple-element.49), channel_id=1, source_target_pairs={{0,4},{1,5},{2,6},{3,7},{4,0},{5,1},{6,2},{7,3},{8,12},{9,13},{10,... | collective-permute-start | bytes 737288 | tf_op jit(solution)/shard_map/ppermute | solution.py:226
  64.1 14.6 %collective-permute-start.17 = (f32[240,384]{1,0:T(8,128)S(1)}, f32[240,384]{1,0:T(8,128)}, u32[]{:S(2)}, u32[]{:S(2)}) collective-permute-start(f32[240,384]{1,0:T(8,128)S(1)} %add.28.refs_6_), channel_id=1, source_target_pairs={{0,8},{1,9},{2,10},{3,11},{4,12},{5,13},{6,14},{7,15},{8,16},{9,17... | collective-permute-start | bytes 1105928 | tf_op jit(solution)/shard_map/ppermute | solution.py:226
  69.4 9.3 %collective-permute-start.21 = (f32[240,256]{1,0:T(8,128)S(1)}, f32[240,256]{1,0:T(8,128)S(1)}, u32[]{:S(2)}, u32[]{:S(2)}) collective-permute-start(f32[240,256]{1,0:T(8,128)S(1)} %add.29.refs_6_), channel_id=1, source_target_pairs={{0,8},{1,9},{2,10},{3,11},{4,12},{5,13},{6,14},{7,15},{8,16},{9,17... | collective-permute-start | bytes 737288 | tf_op jit(solution)/shard_map/ppermute | solution.py:226
  69.5 18.3 %collective-permute-start.23 = (f32[240,640]{1,0:T(8,128)S(1)}, f32[240,640]{1,0:T(8,128)S(1)}, u32[]{:S(2)}, u32[]{:S(2)}) collective-permute-start(f32[240,640]{1,0:T(8,128)S(1)} %pad_maximum_fusion.3), channel_id=1, source_target_pairs={{0,2},{4,6},{9,11},{13,15},{18,16},{22,20},{27,25},{31,29}} | collective-permute-start | bytes 1843208 | tf_op jit(solution)/shard_map/ppermute | solution.py:226
  78.7 11.3 %collective-permute-start.22 = (f32[240,256]{1,0:T(8,128)S(1)}, f32[240,256]{1,0:T(8,128)S(1)}, u32[]{:S(2)}, u32[]{:S(2)}) collective-permute-start(f32[240,256]{1,0:T(8,128)S(1)} %collective-permute-done.21.refs_7_), channel_id=1, source_target_pairs={{0,8},{1,9},{2,10},{3,11},{4,12},{5,13},{6,14},{7,15},{8,16},{9,17... | collective-permute-start | bytes 737288 | tf_op jit(solution)/shard_map/ppermute | solution.py:226
  78.7 16.5 %collective-permute-start.26 = (f32[240,384]{1,0:T(8,128)}, f32[240,384]{1,0:T(8,128)}, u32[]{:S(2)}, u32[]{:S(2)}) collective-permute-start(f32[240,384]{1,0:T(8,128)} %collective-permute-done.17.refs_7_), channel_id=1, source_target_pairs={{0,8},{1,9},{2,10},{3,11},{4,12},{5,13},{6,14},{7,15},{8,16},{9,17... | collective-permute-start | bytes 1105928 | tf_op jit(solution)/shard_map/ppermute | solution.py:226
  79.2 13.8 %collective-permute-start.27 = (f32[240,640]{1,0:T(8,128)S(1)}, f32[240,640]{1,0:T(8,128)S(1)}, u32[]{:S(2)}, u32[]{:S(2)}) collective-permute-start(f32[240,640]{1,0:T(8,128)S(1)} %pad_maximum_fusion.4), channel_id=1, source_target_pairs={{0,2},{4,6},{9,11},{13,15},{18,16},{22,20},{27,25},{31,29}} | collective-permute-start | bytes 1843208 | tf_op jit(solution)/shard_map/ppermute | solution.py:226
  84.6 10.7 %collective-permute-start.25 = (f32[240,640]{1,0:T(8,128)S(1)}, f32[240,640]{1,0:T(8,128)}, u32[]{:S(2)}, u32[]{:S(2)}) collective-permute-start(f32[240,640]{1,0:T(8,128)S(1)} %broadcast_select_fusion.1.held), channel_id=1, source_target_pairs={{0,1},{2,3},{4,5},{6,7},{9,8},{11,10},{13,12},{15,14},{16,17},{18,... | collective-permute-start | bytes 1843208 | tf_op jit(solution)/shard_map/ppermute | solution.py:226
  87.9 11.5 %collective-permute-start.20 = (f32[240,640]{1,0:T(8,128)S(1)}, f32[240,640]{1,0:T(8,128)}, u32[]{:S(2)}, u32[]{:S(2)}) collective-permute-start(f32[240,640]{1,0:T(8,128)S(1)} %broadcast_select_fusion.3.held), channel_id=1, source_target_pairs={{0,1},{2,3},{4,5},{6,7},{9,8},{11,10},{13,12},{15,14},{16,17},{18,... | collective-permute-start | bytes 1843208 | tf_op jit(solution)/shard_map/ppermute | solution.py:226
  90.0 3.0 %copy-start.1 = (f32[240,256]{1,0:T(8,128)}, f32[240,256]{1,0:T(8,128)S(1)}, u32[]{:S(2)}) copy-start(f32[240,256]{1,0:T(8,128)S(1)} %collective-permute-done.22.refs_8_) | copy-start | bytes 737284
  90.9 9.8 %collective-permute-start.24 = (f32[240,640]{1,0:T(8,128)}, f32[240,640]{1,0:T(8,128)}, u32[]{:S(2)}, u32[]{:S(2)}) collective-permute-start(f32[240,640]{1,0:T(8,128)} %broadcast_select_fusion.2.held), channel_id=1, source_target_pairs={{0,1},{2,3},{4,5},{6,7},{9,8},{11,10},{13,12},{15,14},{16,17},{18,... | collective-permute-start | bytes 1843208 | tf_op jit(solution)/shard_map/ppermute | solution.py:226
  93.1 14.9 %collective-permute-start.29 = (f32[240,640]{1,0:T(8,128)S(1)}, f32[240,640]{1,0:T(8,128)}, u32[]{:S(2)}, u32[]{:S(2)}) collective-permute-start(f32[240,640]{1,0:T(8,128)S(1)} %broadcast_select_fusion.held), channel_id=1, source_target_pairs={{0,1},{2,3},{4,5},{6,7},{9,8},{11,10},{13,12},{15,14},{16,17},{18,... | collective-permute-start | bytes 1843208 | tf_op jit(solution)/shard_map/ppermute | solution.py:226
  95.2 12.7 %collective-permute-start.28 = (f32[240,384]{1,0:T(8,128)}, f32[240,384]{1,0:T(8,128)}, u32[]{:S(2)}, u32[]{:S(2)}) collective-permute-start(f32[240,384]{1,0:T(8,128)} %collective-permute-done.26.refs_8_), channel_id=1, source_target_pairs={{0,8},{1,9},{2,10},{3,11},{4,12},{5,13},{6,14},{7,15},{8,16},{9,17... | collective-permute-start | bytes 1105928 | tf_op jit(solution)/shard_map/ppermute | solution.py:226
  95.3 18.3 %collective-permute-start.31 = (f32[240,256]{1,0:T(8,128)}, f32[240,256]{1,0:T(8,128)S(1)}, u32[]{:S(2)}, u32[]{:S(2)}) collective-permute-start(f32[240,256]{1,0:T(8,128)} %copy-done.1), channel_id=1, source_target_pairs={{0,8},{1,9},{2,10},{3,11},{4,12},{5,13},{6,14},{7,15},{8,16},{9,17... | collective-permute-start | bytes 737288 | tf_op jit(solution)/shard_map/ppermute | solution.py:226
  111.1 15.2 %collective-permute-start.30 = (f32[320,384]{1,0:T(8,128)S(1)}, f32[320,384]{1,0:T(8,128)S(1)}, u32[]{:S(2)}, u32[]{:S(2)}) collective-permute-start(f32[320,384]{1,0:T(8,128)S(1)} %get-tuple-element.71), channel_id=1, source_target_pairs={{0,4},{1,5},{2,6},{3,7},{4,0},{5,1},{6,2},{7,3},{8,12},{9,13},{10,... | collective-permute-start | bytes 1474568 | tf_op jit(solution)/shard_map/ppermute | solution.py:226
  111.6 0.9 copy-start.2
  114.1 12.1 %collective-permute-start.32 = (f32[320,256]{1,0:T(8,128)S(1)}, f32[320,256]{1,0:T(8,128)S(1)}, u32[]{:S(2)}, u32[]{:S(2)}) collective-permute-start(f32[320,256]{1,0:T(8,128)S(1)} %get-tuple-element.73), channel_id=1, source_target_pairs={{0,4},{1,5},{2,6},{3,7},{4,0},{5,1},{6,2},{7,3},{8,12},{9,13},{10,... | collective-permute-start | bytes 983048 | tf_op jit(solution)/shard_map/ppermute | solution.py:226

commit v5 on v4

--- a/solution.py
+++ b/solution.py
@@ -180,7 +180,7 @@
         out_specs=whole(strip_width, width),
         out_shape=jax.ShapeDtypeStruct((strip_width, width), F32),
         compiler_params=params(),
-        cost_estimate=cost(6 * count * strip_width * width * len(blocks), 4 * count * strip_width * len(blocks)),
+        cost_estimate=cost(6 * count * strip_width * width * len(blocks) // 10, 4 * count * strip_width * len(blocks) // 10),
         name="diag_first",
     )(*flat)
 
@@ -208,7 +208,7 @@
         ),
         out_shape=(out, out),
         compiler_params=params(),
-        cost_estimate=cost(6 * count * strip_width * width, 8 * count * strip_width),
+        cost_estimate=cost(6 * count * strip_width * width // 10, 8 * count * strip_width // 10),
         name="diag_last",
     )(member, first, base, *strip, block)
 

time: 129 us -> 127 us (0.984)
  waiting for transfers between devices: 42.6 us -> 40 us
    ppermute x33, waiting for transfers between devices: 42.6 us -> 40 us  [move(): lax.ppermute(x, axes, [(place(*d), place(*target(*d))) for d in grid if s...]
  transfers between devices with their start and end apart: 33 -> 33, of which waited for: 13 -> 13; matrix products, arithmetic and copies ran while one was open for 6% -> 6% of each run, Pallas kernels for 16% -> 17%
where the time goes in v5:
time: 127 us; the launch traced here: 126 us
  starting transfers between devices  50.6 us (40%)
  waiting for transfers between devices  40 us (31%)
  Pallas kernels  21.7 us (17%)
  local copies, waits for them, and re-layouts  7.09 us (6%)
  other arithmetic  6.22 us (5%)
    ppermute x33, starting transfers between devices, move(): lax.ppermute(x, axes, [(place(*d), place(*target(*d))) for d in grid if s...  50.6 us
    ppermute x33, waiting for transfers between devices, move(): lax.ppermute(x, axes, [(place(*d), place(*target(*d))) for d in grid if s...  40 us
    pallas_call x2, Pallas kernels, diag_first(): pl.pallas_call(diag_first_kernel, grid=(1,), in_specs=[whole(*x.shape) fo...  4.68 us
    pallas_call x4, Pallas kernels, turn(): pl.pallas_call(turn_kernel, grid_spec=pltpu.PrefetchScalarGridSpec(num_sc...  4.4 us
    pallas_call x1, Pallas kernels, pick(): pl.pallas_call(pick_kernel, grid_spec=pltpu.PrefetchScalarGridSpec(num_sc...  4.26 us
    unnamed x12, local copies, waits for them, and re-layouts  4.21 us
    select_n x4, other arithmetic, keep(): self.block = jnp.where(self.has(), self.block, self.come)  3.28 us
    pallas_call x2, Pallas kernels, diag_last(): pl.pallas_call(functools.partial(diag_last_kernel, start), grid_spec=pltp...  3.2 us
  transfers between devices with their start and end apart: 33, of which 13 were waited for; matrix products, arithmetic and copies ran while one was open for 6% of the time, Pallas kernels for 17%

profile of v5, /device:TPU:0, one launch (start us, length us, event | category | flops | bytes accessed | tf_op | source)
XLA Modules:
  0.0 126.5 jit_solution(15134009624834304866)
XLA Ops:
  0.6 1.1 slice.6.refs_0_
  1.7 3.1 %collective-permute-start.5 = (f32[240,384]{1,0:T(8,128)S(1)}, f32[240,384]{1,0:T(8,128)S(1)}, u32[]{:S(2)}, u32[]{:S(2)}) collective-permute-start(f32[240,384]{1,0:T(8,128)S(1)} %slice.6.refs_0_), channel_id=1, source_target_pairs={{0,8},{1,9},{2,10},{3,11},{4,12},{5,13},{6,14},{7,15},{8,16},{9,17... | collective-permute-start | bytes 1105928 | tf_op jit(solution)/shard_map/ppermute | solution.py:226
  4.8 1.3 %collective-permute-start = (s32[240]{0:T(256)}, s32[240]{0:T(256)S(1)}, u32[]{:S(2)}, u32[]{:S(2)}) collective-permute-start(s32[240]{0:T(256)} %rows_ref.1), channel_id=1, source_target_pairs={{0,0},{1,8},{2,16},{3,24},{4,4},{5,12},{6,20},{7,28},{8,1},{9,9},{... | collective-permute-start | bytes 2888 | tf_op jit(solution)/shard_map/ppermute | solution.py:226
  6.1 1.5 %collective-permute-start.1 = (s32[240]{0:T(256)}, s32[240]{0:T(256)S(1)}, u32[]{:S(2)}, u32[]{:S(2)}) collective-permute-start(s32[240]{0:T(256)} %rows_ref.1), channel_id=1, source_target_pairs={{0,4},{1,12},{2,20},{3,28},{4,0},{5,8},{6,16},{7,24},{8,5},{9,13},... | collective-permute-start | bytes 2888 | tf_op jit(solution)/shard_map/ppermute | solution.py:226
  7.7 0.8 copy.6.own_ref
  8.5 1.4 %collective-permute-done.1 = s32[240]{0:T(256)S(1)} collective-permute-done((s32[240]{0:T(256)}, s32[240]{0:T(256)S(1)}, u32[]{:S(2)}, u32[]{:S(2)}) %collective-permute-start.1) | collective-permute-done | bytes 992 | tf_op jit(solution)/shard_map/ppermute | solution.py:226
  9.9 0.7 copy-done.5
  10.6 4.3 %pick_compact.1 = (f32[240,240]{1,0:T(8,128)S(1)}, f32[240,240]{1,0:T(8,128)S(1)}) custom-call(s32[240]{0:T(256)S(1)} %copy-done.5, s32[1]{0:T(128)} %bitcast.member_ref, f32[2048,4096]{1,0:T(8,128)} %anc.1, s32[240,1]{1,0:T(8,128)S(1)} %copy.6.own_ref, s32[2,240]{1,0:T(2,128)S(1)} %pad_add_fusion.lists_ref), custom_call_target="tpu_custom_call" | custom-call | flops 943718400 | bytes 15728640 | tf_op jit(solution)/shard_map/pick_compact/pallas_call | solution.py:71
  14.9 0.6 collective-permute-done.5.refs_1_
  15.5 4.5 %collective-permute-start.10 = (f32[240,384]{1,0:T(8,128)S(1)}, f32[240,384]{1,0:T(8,128)S(1)}, u32[]{:S(2)}, u32[]{:S(2)}) collective-permute-start(f32[240,384]{1,0:T(8,128)S(1)} %collective-permute-done.5.refs_1_), channel_id=1, source_target_pairs={{0,8},{1,9},{2,10},{3,11},{4,12},{5,13},{6,14},{7,15},{8,16},{9,17... | collective-permute-start | bytes 1105928 | tf_op jit(solution)/shard_map/ppermute | solution.py:226
  20.0 2.5 %collective-permute-start.2 = (f32[240,240]{1,0:T(8,128)S(1)}, f32[240,240]{1,0:T(8,128)}, u32[]{:S(2)}, u32[]{:S(2)}) collective-permute-start(f32[240,240]{1,0:T(8,128)S(1)} %get-tuple-element.38.refs_0_), channel_id=1, source_target_pairs={{0,2},{1,3},{2,0},{3,1},{4,6},{5,7},{6,4},{7,5},{8,10},{9,11},{10,... | collective-permute-start | bytes 691208 | tf_op jit(solution)/shard_map/ppermute | solution.py:226
  22.5 1.0 slice.7.refs_0_
  23.5 1.2 collective-permute-start.11
  24.7 0.6 collective-permute-start.6
  25.2 3.8 %collective-permute-done.2.refs_1_ = f32[240,240]{1,0:T(8,128)} collective-permute-done((f32[240,240]{1,0:T(8,128)S(1)}, f32[240,240]{1,0:T(8,128)}, u32[]{:S(2)}, u32[]{:S(2)}) %collective-permute-start.2) | collective-permute-done | bytes 230432 | tf_op jit(solution)/shard_map/ppermute | solution.py:226
  29.1 2.4 %collective-permute-start.7 = (f32[240,240]{1,0:T(8,128)S(1)}, f32[240,240]{1,0:T(8,128)}, u32[]{:S(2)}, u32[]{:S(2)}) collective-permute-start(f32[240,240]{1,0:T(8,128)S(1)} %get-tuple-element.40), channel_id=1, source_target_pairs={{0,6},{1,7},{2,4},{3,5},{4,2},{5,3},{6,0},{7,1},{8,14},{9,15},{10,... | collective-permute-start | bytes 691208 | tf_op jit(solution)/shard_map/ppermute | solution.py:226
  31.4 0.7 collective-permute-done.10.refs_2_
  32.1 0.5 collective-permute-start.13
  32.6 4.8 %collective-permute-done.11.refs_1_ = f32[240,256]{1,0:T(8,128)S(1)} collective-permute-done((f32[240,256]{1,0:T(8,128)S(1)}, f32[240,256]{1,0:T(8,128)S(1)}, u32[]{:S(2)}, u32[]{:S(2)}) %collective-permute-start.11) | collective-permute-done | bytes 245792 | tf_op jit(solution)/shard_map/ppermute | solution.py:226
  37.4 0.5 collective-permute-start.12
  37.9 0.7 copy-done.3
  38.6 0.5 collective-permute-start.8
  39.2 1.3 collective-permute-done.4.refs_3_
  40.4 0.4 collective-permute-done.8.refs_6_
  40.8 0.4 collective-permute-done.9.refs_7_
  41.1 0.9 copy-done.4
  42.1 2.5 %pack_pieces.1 = (bf16[4,480,240]{2,1,0:T(8,128)(2,1)S(1)}, bf16[4,480,240]{2,1,0:T(8,128)(2,1)S(1)}) custom-call(s32[4]{0:T(128)S(1)} %fusion.2.order_ref, f32[240,240]{1,0:T(8,128)S(1)} %get-tuple-element.38.refs_0_, f32[240,240]{1,0:T(8,128)} %collective-permute-done.2.refs_1_, f32[240,240]{1,0:T(8,128)S(1)} %copy-done.4, ...), custom_call_target="tpu_custom_call" | custom-call | bytes 3686400 | tf_op jit(solution)/shard_map/pack_pieces/pallas_call | solution.py:101
  44.6 5.5 %collective-permute-done.12.refs_2_ = f32[240,256]{1,0:T(8,128)S(1)} collective-permute-done((f32[240,256]{1,0:T(8,128)S(1)}, f32[240,256]{1,0:T(8,128)S(1)}, u32[]{:S(2)}, u32[]{:S(2)}) %collective-permute-start.12) | collective-permute-done | bytes 245792 | tf_op jit(solution)/shard_map/ppermute | solution.py:226
  50.1 1.7 %off_parts.2 = (f32[240,384]{1,0:T(8,128)S(1)}, f32[240,384]{1,0:T(8,128)S(1)}) custom-call(bf16[4,480,240]{2,1,0:T(8,128)(2,1)S(1)} %get-tuple-element.41.high, bf16[4,480,240]{2,1,0:T(8,128)(2,1)S(1)} %get-tuple-element.42.low, f32[240,384]{1,0:T(8,128)S(1)} %slice.6.refs_0_, f32[240,384]{1,0:T(8,128)S(1)} %collective-permute-done.5.refs_1_, ...), custom_call_target="tpu_custom_call" | custom-call | flops 1061683200 | bytes 1843200 | tf_op jit(solution)/shard_map/off_parts/pallas_call | solution.py:130
  51.8 0.7 collective-permute-start.14
  52.5 0.9 pad_maximum_fusion.2
  53.4 6.6 %collective-permute-start.19 = (f32[240,640]{1,0:T(8,128)}, f32[240,640]{1,0:T(8,128)}, u32[]{:S(2)}, u32[]{:S(2)}) collective-permute-start(f32[240,640]{1,0:T(8,128)} %pad_maximum_fusion.2), channel_id=1, source_target_pairs={{0,2},{4,6},{9,11},{13,15},{18,16},{22,20},{27,25},{31,29}} | collective-permute-start | bytes 1843208 | tf_op jit(solution)/shard_map/ppermute | solution.py:226
  60.0 2.1 %collective-permute-start.18 = (f32[240,640]{1,0:T(8,128)}, f32[240,640]{1,0:T(8,128)}, u32[]{:S(2)}, u32[]{:S(2)}) collective-permute-start(f32[240,640]{1,0:T(8,128)} %param.5), channel_id=1, source_target_pairs={{0,2},{4,6},{9,11},{13,15},{18,16},{22,20},{27,25},{31,29}} | collective-permute-start | bytes 1843208 | tf_op jit(solution)/shard_map/ppermute | solution.py:226
  62.2 1.0 off_parts.3
  63.1 0.9 collective-permute-start.16
  64.1 0.3 collective-permute-start.17
  64.4 5.0 %collective-permute-done.16 = f32[240,256]{1,0:T(8,128)S(1)} collective-permute-done((f32[240,256]{1,0:T(8,128)S(1)}, f32[240,256]{1,0:T(8,128)S(1)}, u32[]{:S(2)}, u32[]{:S(2)}) %collective-permute-start.16) | collective-permute-done | bytes 245792 | tf_op jit(solution)/shard_map/ppermute | solution.py:226
  69.5 3.0 %collective-permute-start.23 = (f32[240,640]{1,0:T(8,128)S(1)}, f32[240,640]{1,0:T(8,128)S(1)}, u32[]{:S(2)}, u32[]{:S(2)}) collective-permute-start(f32[240,640]{1,0:T(8,128)S(1)} %pad_maximum_fusion.3), channel_id=1, source_target_pairs={{0,2},{4,6},{9,11},{13,15},{18,16},{22,20},{27,25},{31,29}} | collective-permute-start | bytes 1843208 | tf_op jit(solution)/shard_map/ppermute | solution.py:226
  72.6 6.1 %collective-permute-done.21.refs_7_ = f32[240,256]{1,0:T(8,128)S(1)} collective-permute-done((f32[240,256]{1,0:T(8,128)S(1)}, f32[240,256]{1,0:T(8,128)S(1)}, u32[]{:S(2)}, u32[]{:S(2)}) %collective-permute-start.21) | collective-permute-done | bytes 245792 | tf_op jit(solution)/shard_map/ppermute | solution.py:226
  78.7 0.5 collective-permute-start.26
  79.2 4.2 %collective-permute-start.27 = (f32[240,640]{1,0:T(8,128)S(1)}, f32[240,640]{1,0:T(8,128)S(1)}, u32[]{:S(2)}, u32[]{:S(2)}) collective-permute-start(f32[240,640]{1,0:T(8,128)S(1)} %pad_maximum_fusion.4), channel_id=1, source_target_pairs={{0,2},{4,6},{9,11},{13,15},{18,16},{22,20},{27,25},{31,29}} | collective-permute-start | bytes 1843208 | tf_op jit(solution)/shard_map/ppermute | solution.py:226
  83.4 1.1 broadcast_select_fusion.1.held
  84.6 1.3 %collective-permute-start.25 = (f32[240,640]{1,0:T(8,128)S(1)}, f32[240,640]{1,0:T(8,128)S(1)}, u32[]{:S(2)}, u32[]{:S(2)}) collective-permute-start(f32[240,640]{1,0:T(8,128)S(1)} %broadcast_select_fusion.1.held), channel_id=1, source_target_pairs={{0,1},{2,3},{4,5},{6,7},{9,8},{11,10},{13,12},{15,14},{16,17},{18,... | collective-permute-start | bytes 1843208 | tf_op jit(solution)/shard_map/ppermute | solution.py:226
  85.9 1.1 broadcast_select_fusion.3.held
  87.1 2.1 %collective-permute-start.20 = (f32[240,640]{1,0:T(8,128)S(1)}, f32[240,640]{1,0:T(8,128)}, u32[]{:S(2)}, u32[]{:S(2)}) collective-permute-start(f32[240,640]{1,0:T(8,128)S(1)} %broadcast_select_fusion.3.held), channel_id=1, source_target_pairs={{0,1},{2,3},{4,5},{6,7},{9,8},{11,10},{13,12},{15,14},{16,17},{18,... | collective-permute-start | bytes 1843208 | tf_op jit(solution)/shard_map/ppermute | solution.py:226
  89.2 0.9 broadcast_select_fusion.2.held
  90.1 2.1 %collective-permute-start.24 = (f32[240,640]{1,0:T(8,128)}, f32[240,640]{1,0:T(8,128)}, u32[]{:S(2)}, u32[]{:S(2)}) collective-permute-start(f32[240,640]{1,0:T(8,128)} %broadcast_select_fusion.2.held), channel_id=1, source_target_pairs={{0,1},{2,3},{4,5},{6,7},{9,8},{11,10},{13,12},{15,14},{16,17},{18,... | collective-permute-start | bytes 1843208 | tf_op jit(solution)/shard_map/ppermute | solution.py:226
  92.3 2.1 %collective-permute-start.29 = (f32[240,640]{1,0:T(8,128)S(1)}, f32[240,640]{1,0:T(8,128)}, u32[]{:S(2)}, u32[]{:S(2)}) collective-permute-start(f32[240,640]{1,0:T(8,128)S(1)} %broadcast_select_fusion.held), channel_id=1, source_target_pairs={{0,1},{2,3},{4,5},{6,7},{9,8},{11,10},{13,12},{15,14},{16,17},{18,... | collective-permute-start | bytes 1843208 | tf_op jit(solution)/shard_map/ppermute | solution.py:226
  94.5 0.8 copy-done.1
  95.3 3.5 %collective-permute-start.31 = (f32[240,256]{1,0:T(8,128)}, f32[240,256]{1,0:T(8,128)}, u32[]{:S(2)}, u32[]{:S(2)}) collective-permute-start(f32[240,256]{1,0:T(8,128)} %collective-permute-done.22.refs_8_), channel_id=1, source_target_pairs={{0,8},{1,9},{2,10},{3,11},{4,12},{5,13},{6,14},{7,15},{8,16},{9,17... | collective-permute-start | bytes 737288 | tf_op jit(solution)/shard_map/ppermute | solution.py:226
  98.8 1.1 copy-done.2
  100.2 1.3 %turn_strip.4 = (bf16[640,240]{1,0:T(8,128)(2,1)S(1)}, bf16[640,240]{1,0:T(8,128)(2,1)S(1)}) custom-call(s32[1]{0:T(128)} %bitcast.4.flag_ref, f32[240,640]{1,0:T(8,128)S(1)} %broadcast_select_fusion.3.held, f32[240,640]{1,0:T(8,128)} %collective-permute-done.20.come), custom_call_target="tpu_custom_call" | custom-call | bytes 1843200 | tf_op jit(solution)/shard_map/turn_strip/pallas_call | solution.py:150
  101.5 1.5 %turn_strip.5 = (bf16[640,240]{1,0:T(8,128)(2,1)S(1)}, bf16[640,240]{1,0:T(8,128)(2,1)S(1)}) custom-call(s32[1]{0:T(128)} %bitcast.4.flag_ref, f32[240,640]{1,0:T(8,128)} %broadcast_select_fusion.2.held, f32[240,640]{1,0:T(8,128)} %collective-permute-done.24.come), custom_call_target="tpu_custom_call" | custom-call | bytes 1843200 | tf_op jit(solution)/shard_map/turn_strip/pallas_call | solution.py:150
  103.0 2.8 %diag_first.2.first = f32[640,384]{1,0:T(8,128)S(1)} custom-call(bf16[640,240]{1,0:T(8,128)(2,1)S(1)} %get-tuple-element.53.refs_0_, bf16[640,240]{1,0:T(8,128)(2,1)S(1)} %get-tuple-element.56.refs_1_, bf16[640,240]{1,0:T(8,128)(2,1)S(1)} %get-tuple-element.58.refs_2_, bf16[640,240]{1,0:T(8,128)(2,1)S(1)} %get-tuple-element.59.refs_3_, ...), custom_call_target="tpu_custom_call" | custom-call | flops 106168320 | bytes 184320 | tf_op jit(solution)/shard_map/diag_first/pallas_call | solution.py:176
  105.8 1.6 %collective-permute-done.28.block = f32[240,384]{1,0:T(8,128)} collective-permute-done((f32[240,384]{1,0:T(8,128)}, f32[240,384]{1,0:T(8,128)}, u32[]{:S(2)}, u32[]{:S(2)}) %collective-permute-start.28) | collective-permute-done | bytes 368672 | tf_op jit(solution)/shard_map/ppermute | solution.py:226
  107.4 1.3 %turn_strip.7 = (bf16[640,240]{1,0:T(8,128)(2,1)S(1)}, bf16[640,240]{1,0:T(8,128)(2,1)S(1)}) custom-call(s32[1]{0:T(128)} %bitcast.4.flag_ref, f32[240,640]{1,0:T(8,128)S(1)} %broadcast_select_fusion.held, f32[240,640]{1,0:T(8,128)} %collective-permute-done.29.come), custom_call_target="tpu_custom_call" | custom-call | bytes 1843200 | tf_op jit(solution)/shard_map/turn_strip/pallas_call | solution.py:150
  108.7 1.8 %diag_last.2 = (f32[320,384]{1,0:T(8,128)S(1)}, f32[320,384]{1,0:T(8,128)S(1)}) custom-call(s32[1]{0:T(128)} %bitcast.member_ref, f32[640,384]{1,0:T(8,128)S(1)} %diag_first.2.first, f32[320,640]{1,0:T(8,128)S(1)} %copy-done, bf16[640,240]{1,0:T(8,128)(2,1)S(1)} %get-tuple-element.67.high, bf16[640,240]{1,0:T(8,128)(2,1)S(1)} %get-tuple-element.68.low, ...), custom_call_target="tpu_custom_call" | custom-call | flops 35389440 | bytes 122880 | tf_op jit(solution)/shard_map/diag_last/pallas_call | solution.py:200
  110.5 0.3 collective-permute-start.30
  110.9 1.9 %diag_first.3.first = f32[640,256]{1,0:T(8,128)S(1)} custom-call(bf16[640,240]{1,0:T(8,128)(2,1)S(1)} %get-tuple-element.53.refs_0_, bf16[640,240]{1,0:T(8,128)(2,1)S(1)} %get-tuple-element.56.refs_1_, bf16[640,240]{1,0:T(8,128)(2,1)S(1)} %get-tuple-element.58.refs_2_, bf16[640,240]{1,0:T(8,128)(2,1)S(1)} %get-tuple-element.59.refs_3_, ...), custom_call_target="tpu_custom_call" | custom-call | flops 70778880 | bytes 184320 | tf_op jit(solution)/shard_map/diag_first/pallas_call | solution.py:176
  112.8 1.4 %diag_last.3 = (f32[320,256]{1,0:T(8,128)S(1)}, f32[320,256]{1,0:T(8,128)S(1)}) custom-call(s32[1]{0:T(128)} %bitcast.member_ref, f32[640,256]{1,0:T(8,128)S(1)} %diag_first.3.first, f32[320,640]{1,0:T(8,128)S(1)} %copy-done, bf16[640,240]{1,0:T(8,128)(2,1)S(1)} %get-tuple-element.67.high, bf16[640,240]{1,0:T(8,128)(2,1)S(1)} %get-tuple-element.68.low, ...), custom_call_target="tpu_custom_call" | custom-call | flops 23592960 | bytes 122880 | tf_op jit(solution)/shard_map/diag_last/pallas_call | solution.py:200
  114.2 1.8 %collective-permute-start.32 = (f32[320,256]{1,0:T(8,128)S(1)}, f32[320,256]{1,0:T(8,128)S(1)}, u32[]{:S(2)}, u32[]{:S(2)}) collective-permute-start(f32[320,256]{1,0:T(8,128)S(1)} %get-tuple-element.73), channel_id=1, source_target_pairs={{0,4},{1,5},{2,6},{3,7},{4,0},{5,1},{6,2},{7,3},{8,12},{9,13},{10,... | collective-permute-start | bytes 983048 | tf_op jit(solution)/shard_map/ppermute | solution.py:226
  116.0 0.9 pad_maximum_fusion.1
  116.9 8.5 %collective-permute-done.32 = f32[320,256]{1,0:T(8,128)S(1)} collective-permute-done((f32[320,256]{1,0:T(8,128)S(1)}, f32[320,256]{1,0:T(8,128)S(1)}, u32[]{:S(2)}, u32[]{:S(2)}) %collective-permute-start.32) | collective-permute-done | bytes 327712 | tf_op jit(solution)/shard_map/ppermute | solution.py:226
  125.5 0.9 pad_maximum_fusion
  (44 shorter events, 0.9 us)
Async XLA Ops:
  0.6 108.1 %copy-start = (f32[320,640]{1,0:T(8,128)S(1)}, f32[320,640]{1,0:T(8,128)}, u32[]{:S(2)}) copy-start(f32[320,640]{1,0:T(8,128)} %base_ref.3) | copy-start | bytes 2457604
  1.7 13.7 %collective-permute-start.5 = (f32[240,384]{1,0:T(8,128)S(1)}, f32[240,384]{1,0:T(8,128)S(1)}, u32[]{:S(2)}, u32[]{:S(2)}) collective-permute-start(f32[240,384]{1,0:T(8,128)S(1)} %slice.6.refs_0_), channel_id=1, source_target_pairs={{0,8},{1,9},{2,10},{3,11},{4,12},{5,13},{6,14},{7,15},{8,16},{9,17... | collective-permute-start | bytes 1105928 | tf_op jit(solution)/shard_map/ppermute | solution.py:226
  4.8 3.7 %collective-permute-start = (s32[240]{0:T(256)}, s32[240]{0:T(256)S(1)}, u32[]{:S(2)}, u32[]{:S(2)}) collective-permute-start(s32[240]{0:T(256)} %rows_ref.1), channel_id=1, source_target_pairs={{0,0},{1,8},{2,16},{3,24},{4,4},{5,12},{6,20},{7,28},{8,1},{9,9},{... | collective-permute-start | bytes 2888 | tf_op jit(solution)/shard_map/ppermute | solution.py:226
  6.1 3.8 %collective-permute-start.1 = (s32[240]{0:T(256)}, s32[240]{0:T(256)S(1)}, u32[]{:S(2)}, u32[]{:S(2)}) collective-permute-start(s32[240]{0:T(256)} %rows_ref.1), channel_id=1, source_target_pairs={{0,4},{1,12},{2,20},{3,28},{4,0},{5,8},{6,16},{7,24},{8,5},{9,13},... | collective-permute-start | bytes 2888 | tf_op jit(solution)/shard_map/ppermute | solution.py:226
  9.9 0.7 copy-start.5
  15.5 16.6 %collective-permute-start.10 = (f32[240,384]{1,0:T(8,128)S(1)}, f32[240,384]{1,0:T(8,128)S(1)}, u32[]{:S(2)}, u32[]{:S(2)}) collective-permute-start(f32[240,384]{1,0:T(8,128)S(1)} %collective-permute-done.5.refs_1_), channel_id=1, source_target_pairs={{0,8},{1,9},{2,10},{3,11},{4,12},{5,13},{6,14},{7,15},{8,16},{9,17... | collective-permute-start | bytes 1105928 | tf_op jit(solution)/shard_map/ppermute | solution.py:226
  20.0 9.1 %collective-permute-start.2 = (f32[240,240]{1,0:T(8,128)S(1)}, f32[240,240]{1,0:T(8,128)}, u32[]{:S(2)}, u32[]{:S(2)}) collective-permute-start(f32[240,240]{1,0:T(8,128)S(1)} %get-tuple-element.38.refs_0_), channel_id=1, source_target_pairs={{0,2},{1,3},{2,0},{3,1},{4,6},{5,7},{6,4},{7,5},{8,10},{9,11},{10,... | collective-permute-start | bytes 691208 | tf_op jit(solution)/shard_map/ppermute | solution.py:226
  23.5 13.9 %collective-permute-start.11 = (f32[240,256]{1,0:T(8,128)S(1)}, f32[240,256]{1,0:T(8,128)S(1)}, u32[]{:S(2)}, u32[]{:S(2)}) collective-permute-start(f32[240,256]{1,0:T(8,128)S(1)} %slice.7.refs_0_), channel_id=1, source_target_pairs={{0,8},{1,9},{2,10},{3,11},{4,12},{5,13},{6,14},{7,15},{8,16},{9,17... | collective-permute-start | bytes 737288 | tf_op jit(solution)/shard_map/ppermute | solution.py:226
  24.7 13.2 %collective-permute-start.3 = (f32[240,240]{1,0:T(8,128)S(1)}, f32[240,240]{1,0:T(8,128)S(1)}, u32[]{:S(2)}, u32[]{:S(2)}) collective-permute-start(f32[240,240]{1,0:T(8,128)S(1)} %get-tuple-element.38.refs_0_), channel_id=1, source_target_pairs={{0,1},{1,0},{2,3},{3,2},{4,5},{5,4},{6,7},{7,6},{8,9},{9,8},{10,11... | collective-permute-start | bytes 691208 | tf_op jit(solution)/shard_map/ppermute | solution.py:226
  24.7 13.9 %collective-permute-start.6 = (f32[240,240]{1,0:T(8,128)S(1)}, f32[240,240]{1,0:T(8,128)}, u32[]{:S(2)}, u32[]{:S(2)}) collective-permute-start(f32[240,240]{1,0:T(8,128)S(1)} %get-tuple-element.40), channel_id=1, source_target_pairs={{0,4},{1,5},{2,6},{3,7},{4,0},{5,1},{6,2},{7,3},{8,12},{9,13},{10,... | collective-permute-start | bytes 691208 | tf_op jit(solution)/shard_map/ppermute | solution.py:226
  29.1 10.0 %collective-permute-start.7 = (f32[240,240]{1,0:T(8,128)S(1)}, f32[240,240]{1,0:T(8,128)}, u32[]{:S(2)}, u32[]{:S(2)}) collective-permute-start(f32[240,240]{1,0:T(8,128)S(1)} %get-tuple-element.40), channel_id=1, source_target_pairs={{0,6},{1,7},{2,4},{3,5},{4,2},{5,3},{6,0},{7,1},{8,14},{9,15},{10,... | collective-permute-start | bytes 691208 | tf_op jit(solution)/shard_map/ppermute | solution.py:226
  32.1 17.9 %collective-permute-start.13 = (f32[240,384]{1,0:T(8,128)S(1)}, f32[240,384]{1,0:T(8,128)S(1)}, u32[]{:S(2)}, u32[]{:S(2)}) collective-permute-start(f32[240,384]{1,0:T(8,128)S(1)} %collective-permute-done.10.refs_2_), channel_id=1, source_target_pairs={{0,8},{1,9},{2,10},{3,11},{4,12},{5,13},{6,14},{7,15},{8,16},{9,17... | collective-permute-start | bytes 1105928 | tf_op jit(solution)/shard_map/ppermute | solution.py:226
  37.4 12.7 %collective-permute-start.12 = (f32[240,256]{1,0:T(8,128)S(1)}, f32[240,256]{1,0:T(8,128)S(1)}, u32[]{:S(2)}, u32[]{:S(2)}) collective-permute-start(f32[240,256]{1,0:T(8,128)S(1)} %collective-permute-done.11.refs_1_), channel_id=1, source_target_pairs={{0,8},{1,9},{2,10},{3,11},{4,12},{5,13},{6,14},{7,15},{8,16},{9,17... | collective-permute-start | bytes 737288 | tf_op jit(solution)/shard_map/ppermute | solution.py:226
  37.9 0.7 copy-start.3
  38.6 1.9 %collective-permute-start.4 = (f32[240,240]{1,0:T(8,128)}, f32[240,240]{1,0:T(8,128)}, u32[]{:S(2)}, u32[]{:S(2)}) collective-permute-start(f32[240,240]{1,0:T(8,128)} %collective-permute-done.2.refs_1_), channel_id=1, source_target_pairs={{0,1},{1,0},{2,3},{3,2},{4,5},{5,4},{6,7},{7,6},{8,9},{9,8},{10,11... | collective-permute-start | bytes 691208 | tf_op jit(solution)/shard_map/ppermute | solution.py:226
  38.6 2.2 %collective-permute-start.8 = (f32[240,240]{1,0:T(8,128)}, f32[240,240]{1,0:T(8,128)}, u32[]{:S(2)}, u32[]{:S(2)}) collective-permute-start(f32[240,240]{1,0:T(8,128)} %collective-permute-done.6.refs_4_), channel_id=1, source_target_pairs={{0,1},{1,0},{2,3},{3,2},{4,5},{5,4},{6,7},{7,6},{8,9},{9,8},{10,11... | collective-permute-start | bytes 691208 | tf_op jit(solution)/shard_map/ppermute | solution.py:226
  39.1 2.0 %collective-permute-start.9 = (f32[240,240]{1,0:T(8,128)}, f32[240,240]{1,0:T(8,128)}, u32[]{:S(2)}, u32[]{:S(2)}) collective-permute-start(f32[240,240]{1,0:T(8,128)} %collective-permute-done.7.refs_5_), channel_id=1, source_target_pairs={{0,1},{1,0},{2,3},{3,2},{4,5},{5,4},{6,7},{7,6},{8,9},{9,8},{10,11... | collective-permute-start | bytes 691208 | tf_op jit(solution)/shard_map/ppermute | solution.py:226
  41.1 0.9 copy-start.4
  50.0 12.1 %collective-permute-start.15 = (f32[240,256]{1,0:T(8,128)S(1)}, f32[240,256]{1,0:T(8,128)S(1)}, u32[]{:S(2)}, u32[]{:S(2)}) collective-permute-start(f32[240,256]{1,0:T(8,128)S(1)} %collective-permute-done.12.refs_2_), channel_id=1, source_target_pairs={{0,8},{1,9},{2,10},{3,11},{4,12},{5,13},{6,14},{7,15},{8,16},{9,17... | collective-permute-start | bytes 737288 | tf_op jit(solution)/shard_map/ppermute | solution.py:226
  51.8 12.2 %collective-permute-start.14 = (f32[240,384]{1,0:T(8,128)S(1)}, f32[240,384]{1,0:T(8,128)S(1)}, u32[]{:S(2)}, u32[]{:S(2)}) collective-permute-start(f32[240,384]{1,0:T(8,128)S(1)} %get-tuple-element.46), channel_id=1, source_target_pairs={{0,4},{1,5},{2,6},{3,7},{4,0},{5,1},{6,2},{7,3},{8,12},{9,13},{10,... | collective-permute-start | bytes 1105928 | tf_op jit(solution)/shard_map/ppermute | solution.py:226
  53.4 25.3 %collective-permute-start.19 = (f32[240,640]{1,0:T(8,128)}, f32[240,640]{1,0:T(8,128)}, u32[]{:S(2)}, u32[]{:S(2)}) collective-permute-start(f32[240,640]{1,0:T(8,128)} %pad_maximum_fusion.2), channel_id=1, source_target_pairs={{0,2},{4,6},{9,11},{13,15},{18,16},{22,20},{27,25},{31,29}} | collective-permute-start | bytes 1843208 | tf_op jit(solution)/shard_map/ppermute | solution.py:226
  60.0 18.7 %collective-permute-start.18 = (f32[240,640]{1,0:T(8,128)}, f32[240,640]{1,0:T(8,128)}, u32[]{:S(2)}, u32[]{:S(2)}) collective-permute-start(f32[240,640]{1,0:T(8,128)} %param.5), channel_id=1, source_target_pairs={{0,2},{4,6},{9,11},{13,15},{18,16},{22,20},{27,25},{31,29}} | collective-permute-start | bytes 1843208 | tf_op jit(solution)/shard_map/ppermute | solution.py:226
  63.1 6.3 %collective-permute-start.16 = (f32[240,256]{1,0:T(8,128)S(1)}, f32[240,256]{1,0:T(8,128)S(1)}, u32[]{:S(2)}, u32[]{:S(2)}) collective-permute-start(f32[240,256]{1,0:T(8,128)S(1)} %get-tuple-element.49), channel_id=1, source_target_pairs={{0,4},{1,5},{2,6},{3,7},{4,0},{5,1},{6,2},{7,3},{8,12},{9,13},{10,... | collective-permute-start | bytes 737288 | tf_op jit(solution)/shard_map/ppermute | solution.py:226
  64.1 14.6 %collective-permute-start.17 = (f32[240,384]{1,0:T(8,128)S(1)}, f32[240,384]{1,0:T(8,128)}, u32[]{:S(2)}, u32[]{:S(2)}) collective-permute-start(f32[240,384]{1,0:T(8,128)S(1)} %add.28.refs_6_), channel_id=1, source_target_pairs={{0,8},{1,9},{2,10},{3,11},{4,12},{5,13},{6,14},{7,15},{8,16},{9,17... | collective-permute-start | bytes 1105928 | tf_op jit(solution)/shard_map/ppermute | solution.py:226
  69.4 9.3 %collective-permute-start.21 = (f32[240,256]{1,0:T(8,128)S(1)}, f32[240,256]{1,0:T(8,128)S(1)}, u32[]{:S(2)}, u32[]{:S(2)}) collective-permute-start(f32[240,256]{1,0:T(8,128)S(1)} %add.29.refs_6_), channel_id=1, source_target_pairs={{0,8},{1,9},{2,10},{3,11},{4,12},{5,13},{6,14},{7,15},{8,16},{9,17... | collective-permute-start | bytes 737288 | tf_op jit(solution)/shard_map/ppermute | solution.py:226
  69.5 17.5 %collective-permute-start.23 = (f32[240,640]{1,0:T(8,128)S(1)}, f32[240,640]{1,0:T(8,128)S(1)}, u32[]{:S(2)}, u32[]{:S(2)}) collective-permute-start(f32[240,640]{1,0:T(8,128)S(1)} %pad_maximum_fusion.3), channel_id=1, source_target_pairs={{0,2},{4,6},{9,11},{13,15},{18,16},{22,20},{27,25},{31,29}} | collective-permute-start | bytes 1843208 | tf_op jit(solution)/shard_map/ppermute | solution.py:226
  78.7 10.5 %collective-permute-start.22 = (f32[240,256]{1,0:T(8,128)S(1)}, f32[240,256]{1,0:T(8,128)}, u32[]{:S(2)}, u32[]{:S(2)}) collective-permute-start(f32[240,256]{1,0:T(8,128)S(1)} %collective-permute-done.21.refs_7_), channel_id=1, source_target_pairs={{0,8},{1,9},{2,10},{3,11},{4,12},{5,13},{6,14},{7,15},{8,16},{9,17... | collective-permute-start | bytes 737288 | tf_op jit(solution)/shard_map/ppermute | solution.py:226
  78.7 15.7 %collective-permute-start.26 = (f32[240,384]{1,0:T(8,128)}, f32[240,384]{1,0:T(8,128)}, u32[]{:S(2)}, u32[]{:S(2)}) collective-permute-start(f32[240,384]{1,0:T(8,128)} %collective-permute-done.17.refs_7_), channel_id=1, source_target_pairs={{0,8},{1,9},{2,10},{3,11},{4,12},{5,13},{6,14},{7,15},{8,16},{9,17... | collective-permute-start | bytes 1105928 | tf_op jit(solution)/shard_map/ppermute | solution.py:226
  79.2 13.0 %collective-permute-start.27 = (f32[240,640]{1,0:T(8,128)S(1)}, f32[240,640]{1,0:T(8,128)S(1)}, u32[]{:S(2)}, u32[]{:S(2)}) collective-permute-start(f32[240,640]{1,0:T(8,128)S(1)} %pad_maximum_fusion.4), channel_id=1, source_target_pairs={{0,2},{4,6},{9,11},{13,15},{18,16},{22,20},{27,25},{31,29}} | collective-permute-start | bytes 1843208 | tf_op jit(solution)/shard_map/ppermute | solution.py:226
  84.6 9.9 %collective-permute-start.25 = (f32[240,640]{1,0:T(8,128)S(1)}, f32[240,640]{1,0:T(8,128)S(1)}, u32[]{:S(2)}, u32[]{:S(2)}) collective-permute-start(f32[240,640]{1,0:T(8,128)S(1)} %broadcast_select_fusion.1.held), channel_id=1, source_target_pairs={{0,1},{2,3},{4,5},{6,7},{9,8},{11,10},{13,12},{15,14},{16,17},{18,... | collective-permute-start | bytes 1843208 | tf_op jit(solution)/shard_map/ppermute | solution.py:226
  87.1 13.1 %collective-permute-start.20 = (f32[240,640]{1,0:T(8,128)S(1)}, f32[240,640]{1,0:T(8,128)}, u32[]{:S(2)}, u32[]{:S(2)}) collective-permute-start(f32[240,640]{1,0:T(8,128)S(1)} %broadcast_select_fusion.3.held), channel_id=1, source_target_pairs={{0,1},{2,3},{4,5},{6,7},{9,8},{11,10},{13,12},{15,14},{16,17},{18,... | collective-permute-start | bytes 1843208 | tf_op jit(solution)/shard_map/ppermute | solution.py:226
  90.1 11.4 %collective-permute-start.24 = (f32[240,640]{1,0:T(8,128)}, f32[240,640]{1,0:T(8,128)}, u32[]{:S(2)}, u32[]{:S(2)}) collective-permute-start(f32[240,640]{1,0:T(8,128)} %broadcast_select_fusion.2.held), channel_id=1, source_target_pairs={{0,1},{2,3},{4,5},{6,7},{9,8},{11,10},{13,12},{15,14},{16,17},{18,... | collective-permute-start | bytes 1843208 | tf_op jit(solution)/shard_map/ppermute | solution.py:226
  92.3 15.1 %collective-permute-start.29 = (f32[240,640]{1,0:T(8,128)S(1)}, f32[240,640]{1,0:T(8,128)}, u32[]{:S(2)}, u32[]{:S(2)}) collective-permute-start(f32[240,640]{1,0:T(8,128)S(1)} %broadcast_select_fusion.held), channel_id=1, source_target_pairs={{0,1},{2,3},{4,5},{6,7},{9,8},{11,10},{13,12},{15,14},{16,17},{18,... | collective-permute-start | bytes 1843208 | tf_op jit(solution)/shard_map/ppermute | solution.py:226
  94.5 12.9 %collective-permute-start.28 = (f32[240,384]{1,0:T(8,128)}, f32[240,384]{1,0:T(8,128)}, u32[]{:S(2)}, u32[]{:S(2)}) collective-permute-start(f32[240,384]{1,0:T(8,128)} %collective-permute-done.26.refs_8_), channel_id=1, source_target_pairs={{0,8},{1,9},{2,10},{3,11},{4,12},{5,13},{6,14},{7,15},{8,16},{9,17... | collective-permute-start | bytes 1105928 | tf_op jit(solution)/shard_map/ppermute | solution.py:226
  94.5 0.8 copy-start.1
  95.3 17.5 %collective-permute-start.31 = (f32[240,256]{1,0:T(8,128)}, f32[240,256]{1,0:T(8,128)}, u32[]{:S(2)}, u32[]{:S(2)}) collective-permute-start(f32[240,256]{1,0:T(8,128)} %collective-permute-done.22.refs_8_), channel_id=1, source_target_pairs={{0,8},{1,9},{2,10},{3,11},{4,12},{5,13},{6,14},{7,15},{8,16},{9,17... | collective-permute-start | bytes 737288 | tf_op jit(solution)/shard_map/ppermute | solution.py:226
  98.8 1.1 copy-start.2
  110.5 15.0 %collective-permute-start.30 = (f32[320,384]{1,0:T(8,128)S(1)}, f32[320,384]{1,0:T(8,128)S(1)}, u32[]{:S(2)}, u32[]{:S(2)}) collective-permute-start(f32[320,384]{1,0:T(8,128)S(1)} %get-tuple-element.71), channel_id=1, source_target_pairs={{0,4},{1,5},{2,6},{3,7},{4,0},{5,1},{6,2},{7,3},{8,12},{9,13},{10,... | collective-permute-start | bytes 1474568 | tf_op jit(solution)/shard_map/ppermute | solution.py:226
  114.2 11.2 %collective-permute-start.32 = (f32[320,256]{1,0:T(8,128)S(1)}, f32[320,256]{1,0:T(8,128)S(1)}, u32[]{:S(2)}, u32[]{:S(2)}) collective-permute-start(f32[320,256]{1,0:T(8,128)S(1)} %get-tuple-element.73), channel_id=1, source_target_pairs={{0,4},{1,5},{2,6},{3,7},{4,0},{5,1},{6,2},{7,3},{8,12},{9,13},{10,... | collective-permute-start | bytes 983048 | tf_op jit(solution)/shard_map/ppermute | solution.py:226
